TPU v7x, 128 devices: a whole 4x4x4 slice. The times are simulated.
128 devices in a mesh: seq: 16 (over z, y), exp: 8 (over x, core).
Axes of the slice: x: 4, y: 4, z: 4, core: 2. Of those that a mesh axis runs over, the one named last changes fastest.
Arguments:
- layer_input: bfloat16 [16384, 2048], P(('seq', 'exp')), may hold values from -24 to 24, as said below
- attn_gain: float32 [2048], replicated, may hold values from 0.1 to 1.9
- query_proj: bfloat16 [2048, 3072], P(None, 'exp'), may hold values from -0.1875 to 0.1875
- latent_proj: bfloat16 [2048, 576], replicated, may hold values from -0.125 to 0.125
- latent_gain: float32 [512], replicated, may hold values from 0.1 to 1.9
- kv_proj: bfloat16 [512, 4096], P(None, 'exp'), may hold values from -0.25 to 0.25
- output_proj: bfloat16 [2048, 2048], P('exp'), may hold values from -3 to 3
- ffn_gain: float32 [2048], replicated, may hold values from 0.1 to 1.9
- router_proj: float32 [2048, 8], replicated, may hold values from -0.0625 to 0.0625
- shared_gate_up: bfloat16 [2048, 2, 2816], P(None, None, 'exp'), may hold values from -0.125 to 0.125
- shared_down: bfloat16 [2816, 2048], P('exp'), may hold values from -0.15625 to 0.15625
- expert_gate_up: bfloat16 [8, 2048, 2816], P('exp'), may hold values from -0.125 to 0.125
- expert_down: bfloat16 [8, 1408, 2048], P('exp'), may hold values from -0.625 to 0.625
- segment_ids: int32 [16384], replicated, may hold values from 0 to 31, as said below
- expert_routes: int32 [16384, 6], P(('seq', 'exp')), may hold values from 0 to 7, all different within a row; in each aligned block of 128 rows (0 to 127, 128 to 255, ...) at most 128 rows name the same one
- out_grad: bfloat16 [16384, 2048], P(('seq', 'exp')), may hold values from -6 to 6
Outputs:
- layer_output: bfloat16 [16384, 2048], P(('seq', 'exp'))
- input_grad: bfloat16 [16384, 2048], P(('seq', 'exp'))
- attn_gain_grad: float32 [2048], replicated
- query_proj_grad: float32 [2048, 3072], P(None, 'exp')
- latent_proj_grad: float32 [2048, 576], replicated
- latent_gain_grad: float32 [512], replicated
- kv_proj_grad: float32 [512, 4096], P(None, 'exp')
- output_proj_grad: float32 [2048, 2048], P('exp')
- ffn_gain_grad: float32 [2048], replicated
- router_grad: float32 [2048, 8], replicated
- shared_gate_up_grad: float32 [2048, 2, 2816], P('seq', None, 'exp')
- shared_down_grad: float32 [2816, 2048], P('exp', 'seq')
- expert_gate_up_grad: float32 [8, 2048, 2816], P('exp', 'seq')
- expert_down_grad: float32 [8, 1408, 2048], P('exp', None, 'seq')
Inputs may be any that keep to these rules, and one draw needn't show every extreme that they name: `layer_input`: the block's input. `segment_ids`: never falls along the tokens; every document lies within one packed sequence of 2048 tokens, and the documents of packed sequence s are numbered 4 s to 4 s + 3. `expert_routes`: each token names 6 different experts; the 128 rows of one device name one expert at most 128 times.
All inputs are finite; a program needn't handle non-finite values.
Results may differ from a plain program's by a relative error of at most 0.029.
Values may be sent and summed in bfloat16 or wider, within the bound.
A program may use at most 256 MiB of HBM per device.

v0:
```python
import math

import jax
import jax.numpy as jnp
from jax import lax
from jax.sharding import PartitionSpec as P

NOPE = 128
ROPE = 64
VDIM = 128
LAT = 512
F = 1408
TOP = 6
EXPERTS = 8


highest = lax.Precision.HIGHEST
EPSILON = 1e-06


def shifted(block, axis, distance):
    devices = range(lax.axis_size(axis))
    route = [(i - distance, i) for i in devices if i - distance in devices]
    return lax.ppermute(block, axis, route)


def rms_scale(tensor, gain_vec):
    return (
        tensor * lax.rsqrt(jnp.mean(tensor * tensor, axis=-1, keepdims=True) + EPSILON) * gain_vec
    )


def rms_back(tensor, gain_vec, upstream):
    inverse = lax.rsqrt(jnp.mean(tensor * tensor, axis=-1, keepdims=True) + EPSILON)
    gain_grad = jnp.sum(upstream * tensor * inverse, axis=0)
    scaled = upstream * gain_vec
    inner = jnp.mean(scaled * tensor, axis=-1, keepdims=True)
    return (inverse * scaled - tensor * inverse**3 * inner, gain_grad)


def silu(tensor):
    return tensor * jax.nn.sigmoid(tensor)


def silu_back(gate_pre, up_pre, upstream):
    logistic = jax.nn.sigmoid(gate_pre)
    return (
        upstream * up_pre * logistic * (1.0 + gate_pre * (1.0 - logistic)),
        upstream * gate_pre * logistic,
    )


def rotate(tensor, position, direction):
    half_width = tensor.shape[-1] // 2
    frequency = jnp.exp(
        jnp.arange(half_width, dtype=jnp.float32) * (-math.log(10000.0) / half_width)
    )
    angles = position.astype(jnp.float32)[:, None] * frequency[None, :]
    shape_out = (tensor.shape[0],) + (1,) * (tensor.ndim - 2) + (half_width,)
    cosine = jnp.cos(angles).reshape(shape_out)
    sine_term = direction * jnp.sin(angles).reshape(shape_out)
    first_half = tensor[..., :half_width]
    second_half = tensor[..., half_width:]
    return jnp.concatenate(
        [
            first_half * cosine - second_half * sine_term,
            first_half * sine_term + second_half * cosine,
        ],
        axis=-1,
    )


def gather_rows(tensor):
    return lax.all_gather(tensor, "exp", axis=0, tiled=True)


def sum_rows(tensor):
    return lax.psum_scatter(
        tensor.astype(jnp.bfloat16), "exp", scatter_dimension=0, tiled=True
    ).astype(jnp.float32)


def route_move(tensor):
    return lax.all_to_all(tensor, "exp", split_axis=1, concat_axis=1, tiled=True)


def add_own(full_term, own_term, row_offset):
    current = lax.dynamic_slice_in_dim(full_term, row_offset, own_term.shape[0], 0)
    return lax.dynamic_update_slice_in_dim(full_term, current + own_term, row_offset, 0)


def expand_keys(latent_all, kv_proj, head_count):
    return (
        jnp.dot(latent_all, kv_proj, preferred_element_type=jnp.float32)
        .astype(jnp.bfloat16)
        .reshape(latent_all.shape[0], head_count, NOPE + VDIM)
    )


def score_block(queries, packed, rope_all, query_pos, query_seg, key_pos, key_seg):
    score_scale = (NOPE + ROPE) ** (-0.5)
    nope_part = jnp.einsum(
        "qhc,khc->hqk", queries[..., :NOPE], packed[..., :NOPE], preferred_element_type=jnp.float32
    )
    rope_part = jnp.einsum(
        "qhc,kc->hqk", queries[..., NOPE:], rope_all, preferred_element_type=jnp.float32
    )
    allowed = (query_seg[:, None] == key_seg[None, :]) & (key_pos[None, :] <= query_pos[:, None])
    return jnp.where(allowed[None], (nope_part + rope_part) * score_scale, -1e30)


def local(
    layer_input,
    attn_gain,
    query_proj,
    latent_proj,
    latent_gain,
    kv_proj,
    output_proj,
    ffn_gain,
    router_proj,
    shared_gate_up,
    shared_down,
    expert_gate_up,
    expert_down,
    segment_ids,
    expert_routes,
    out_grad,
):
    f32 = jnp.float32
    bf16 = jnp.bfloat16
    exp_count = lax.axis_size("exp")
    own_rows = layer_input.shape[0]
    model_width = layer_input.shape[1]
    block_rows = own_rows * exp_count
    key_rows = 2 * block_rows
    head_count = query_proj.shape[1] // (NOPE + ROPE)
    per_device = expert_gate_up.shape[0]
    capacity = 4 * own_rows * TOP // (3 * EXPERTS)
    slot_total = EXPERTS * capacity
    score_scale = (NOPE + ROPE) ** (-0.5)
    block_start = lax.axis_index("seq") * block_rows
    row_offset = lax.axis_index("exp") * own_rows
    query_pos = block_start + jnp.arange(block_rows, dtype=jnp.int32)
    own_pos = block_start + row_offset + jnp.arange(own_rows, dtype=jnp.int32)
    query_seg = lax.dynamic_slice_in_dim(segment_ids, block_start, block_rows)
    key_start = block_start - block_rows
    key_pos = key_start + jnp.arange(key_rows, dtype=jnp.int32)
    prev_seg = lax.dynamic_slice_in_dim(segment_ids, jnp.maximum(key_start, 0), block_rows)
    prev_seg = jnp.where(key_start >= 0, prev_seg, -1)
    key_seg = jnp.concatenate([prev_seg, query_seg], axis=0)
    input_f = layer_input.astype(f32)
    normed_low = rms_scale(input_f, attn_gain).astype(bf16)
    normed_all = gather_rows(normed_low)
    query_raw = jnp.dot(normed_all, query_proj, preferred_element_type=f32).reshape(
        block_rows, head_count, NOPE + ROPE
    )
    queries = jnp.concatenate(
        [query_raw[..., :NOPE], rotate(query_raw[..., NOPE:], query_pos % key_rows, 1.0)], axis=-1
    ).astype(bf16)
    latent_raw = jnp.dot(normed_low, latent_proj, preferred_element_type=f32)
    latent_normed = rms_scale(latent_raw[:, :LAT], latent_gain).astype(bf16)
    rope_key = rotate(latent_raw[:, LAT:], own_pos % key_rows, 1.0).astype(bf16)
    key_latent = jnp.concatenate([latent_normed, rope_key], axis=-1)
    block_keys = lax.all_gather(key_latent, "exp", axis=0, tiled=True)
    prev_keys = shifted(block_keys, "seq", 1)
    keys_all = jnp.concatenate([prev_keys, block_keys], axis=0)
    latent_all = keys_all[:, :LAT]
    rope_all = keys_all[:, LAT:]
    packed = expand_keys(latent_all, kv_proj, head_count)
    scores = score_block(queries, packed, rope_all, query_pos, query_seg, key_pos, key_seg)
    top_score = jnp.max(scores, axis=-1, keepdims=True)
    weights = jnp.exp(scores - top_score)
    weight_sum = jnp.sum(weights, axis=-1, keepdims=True)
    soft_weights = weights / weight_sum
    log_total = top_score + jnp.log(weight_sum)
    head_rows = jnp.einsum(
        "hqk,khc->qhc", soft_weights.astype(bf16), packed[..., NOPE:], preferred_element_type=f32
    )
    heads_low = head_rows.astype(bf16).reshape(block_rows, head_count * VDIM)
    attn_rows = sum_rows(jnp.dot(heads_low, output_proj, preferred_element_type=f32))
    residual = input_f + attn_rows
    mid_low = rms_scale(residual, ffn_gain).astype(bf16)
    mid_all = gather_rows(mid_low)
    shared_pre = jnp.einsum("td,dgf->tgf", mid_all, shared_gate_up, preferred_element_type=f32)
    shared_act = (silu(shared_pre[:, 0]) * shared_pre[:, 1]).astype(bf16)
    shared_part = jnp.dot(shared_act, shared_down, preferred_element_type=f32)
    logits = jnp.dot(mid_low.astype(f32), router_proj, precision=highest)
    logit_top = jnp.max(logits, axis=-1, keepdims=True)
    logit_exp = jnp.exp(logits - logit_top)
    gate_probs = logit_exp / jnp.sum(logit_exp, axis=-1, keepdims=True)
    route_hot = (
        expert_routes[:, :, None] == jnp.arange(EXPERTS, dtype=jnp.int32)[None, None, :]
    ).astype(f32)
    route_weights = jnp.sum(route_hot * gate_probs[:, None, :], axis=-1)
    flat_routes = expert_routes.reshape(own_rows * TOP)
    flat_hot = (flat_routes[:, None] == jnp.arange(EXPERTS, dtype=jnp.int32)[None, :]).astype(
        jnp.int32
    )
    rank_in = jnp.sum((jnp.cumsum(flat_hot, axis=0) - flat_hot) * flat_hot, axis=1)
    slot_index = (
        flat_routes % per_device * exp_count + flat_routes // per_device
    ) * capacity + rank_in
    slot_source = (
        jnp.zeros((slot_total,), jnp.int32)
        .at[slot_index]
        .set(jnp.arange(own_rows * TOP, dtype=jnp.int32))
    )
    slot_used = jnp.zeros((slot_total,), jnp.bool_).at[slot_index].set(True)
    send_rows = jnp.where(slot_used[:, None], mid_low[slot_source // TOP], jnp.zeros((), bf16))
    arrived = route_move(send_rows.reshape(per_device, exp_count, capacity, model_width)).reshape(
        per_device, exp_count * capacity, model_width
    )
    expert_pre = jnp.einsum("erd,edf->erf", arrived, expert_gate_up, preferred_element_type=f32)
    expert_act = (silu(expert_pre[..., :F]) * expert_pre[..., F:]).astype(bf16)
    expert_out = jnp.einsum(
        "erf,efd->erd", expert_act, expert_down, preferred_element_type=f32
    ).astype(bf16)
    came_back = route_move(
        expert_out.reshape(per_device, exp_count, capacity, model_width)
    ).reshape(slot_total, model_width)
    route_out = came_back[slot_index].reshape(own_rows, TOP, model_width)
    routed = jnp.sum(route_weights[:, :, None] * route_out.astype(f32), axis=1)
    moe_rows = sum_rows(shared_part) + routed
    layer_output = (residual + moe_rows).astype(bf16)
    grad_f = out_grad.astype(f32)
    grad_all = gather_rows(out_grad)
    shared_dact = jnp.einsum("td,fd->tf", grad_all, shared_down, preferred_element_type=f32)
    shared_dgate, shared_dup = silu_back(shared_pre[:, 0], shared_pre[:, 1], shared_dact)
    shared_dpre = jnp.stack([shared_dgate, shared_dup], axis=1).astype(bf16)
    mid_grad_all = jnp.einsum(
        "tgf,dgf->td", shared_dpre, shared_gate_up, preferred_element_type=f32
    )
    route_grad = (
        (route_weights[:, :, None] * grad_f[:, None, :])
        .astype(bf16)
        .reshape(own_rows * TOP, model_width)
    )
    send_grad = jnp.where(slot_used[:, None], route_grad[slot_source], jnp.zeros((), bf16))
    grad_arrived = route_move(
        send_grad.reshape(per_device, exp_count, capacity, model_width)
    ).reshape(per_device, exp_count * capacity, model_width)
    expert_dact = jnp.einsum("erd,efd->erf", grad_arrived, expert_down, preferred_element_type=f32)
    expert_dgate, expert_dup = silu_back(expert_pre[..., :F], expert_pre[..., F:], expert_dact)
    expert_dpre = jnp.concatenate([expert_dgate, expert_dup], axis=-1).astype(bf16)
    row_back = jnp.einsum(
        "erf,edf->erd", expert_dpre, expert_gate_up, preferred_element_type=f32
    ).astype(bf16)
    back_home = route_move(row_back.reshape(per_device, exp_count, capacity, model_width)).reshape(
        slot_total, model_width
    )
    route_in_grad = jnp.sum(
        back_home[slot_index].reshape(own_rows, TOP, model_width).astype(f32), axis=1
    )
    weight_grad = jnp.sum(route_out.astype(f32) * grad_f[:, None, :], axis=-1)
    gate_grad = jnp.sum(route_hot * weight_grad[:, :, None], axis=1)
    logit_grad = gate_probs * (gate_grad - jnp.sum(gate_probs * gate_grad, axis=-1, keepdims=True))
    router_term = jnp.einsum("td,te->de", mid_low.astype(f32), logit_grad, precision=highest)
    mid_grad_own = route_in_grad + jnp.einsum(
        "te,de->td", logit_grad, router_proj, precision=highest
    )
    mid_grad = sum_rows(add_own(mid_grad_all, mid_grad_own, row_offset))
    mid_input_grad, ffn_gain_term = rms_back(residual, ffn_gain, mid_grad)
    residual_grad = grad_f + mid_input_grad
    attn_grad_all = gather_rows(residual_grad.astype(bf16))
    output_term = jnp.einsum("tc,td->cd", heads_low, attn_grad_all, preferred_element_type=f32)
    heads_grad = (
        jnp.einsum("td,cd->tc", attn_grad_all, output_proj, preferred_element_type=f32)
        .astype(bf16)
        .reshape(block_rows, head_count, VDIM)
    )
    block_back = lax.all_gather(key_latent, "exp", axis=0, tiled=True)
    prev_back = shifted(block_back, "seq", 1)
    keys_back = jnp.concatenate([prev_back, block_back], axis=0)
    latent_back = keys_back[:, :LAT]
    rope_back = keys_back[:, LAT:]
    packed_back = expand_keys(latent_back, kv_proj, head_count)
    scores_back = score_block(
        queries, packed_back, rope_back, query_pos, query_seg, key_pos, key_seg
    )
    soft_back = jnp.exp(scores_back - log_total)
    prob_grad = jnp.einsum(
        "qhc,khc->hqk", heads_grad, packed_back[..., NOPE:], preferred_element_type=f32
    )
    score_grad = (
        soft_back * (prob_grad - jnp.sum(soft_back * prob_grad, axis=-1, keepdims=True))
    ).astype(bf16)
    query_nope_grad = score_scale * jnp.einsum(
        "hqk,khc->qhc", score_grad, packed_back[..., :NOPE], preferred_element_type=f32
    )
    query_rope_grad = score_scale * jnp.einsum(
        "hqk,kc->qhc", score_grad, rope_back, preferred_element_type=f32
    )
    query_raw_grad = (
        jnp.concatenate(
            [query_nope_grad, rotate(query_rope_grad, query_pos % key_rows, -1.0)], axis=-1
        )
        .astype(bf16)
        .reshape(block_rows, head_count * (NOPE + ROPE))
    )
    key_nope_grad = score_scale * jnp.einsum(
        "hqk,qhc->khc", score_grad, queries[..., :NOPE], preferred_element_type=f32
    )
    rope_key_grad = score_scale * jnp.einsum(
        "hqk,qhc->kc", score_grad, queries[..., NOPE:], preferred_element_type=f32
    )
    value_grad = jnp.einsum(
        "hqk,qhc->khc", soft_back.astype(bf16), heads_grad, preferred_element_type=f32
    )
    packed_grad = (
        jnp.concatenate([key_nope_grad, value_grad], axis=-1)
        .astype(bf16)
        .reshape(key_rows, head_count * (NOPE + VDIM))
    )
    kv_term = jnp.einsum("tl,tc->lc", latent_back, packed_grad, preferred_element_type=f32)
    latent_grad_all = jnp.einsum("tc,lc->tl", packed_grad, kv_proj, preferred_element_type=f32)
    key_grad = jnp.concatenate([latent_grad_all, rope_key_grad], axis=-1)
    prev_grad = shifted(key_grad[:block_rows].astype(jnp.bfloat16), "seq", -1).astype(jnp.float32)
    own_key_grad = lax.psum_scatter(
        (key_grad[block_rows:] + prev_grad).astype(jnp.bfloat16),
        "exp",
        scatter_dimension=0,
        tiled=True,
    ).astype(jnp.float32)
    latent_own = own_key_grad[:, :LAT]
    rope_own = own_key_grad[:, LAT:]
    query_term = jnp.einsum("td,tc->dc", normed_all, query_raw_grad, preferred_element_type=f32)
    in_grad_all = jnp.einsum("tc,dc->td", query_raw_grad, query_proj, preferred_element_type=f32)
    latent_pre_grad, latent_gain_term = rms_back(latent_raw[:, :LAT], latent_gain, latent_own)
    latent_raw_grad = jnp.concatenate(
        [latent_pre_grad, rotate(rope_own, own_pos % key_rows, -1.0)], axis=-1
    ).astype(bf16)
    latent_term = jnp.einsum("td,tc->dc", normed_low, latent_raw_grad, preferred_element_type=f32)
    in_grad_own = jnp.einsum("tc,dc->td", latent_raw_grad, latent_proj, preferred_element_type=f32)
    normed_grad = sum_rows(add_own(in_grad_all, in_grad_own, row_offset))
    input_part, attn_gain_term = rms_back(input_f, attn_gain, normed_grad)
    input_grad = (residual_grad + input_part).astype(bf16)
    shared_down_term = jnp.einsum("tf,td->fd", shared_act, grad_all, preferred_element_type=f32)
    shared_gate_term = jnp.einsum("td,tgf->dgf", mid_all, shared_dpre, preferred_element_type=f32)
    expert_down_term = jnp.einsum(
        "erf,erd->efd", expert_act, grad_arrived, preferred_element_type=f32
    )
    expert_gate_term = jnp.einsum("erd,erf->edf", arrived, expert_dpre, preferred_element_type=f32)
    expert_gate_sum, expert_down_sum, shared_gate_sum, shared_down_sum = (
        lax.psum_scatter(
            expert_gate_term.astype(jnp.bfloat16), "seq", scatter_dimension=1, tiled=True
        ).astype(jnp.float32),
        lax.psum_scatter(
            expert_down_term.astype(jnp.bfloat16), "seq", scatter_dimension=2, tiled=True
        ).astype(jnp.float32),
        lax.psum_scatter(
            shared_gate_term.astype(jnp.bfloat16), "seq", scatter_dimension=0, tiled=True
        ).astype(jnp.float32),
        lax.psum_scatter(
            shared_down_term.astype(jnp.bfloat16), "seq", scatter_dimension=1, tiled=True
        ).astype(jnp.float32),
    )
    query_sum, kv_sum, output_sum = (
        lax.psum(query_term.astype(jnp.bfloat16), "seq").astype(jnp.float32),
        lax.psum(kv_term.astype(jnp.bfloat16), "seq").astype(jnp.float32),
        lax.psum(output_term.astype(jnp.bfloat16), "seq").astype(jnp.float32),
    )
    latent_sum, attn_gain_sum, latent_gain_sum, ffn_gain_sum, router_sum = lax.psum(
        (latent_term, attn_gain_term, latent_gain_term, ffn_gain_term, router_term), ("seq", "exp")
    )
    return (
        layer_output,
        input_grad,
        attn_gain_sum,
        query_sum,
        latent_sum,
        latent_gain_sum,
        kv_sum,
        output_sum,
        ffn_gain_sum,
        router_sum,
        shared_gate_sum,
        shared_down_sum,
        expert_gate_sum,
        expert_down_sum,
    )


def solution(mesh):
    in_specs = (
        P(("seq", "exp"), None),
        P(),
        P(None, "exp"),
        P(),
        P(),
        P(None, "exp"),
        P("exp", None),
        P(),
        P(),
        P(None, None, "exp"),
        P("exp", None),
        P("exp", None, None),
        P("exp", None, None),
        P(),
        P(("seq", "exp"), None),
        P(("seq", "exp"), None),
    )
    out_specs = (
        P(("seq", "exp"), None),
        P(("seq", "exp"), None),
        P(),
        P(None, "exp"),
        P(),
        P(),
        P(None, "exp"),
        P("exp", None),
        P(),
        P(),
        P("seq", None, "exp"),
        P("exp", "seq"),
        P("exp", "seq", None),
        P("exp", None, "seq"),
    )
    return jax.shard_map(local, mesh=mesh, in_specs=in_specs, out_specs=out_specs, check_vma=False)
```

profile of v0, /device:TPU:1, one launch (start us, length us, event | category | flops | bytes accessed | tf_op | source)
XLA Modules:
  0.0 1412.1 jit_solution(1146957911307482463)
XLA Ops:
  16.4 26.7 %all-gather.6.cloned.1.call-done = bf16[1024,576]{0,1:T(8,128)(2,1)} async-done(((bf16[128,576]{0,1:T(8,128)(2,1)}), bf16[1024,576]{0,1:T(8,128)(2,1)}) %all-gather.6.cloned.1.call-update) | async-done | bytes 1179664 | tf_op jit(solution)/shard_map/all_gather | solution.py:165
  52.8 18.7 %collective-permute-done = bf16[1024,576]{0,1:T(8,128)(2,1)} collective-permute-done((bf16[1024,576]{0,1:T(8,128)(2,1)}, bf16[1024,576]{0,1:T(8,128)(2,1)}, u32[]{:S(2)}, u32[]{:S(2)}) %collective-permute-start) | collective-permute-done | bytes 1179680 | tf_op jit(solution)/shard_map/ppermute | solution.py:24
  83.2 8.2 fusion.86
  91.4 11.6 fusion.139
  103.0 8.1 fusion.2
  111.2 8.4 fusion.65
  131.0 8.4 mul.571
  146.3 13.6 reduce-scatter.18.cloned.1.call-done
  175.7 11.1 gather_fusion.2
  192.7 8.1 all-to-all-start
  201.4 65.2 %all-to-all-done = bf16[1,8,128,2048]{3,2,0,1:T(8,128)(2,1)} async-done(((bf16[1,8,128,2048]{3,2,0,1:T(8,128)(2,1)}), bf16[1,8,128,2048]{3,2,0,1:T(8,128)(2,1)}, u32[]{:S(2)}, u32[]{:S(2)}) %all-to-all-start) | async-done | bytes 4194336 | tf_op jit(solution)/shard_map/all_to_all | solution.py:84
  272.1 18.7 %fusion.13 = f32[1,1024,2816]{2,1,0:T(8,128)} fusion(bf16[1024,2048]{1,0:T(8,128)(2,1)} %bitcast.15, bf16[1,2048,2816]{2,1,0:T(8,128)(2,1)} %param.27), kind=kOutput, calls=%fused_computation.29 | convolution fusion | flops 11811160064 | bytes 27262976 | tf_op jit(solution)/shard_map/erd,edf->erf/dot_general | solution.py:214
  290.8 30.2 %all-to-all-done.2 = bf16[1,8,128,2048]{3,2,0,1:T(8,128)(2,1)} async-done(((bf16[1,8,128,2048]{3,2,0,1:T(8,128)(2,1)}), bf16[1,8,128,2048]{3,2,0,1:T(8,128)(2,1)}, u32[]{:S(2)}, u32[]{:S(2)}) %all-to-all-start.2) | async-done | bytes 4194336 | tf_op jit(solution)/shard_map/all_to_all | solution.py:84
  321.0 16.7 %fusion.41 = (bf16[1024,1408]{1,0:T(8,128)(2,1)}, bf16[1024,1408]{1,0:T(8,128)(2,1)}, bf16[1,1024,1408]{2,1,0:T(8,128)(2,1)S(1)}) fusion(f32[1,1024,2816]{2,1,0:T(8,128)} %fusion.13, bf16[1024,2048]{1,0:T(8,128)(2,1)} %bitcast.28, bf16[1,1408,2048]{2,1,0:T(8,128)(2,1)} %param.28), kind=kOutput, calls=%fused_computation.64 | convolution fusion | flops 5928648704 | bytes 30146560 | tf_op jit(solution)/shard_map/erd,efd->erf/dot_general | solution.py:243
  337.7 12.1 fusion.32
  355.7 18.0 %fusion.29 = bf16[1024,2048]{1,0:T(8,128)(2,1)} fusion(bf16[1,2048,2816]{2,1,0:T(8,128)(2,1)} %param.27, bf16[1024,1408]{1,0:T(8,128)(2,1)} %get-tuple-element.31, bf16[1024,1408]{1,0:T(8,128)(2,1)} %get-tuple-element.30), kind=kOutput, calls=%fused_computation.55 | convolution fusion | flops 11824791552 | bytes 21495808 | tf_op jit(solution)/shard_map/erf,edf->erd/dot_general | solution.py:246
  373.7 47.2 %all-to-all-done.1 = bf16[1,8,128,2048]{3,2,0,1:T(8,128)(2,1)} async-done(((bf16[1,8,128,2048]{3,2,0,1:T(8,128)(2,1)}), bf16[1,8,128,2048]{3,2,0,1:T(8,128)(2,1)}, u32[]{:S(2)}, u32[]{:S(2)}) %all-to-all-start.1) | async-done | bytes 4194336 | tf_op jit(solution)/shard_map/all_to_all | solution.py:84
  427.4 10.0 gather_fusion.1
  437.4 37.8 %all-to-all-done.3 = bf16[1,8,128,2048]{3,2,0,1:T(8,128)(2,1)} async-done(((bf16[1,8,128,2048]{3,2,0,1:T(8,128)(2,1)}), bf16[1,8,128,2048]{3,2,0,1:T(8,128)(2,1)}, u32[]{:S(2)}, u32[]{:S(2)}) %all-to-all-start.3) | async-done | bytes 4194336 | tf_op jit(solution)/shard_map/all_to_all | solution.py:84
  475.3 9.8 gather_fusion.3
  485.1 6.6 reshape.481
  491.7 6.5 reshape.480
  498.2 7.4 multiply_reduce_fusion.1
  505.8 6.9 fusion.27
  512.7 6.5 fusion.93
  526.4 7.0 reduce_sum.194
  543.1 34.7 %reduce-scatter.22.cloned.1.call-done = bf16[128,2048]{1,0:T(8,128)(2,1)} async-done(((bf16[1024,2048]{1,0:T(8,128)(2,1)}), bf16[128,2048]{1,0:T(8,128)(2,1)}) %reduce-scatter.22.cloned.1.call-update) | async-done | bytes 524304 | tf_op jit(solution)/shard_map/reduce_scatter | solution.py:78
  582.7 34.5 %all-gather.14.cloned.1.call-done = bf16[1024,2048]{1,0:T(8,128)(2,1)} async-done(((bf16[128,2048]{1,0:T(8,128)(2,1)}), bf16[1024,2048]{1,0:T(8,128)(2,1)}) %all-gather.14.cloned.1.call-update) | async-done | bytes 4194320 | tf_op jit(solution)/shard_map/all_gather | solution.py:74
  621.0 8.9 fusion.46
  630.0 11.1 multiply_reduce_fusion
  641.1 11.9 multiply_convert_fusion
  661.6 27.9 %collective-permute-done.1 = bf16[1024,576]{0,1:T(8,128)(2,1)S(1)} collective-permute-done((bf16[1024,576]{0,1:T(8,128)(2,1)S(1)}, bf16[1024,576]{0,1:T(8,128)(2,1)S(1)}, u32[]{:S(2)}, u32[]{:S(2)}) %collective-permute-start.1) | collective-permute-done | bytes 1179680 | tf_op jit(solution)/shard_map/ppermute | solution.py:24
  701.5 7.3 fusion.35
  713.5 10.5 fusion.12
  724.0 28.1 %copy.139 = bf16[1,1408,2048]{1,0,2:T(2,128)(2,1)} copy(bf16[1,1408,2048]{2,1,0:T(8,128)(2,1)} %fusion.12) | data formatting | bytes 11534336
  752.1 7.8 copy.146
  760.2 6.3 fusion.70
  766.6 6.5 fusion.69
  782.5 18.3 %convert_bitcast_fusion = bf16[1,2048,2816]{2,1,0:T(8,128)(2,1)} fusion(bf16[1024,2048]{1,0:T(8,128)(2,1)} %bitcast.15, bf16[1024,1408]{1,0:T(8,128)(2,1)} %get-tuple-element.31, bf16[1024,1408]{1,0:T(8,128)(2,1)} %get-tuple-element.30), kind=kOutput, calls=%fused_computation.20 | convolution fusion | flops 11828461568 | bytes 21495808 | tf_op jit(solution)/shard_map/erd,erf->edf/dot_general | solution.py:343
  800.9 7.3 fusion.145
  814.0 6.3 convert_element_type.246
  834.9 46.4 %reduce-scatter.30.cloned.1.call-done = bf16[128,704]{1,0:T(8,128)(2,1)} async-done(((bf16[2048,704]{1,0:T(8,128)(2,1)}), bf16[128,704]{1,0:T(8,128)(2,1)}) %reduce-scatter.30.cloned.1.call-update) | async-done | bytes 180240
  883.2 81.5 %reduce-scatter.34.cloned.1.call-done = bf16[128,1408]{1,0:T(8,128)(2,1)} async-done(((bf16[2048,1408]{1,0:T(8,128)(2,1)}), bf16[128,1408]{1,0:T(8,128)(2,1)}) %reduce-scatter.34.cloned.1.call-update) | async-done | bytes 360464
  970.2 94.6 %all-reduce.8.cloned.1.call-done = (bf16[2048,384]{1,0:T(8,128)(2,1)}, bf16[512,512]{1,0:T(8,128)(2,1)}, bf16[256,2048]{1,0:T(8,128)(2,1)}) async-done(((bf16[2048,384]{1,0:T(8,128)(2,1)}, bf16[512,512]{1,0:T(8,128)(2,1)}, bf16[256,2048]{1,0:T(8,128)(2,1)}), (bf16[2048,384]{1,0:T(8,128)(2,1)}, bf16[512,512]{1,0:T(8,128)(2,1)}, bf16[256,2048]{1,0:T(8,128)(2,1)})) %all-reduce.8.cloned.1.call-update) | async-done | bytes 3145744 | tf_op jit(solution)/shard_map/psum | solution.py:359
  1072.0 87.2 %reduce-scatter.26.cloned.1.call-done = bf16[1,128,2816]{2,1,0:T(8,128)(2,1)} async-done(((bf16[1,2048,2816]{2,1,0:T(8,128)(2,1)}), bf16[1,128,2816]{2,1,0:T(8,128)(2,1)}) %reduce-scatter.26.cloned.1.call-update) | async-done | bytes 720912 | tf_op jit(solution)/shard_map/reduce_scatter | solution.py:345
  1161.6 34.4 %reduce-scatter.24.cloned.1.call-done = bf16[128,2048]{1,0:T(8,128)(2,1)} async-done(((bf16[1024,2048]{1,0:T(8,128)(2,1)}), bf16[128,2048]{1,0:T(8,128)(2,1)}) %reduce-scatter.24.cloned.1.call-update) | async-done | bytes 524304 | tf_op jit(solution)/shard_map/reduce_scatter | solution.py:78
  1197.4 69.1 %all-reduce = (f32[2048]{0:T(1024)}, f32[512]{0:T(512)}, f32[2048]{0:T(1024)}) all-reduce(f32[2048]{0:T(1024)S(1)} %get-tuple-element.18, f32[512]{0:T(512)S(1)} %copy-done.55, f32[2048]{0:T(1024)S(1)} %copy-done.52), channel_id=1, replica_groups=mesh['seq'=16,'exp'=8] {'seq','exp'}, use_global_device_ids=true, to_apply=%region_28.29 | all-reduce | flops 4608 | bytes 36864 | tf_op jit(solution)/shard_map/psum | solution.py:363
  1270.3 129.3 %all-reduce.6.cloned.1.call-done = (f32[2048,576]{0,1:T(8,128)}, f32[2048,8]{0,1:T(8,128)}) async-done(((f32[2048,576]{0,1:T(8,128)}, f32[2048,8]{0,1:T(8,128)}), (f32[2048,576]{0,1:T(8,128)}, f32[2048,8]{0,1:T(8,128)})) %all-reduce.6.cloned.1.call-update) | async-done | bytes 4784144 | tf_op jit(solution)/shard_map/psum | solution.py:363
  (310 shorter events, 197.3 us)
Async XLA Ops:
  7.2 498.6 %copy-start = (bf16[2048,2,352]{0,2,1:T(8,128)(2,1)S(1)}, bf16[2048,2,352]{0,2,1:T(8,128)(2,1)}, u32[]{:S(2)}) copy-start(bf16[2048,2,352]{0,2,1:T(8,128)(2,1)} %param.25) | copy-start | bytes 8650756
  7.2 35.9 %all-gather.6.cloned.1.call-start = ((), (), s32[]{:S(2)}) async-start(), calls=%async_computation.13 | async-start | bytes 1327104 | tf_op jit(solution)/shard_map/all_gather | solution.py:165
  7.3 45.6 %copy-start.59 = (f32[32]{0:T(128)}, f32[32]{0:T(128)S(1)}, u32[]{:S(2)}) copy-start(f32[32]{0:T(128)S(1)} %multiply_exponential_fusion) | copy-start | bytes 388
  7.3 45.5 %copy-start.66 = (f32[128]{0:T(128)}, f32[128]{0:T(128)S(1)}, u32[]{:S(2)}) copy-start(f32[128]{0:T(128)S(1)} %fusion.128) | copy-start | bytes 1540
  15.6 62.9 %all-gather.8.cloned.1.call-start = ((), (), s32[]{:S(2)}) async-start(), calls=%async_computation.14 | async-start | bytes 4718592 | tf_op jit(solution)/shard_map/all_gather | solution.py:74
  16.3 143.6 %reduce-scatter.18.cloned.1.call-start = ((), (), s32[]{:S(2)}) async-start(), calls=%async_computation.15 | async-start | bytes 4718592 | tf_op jit(solution)/shard_map/reduce_scatter | solution.py:78
  43.1 28.5 %collective-permute-start = (bf16[1024,576]{0,1:T(8,128)(2,1)}, bf16[1024,576]{0,1:T(8,128)(2,1)}, u32[]{:S(2)}, u32[]{:S(2)}) collective-permute-start(bf16[1024,576]{0,1:T(8,128)(2,1)} %all-gather.6.cloned.1.call-done), channel_id=1, source_target_pairs={{0,8},{8,16},{16,24},{24,32},{32,40},{40,48},{48,56},{56,64},{64,7... | collective-permute-start | bytes 3538952 | tf_op jit(solution)/shard_map/ppermute | solution.py:24
  47.2 27.3 %copy-start.35 = (bf16[512,512]{1,0:T(8,128)(2,1)S(1)}, bf16[512,512]{1,0:T(8,128)(2,1)}, u32[]{:S(2)}) copy-start(bf16[512,512]{1,0:T(8,128)(2,1)} %param.21) | copy-start | bytes 1572868
  49.4 42.0 %copy-start.28 = (f32[1024,32]{0,1:T(8,128)}, f32[1024,32]{0,1:T(8,128)S(1)}, u32[]{:S(2)}) copy-start(f32[1024,32]{0,1:T(8,128)S(1)} %get-tuple-element.50) | copy-start | bytes 393220
  131.0 29.0 %copy-start.4 = (bf16[128,2048]{1,0:T(8,128)(2,1)S(1)}, bf16[128,2048]{1,0:T(8,128)(2,1)}, u32[]{:S(2)}) copy-start(bf16[128,2048]{1,0:T(8,128)(2,1)} %param.16) | copy-start | bytes 1572868
  131.0 30.9 %copy-start.39 = (f32[2048]{0:T(1024)S(1)}, f32[2048]{0:T(1024)}, u32[]{:S(2)}) copy-start(f32[2048]{0:T(1024)} %param.23) | copy-start | bytes 24580
  131.0 32.3 %copy-start.37 = (f32[2048,8]{0,1:T(8,128)S(1)}, f32[2048,8]{0,1:T(8,128)}, u32[]{:S(2)}) copy-start(f32[2048,8]{0,1:T(8,128)} %param.24) | copy-start | bytes 196612
  192.7 73.9 %all-to-all-start = ((bf16[1,8,128,2048]{3,2,0,1:T(8,128)(2,1)}), bf16[1,8,128,2048]{3,2,0,1:T(8,128)(2,1)}, u32[]{:S(2)}, u32[]{:S(2)}) async-start(bf16[1,8,128,2048]{3,2,0,1:T(8,128)(2,1)} %get-tuple-element.54), calls=%async_computation.2 | async-start | bytes 8388608 | tf_op jit(solution)/shard_map/all_to_all | solution.py:84
  200.8 304.9 %all-gather.10.cloned.1.call-start = ((), (), s32[]{:S(2)}) async-start(), calls=%async_computation.16 | async-start | bytes 4718592 | tf_op jit(solution)/shard_map/all_gather | solution.py:74
  266.6 54.4 %all-to-all-start.2 = ((bf16[1,8,128,2048]{3,2,0,1:T(8,128)(2,1)}), bf16[1,8,128,2048]{3,2,0,1:T(8,128)(2,1)}, u32[]{:S(2)}, u32[]{:S(2)}) async-start(bf16[1,8,128,2048]{3,2,0,1:T(8,128)(2,1)} %get-tuple-element.53), calls=%async_computation.4 | async-start | bytes 8388608 | tf_op jit(solution)/shard_map/all_to_all | solution.py:84
  349.8 71.1 %all-to-all-start.1 = ((bf16[1,8,128,2048]{3,2,0,1:T(8,128)(2,1)}), bf16[1,8,128,2048]{3,2,0,1:T(8,128)(2,1)}, u32[]{:S(2)}, u32[]{:S(2)}) async-start(bf16[1,8,128,2048]{3,2,0,1:T(8,128)(2,1)} %bitcast.213), calls=%async_computation.3 | async-start | bytes 8388608 | tf_op jit(solution)/shard_map/all_to_all | solution.py:84
  355.1 157.6 %all-gather.12.cloned.1.call-start = ((), (), s32[]{:S(2)}) async-start(), calls=%async_computation.18 | async-start | bytes 4718592 | tf_op jit(solution)/shard_map/all_gather | solution.py:74
  420.9 54.4 %all-to-all-start.3 = ((bf16[1,8,128,2048]{3,2,0,1:T(8,128)(2,1)}), bf16[1,8,128,2048]{3,2,0,1:T(8,128)(2,1)}, u32[]{:S(2)}, u32[]{:S(2)}) async-start(bf16[1,8,128,2048]{3,2,0,1:T(8,128)(2,1)} %bitcast.212), calls=%async_computation.5 | async-start | bytes 8388608 | tf_op jit(solution)/shard_map/all_to_all | solution.py:84
  426.3 151.5 %reduce-scatter.22.cloned.1.call-start = ((), (), s32[]{:S(2)}) async-start(), calls=%async_computation.19 | async-start | bytes 4718592 | tf_op jit(solution)/shard_map/reduce_scatter | solution.py:78
  505.7 27.7 %copy-start.47 = (f32[128,8]{0,1:T(8,128)}, f32[128,8]{0,1:T(8,128)S(1)}, u32[]{:S(2)}) copy-start(f32[128,8]{0,1:T(8,128)S(1)} %select_reduce_fusion) | copy-start | bytes 12292
  505.7 27.7 %copy-start.61 = (f32[128]{0:T(128)}, f32[128]{0:T(128)S(1)}, u32[]{:S(2)}) copy-start(f32[128]{0:T(128)S(1)} %multiply_reduce_fusion.7) | copy-start | bytes 1540
  543.0 34.8 %copy-start.5 = (bf16[128,2048]{1,0:T(8,128)(2,1)S(1)}, bf16[128,2048]{1,0:T(8,128)(2,1)}, u32[]{:S(2)}) copy-start(bf16[128,2048]{1,0:T(8,128)(2,1)} %param.16) | copy-start | bytes 1572868
  543.0 34.8 %copy-start.40 = (f32[2048]{0:T(1024)S(1)}, f32[2048]{0:T(1024)}, u32[]{:S(2)}) copy-start(f32[2048]{0:T(1024)} %param.23) | copy-start | bytes 24580
  543.0 34.8 %copy-start.57 = (f32[128]{0:T(128)S(1)}, f32[128]{0:T(128)}, u32[]{:S(2)}) copy-start(f32[128]{0:T(128)} %copy-done.56) | copy-start | bytes 1540
  543.0 37.0 %copy-start.68 = (f32[128]{0:T(128)S(1)}, f32[128]{0:T(128)}, u32[]{:S(2)}) copy-start(f32[128]{0:T(128)} %get-tuple-element.59) | copy-start | bytes 1540
  543.0 39.7 %copy-start.44 = (f32[2,1024]{1,0:T(2,128)S(1)}, f32[2,1024]{1,0:T(2,128)}, u32[]{:S(2)}) copy-start(f32[2,1024]{1,0:T(2,128)} %copy-done.43) | copy-start | bytes 24580
  543.0 39.7 %copy-start.51 = (f32[2,1024]{1,0:T(2,128)S(1)}, f32[2,1024]{1,0:T(2,128)}, u32[]{:S(2)}) copy-start(f32[2,1024]{1,0:T(2,128)} %copy-done.50) | copy-start | bytes 24580
  543.1 74.2 %all-gather.14.cloned.1.call-start = ((), (), s32[]{:S(2)}) async-start(), calls=%async_computation.20 | async-start | bytes 4718592 | tf_op jit(solution)/shard_map/all_gather | solution.py:74
  580.0 41.0 %copy-start.70 = (f32[128]{0:T(128)}, f32[128]{0:T(128)S(1)}, u32[]{:S(2)}) copy-start(f32[128]{0:T(128)S(1)} %broadcast_multiply_fusion.4) | copy-start | bytes 1540
  582.6 225.5 %reduce-scatter.28.cloned.1.call-start = ((), (), s32[]{:S(2)}) async-start(), calls=%async_computation.23 | async-start | bytes 1474560
  660.3 29.2 %collective-permute-start.1 = (bf16[1024,576]{0,1:T(8,128)(2,1)S(1)}, bf16[1024,576]{0,1:T(8,128)(2,1)S(1)}, u32[]{:S(2)}, u32[]{:S(2)}) collective-permute-start(bf16[1024,576]{0,1:T(8,128)(2,1)S(1)} %fusion.56), channel_id=1, source_target_pairs={{8,0},{16,8},{24,16},{32,24},{40,32},{48,40},{56,48},{64,56},{72,6... | collective-permute-start | bytes 3538952 | tf_op jit(solution)/shard_map/ppermute | solution.py:24
  693.4 139.8 %reduce-scatter.32.cloned.1.call-start = ((), (), s32[]{:S(2)}) async-start(), calls=%async_computation.25 | async-start | bytes 1671168
  701.2 180.1 %reduce-scatter.30.cloned.1.call-start = ((), (), s32[]{:S(2)}) async-start(), calls=%async_computation.24 | async-start | bytes 3342336
  713.4 251.2 %reduce-scatter.34.cloned.1.call-start = ((), (), s32[]{:S(2)}) async-start(), calls=%async_computation.26 | async-start | bytes 6127616
  759.9 305.0 %all-reduce.8.cloned.1.call-start = ((), (), s32[]{:S(2)}) async-start(), calls=%async_computation.28 | async-start | bytes 6291456 | tf_op jit(solution)/shard_map/psum | solution.py:359
  781.9 377.3 %reduce-scatter.26.cloned.1.call-start = ((), (), s32[]{:S(2)}) async-start(), calls=%async_computation.22 | async-start | bytes 12255232 | tf_op jit(solution)/shard_map/reduce_scatter | solution.py:345
  800.8 395.1 %reduce-scatter.24.cloned.1.call-start = ((), (), s32[]{:S(2)}) async-start(), calls=%async_computation.21 | async-start | bytes 4718592 | tf_op jit(solution)/shard_map/reduce_scatter | solution.py:78
  820.3 446.2 %reduce-scatter.20.cloned.1.call-start = ((), (), s32[]{:S(2)}) async-start(), calls=%async_computation.17 | async-start | bytes 4718592 | tf_op jit(solution)/shard_map/reduce_scatter | solution.py:78
  826.5 573.1 %all-reduce.6.cloned.1.call-start = ((), (), s32[]{:S(2)}) async-start(), calls=%async_computation.27 | async-start | bytes 9568256 | tf_op jit(solution)/shard_map/psum | solution.py:363
  1067.1 128.9 %copy-start.6 = (bf16[128,2048]{1,0:T(8,128)(2,1)S(1)}, bf16[128,2048]{1,0:T(8,128)(2,1)}, u32[]{:S(2)}) copy-start(bf16[128,2048]{1,0:T(8,128)(2,1)} %param.16) | copy-start | bytes 1572868
  1067.1 128.9 %copy-start.41 = (f32[2048]{0:T(1024)S(1)}, f32[2048]{0:T(1024)}, u32[]{:S(2)}) copy-start(f32[2048]{0:T(1024)} %param.17) | copy-start | bytes 24580
  1067.1 128.9 %copy-start.65 = (f32[128]{0:T(128)S(1)}, f32[128]{0:T(128)}, u32[]{:S(2)}) copy-start(f32[128]{0:T(128)} %copy-done.64) | copy-start | bytes 1540
  1070.4 126.9 %copy-start.52 = (f32[2048]{0:T(1024)S(1)}, f32[2048]{0:T(1024)}, u32[]{:S(2)}) copy-start(f32[2048]{0:T(1024)} %get-tuple-element.16) | copy-start | bytes 24580
  1070.4 126.9 %copy-start.55 = (f32[512]{0:T(512)S(1)}, f32[512]{0:T(512)}, u32[]{:S(2)}) copy-start(f32[512]{0:T(512)} %get-tuple-element.20) | copy-start | bytes 6148
  1070.4 196.0 %copy-start.58 = (f32[128]{0:T(128)S(1)}, f32[128]{0:T(128)}, u32[]{:S(2)}) copy-start(f32[128]{0:T(128)} %copy-done.56) | copy-start | bytes 1540
  1070.4 196.0 %copy-start.69 = (f32[128]{0:T(128)S(1)}, f32[128]{0:T(128)}, u32[]{:S(2)}) copy-start(f32[128]{0:T(128)} %get-tuple-element.59) | copy-start | bytes 1540
  1070.4 196.1 %copy-start.71 = (f32[128]{0:T(128)S(1)}, f32[128]{0:T(128)}, u32[]{:S(2)}) copy-start(f32[128]{0:T(128)} %copy-done.70) | copy-start | bytes 1540
  1070.5 196.1 %copy-start.73 = (f32[128]{0:T(128)S(1)}, f32[128]{0:T(128)}, u32[]{:S(2)}) copy-start(f32[128]{0:T(128)} %get-tuple-element.55) | copy-start | bytes 1540
  (53 other events, 315.4 us)
Sparse Core Ops, SparseCore 0:
  15.7 27.3 all-gather.5
  45.4 33.0 all-gather.7
  123.9 36.0 reduce-scatter.17
  203.6 52.8 all-gather.9
  357.3 53.4 all-gather.11
  543.2 34.6 reduce-scatter.21
  582.8 34.4 all-gather.13
  693.5 31.6 reduce-scatter.27
  728.4 73.9 reduce-scatter.31
  806.2 75.0 reduce-scatter.29
  884.7 79.9 reduce-scatter.33
  968.8 96.0 all-reduce.7
  1068.3 90.8 reduce-scatter.25
  1161.7 34.2 reduce-scatter.23
  1198.4 37.0 reduce-scatter.19
  1242.4 157.2 all-reduce.5
where the time goes:
time: 1420 us; the launch traced here: 1410 us
  waiting for transfers between devices  813 us (57%)
  matrix products  243 us (17%)
  local copies, waits for them, and re-layouts  141 us (10%)
  other arithmetic  99.3 us (7%)
  blocking collectives  69.1 us (5%)
  starting transfers between devices  31.4 us (2%)
  between operations  15.2 us (1%)
    all_to_all x4, waiting for transfers between devices, route_move(): lax.all_to_all(tensor, 'exp', split_axis=1, concat_axis=1, tiled=True)  180 us
    unnamed x20, waiting for transfers between devices  130 us
    psum x1, waiting for transfers between devices, local(): lax.psum((latent_term, attn_gain_term, latent_gain_term, ffn_gain_term, r...  129 us
    psum x1, waiting for transfers between devices, local(): lax.psum(query_term.astype(jnp.bfloat16), 'seq').astype(jnp.float32)  94.6 us
    reduce_scatter x1, waiting for transfers between devices, local(): lax.psum_scatter(expert_gate_term.astype(jnp.bfloat16), 'seq', scatter_di...  87.2 us
    reduce_scatter x4, waiting for transfers between devices, sum_rows(): lax.psum_scatter(tensor.astype(jnp.bfloat16), 'exp', scatter_dimension=0,...  82.8 us
    unnamed x172, local copies, waits for them, and re-layouts  69.9 us
    psum x1, blocking collectives, local(): lax.psum((latent_term, attn_gain_term, latent_gain_term, ffn_gain_term, r...  69.1 us
  transfers between devices with their start and end apart: 22, of which 17 were waited for; matrix products, arithmetic and copies ran while one was open for 22% of the time, Pallas kernels for 0%

commit v1 on v0

--- a/solution.py
+++ b/solution.py
@@ -18,10 +18,10 @@
 EPSILON = 1e-06
 
 
-def shifted(block, axis, distance):
-    devices = range(lax.axis_size(axis))
-    route = [(i - distance, i) for i in devices if i - distance in devices]
-    return lax.ppermute(block, axis, route)
+def shifted_pair(block, distance):
+    pairs = range(0, lax.axis_size("seq"), 2)
+    route = [(i, i + 1) if distance > 0 else (i + 1, i) for i in pairs]
+    return lax.ppermute(block, "seq", route)
 
 
 def rms_scale(tensor, gain_vec):
@@ -78,10 +78,6 @@
     return lax.psum_scatter(
         tensor.astype(jnp.bfloat16), "exp", scatter_dimension=0, tiled=True
     ).astype(jnp.float32)
-
-
-def route_move(tensor):
-    return lax.all_to_all(tensor, "exp", split_axis=1, concat_axis=1, tiled=True)
 
 
 def add_own(full_term, own_term, row_offset):
@@ -135,9 +131,6 @@
     block_rows = own_rows * exp_count
     key_rows = 2 * block_rows
     head_count = query_proj.shape[1] // (NOPE + ROPE)
-    per_device = expert_gate_up.shape[0]
-    capacity = 4 * own_rows * TOP // (3 * EXPERTS)
-    slot_total = EXPERTS * capacity
     score_scale = (NOPE + ROPE) ** (-0.5)
     block_start = lax.axis_index("seq") * block_rows
     row_offset = lax.axis_index("exp") * own_rows
@@ -161,10 +154,15 @@
     latent_raw = jnp.dot(normed_low, latent_proj, preferred_element_type=f32)
     latent_normed = rms_scale(latent_raw[:, :LAT], latent_gain).astype(bf16)
     rope_key = rotate(latent_raw[:, LAT:], own_pos % key_rows, 1.0).astype(bf16)
+    hot = jnp.sum(
+        expert_routes[:, :, None] == jnp.arange(EXPERTS, dtype=jnp.int32)[None, None, :], axis=1
+    ).astype(bf16)
     key_latent = jnp.concatenate([latent_normed, rope_key], axis=-1)
-    block_keys = lax.all_gather(key_latent, "exp", axis=0, tiled=True)
-    prev_keys = shifted(block_keys, "seq", 1)
-    keys_all = jnp.concatenate([prev_keys, block_keys], axis=0)
+    prev_latent = shifted_pair(key_latent, 1)
+    gathered = gather_rows(jnp.concatenate([key_latent, prev_latent, hot], axis=-1))
+    width = LAT + ROPE
+    keys_all = jnp.concatenate([gathered[:, width : 2 * width], gathered[:, :width]], axis=0)
+    hot_all = gathered[:, 2 * width :].astype(f32)
     latent_all = keys_all[:, :LAT]
     rope_all = keys_all[:, LAT:]
     packed = expand_keys(latent_all, kv_proj, head_count)
@@ -182,84 +180,50 @@
     residual = input_f + attn_rows
     mid_low = rms_scale(residual, ffn_gain).astype(bf16)
     mid_all = gather_rows(mid_low)
-    shared_pre = jnp.einsum("td,dgf->tgf", mid_all, shared_gate_up, preferred_element_type=f32)
-    shared_act = (silu(shared_pre[:, 0]) * shared_pre[:, 1]).astype(bf16)
-    shared_part = jnp.dot(shared_act, shared_down, preferred_element_type=f32)
-    logits = jnp.dot(mid_low.astype(f32), router_proj, precision=highest)
+    grad_f = out_grad.astype(f32)
+    grad_all = gather_rows(out_grad)
+    router_high = lax.reduce_precision(router_proj, 8, 7)
+    router_rest = router_proj - router_high
+    router_mid = lax.reduce_precision(router_rest, 8, 7)
+    router_low = router_rest - router_mid
+    logits = jnp.dot(
+        mid_all,
+        jnp.concatenate([router_high, router_mid, router_low], axis=1).astype(bf16),
+        preferred_element_type=f32,
+    )
+    logits = logits[:, :EXPERTS] + (logits[:, EXPERTS : 2 * EXPERTS] + logits[:, 2 * EXPERTS :])
     logit_top = jnp.max(logits, axis=-1, keepdims=True)
     logit_exp = jnp.exp(logits - logit_top)
     gate_probs = logit_exp / jnp.sum(logit_exp, axis=-1, keepdims=True)
-    route_hot = (
-        expert_routes[:, :, None] == jnp.arange(EXPERTS, dtype=jnp.int32)[None, None, :]
-    ).astype(f32)
-    route_weights = jnp.sum(route_hot * gate_probs[:, None, :], axis=-1)
-    flat_routes = expert_routes.reshape(own_rows * TOP)
-    flat_hot = (flat_routes[:, None] == jnp.arange(EXPERTS, dtype=jnp.int32)[None, :]).astype(
-        jnp.int32
-    )
-    rank_in = jnp.sum((jnp.cumsum(flat_hot, axis=0) - flat_hot) * flat_hot, axis=1)
-    slot_index = (
-        flat_routes % per_device * exp_count + flat_routes // per_device
-    ) * capacity + rank_in
-    slot_source = (
-        jnp.zeros((slot_total,), jnp.int32)
-        .at[slot_index]
-        .set(jnp.arange(own_rows * TOP, dtype=jnp.int32))
-    )
-    slot_used = jnp.zeros((slot_total,), jnp.bool_).at[slot_index].set(True)
-    send_rows = jnp.where(slot_used[:, None], mid_low[slot_source // TOP], jnp.zeros((), bf16))
-    arrived = route_move(send_rows.reshape(per_device, exp_count, capacity, model_width)).reshape(
-        per_device, exp_count * capacity, model_width
-    )
-    expert_pre = jnp.einsum("erd,edf->erf", arrived, expert_gate_up, preferred_element_type=f32)
-    expert_act = (silu(expert_pre[..., :F]) * expert_pre[..., F:]).astype(bf16)
-    expert_out = jnp.einsum(
-        "erf,efd->erd", expert_act, expert_down, preferred_element_type=f32
-    ).astype(bf16)
-    came_back = route_move(
-        expert_out.reshape(per_device, exp_count, capacity, model_width)
-    ).reshape(slot_total, model_width)
-    route_out = came_back[slot_index].reshape(own_rows, TOP, model_width)
-    routed = jnp.sum(route_weights[:, :, None] * route_out.astype(f32), axis=1)
-    moe_rows = sum_rows(shared_part) + routed
-    layer_output = (residual + moe_rows).astype(bf16)
-    grad_f = out_grad.astype(f32)
-    grad_all = gather_rows(out_grad)
-    shared_dact = jnp.einsum("td,fd->tf", grad_all, shared_down, preferred_element_type=f32)
-    shared_dgate, shared_dup = silu_back(shared_pre[:, 0], shared_pre[:, 1], shared_dact)
-    shared_dpre = jnp.stack([shared_dgate, shared_dup], axis=1).astype(bf16)
-    mid_grad_all = jnp.einsum(
-        "tgf,dgf->td", shared_dpre, shared_gate_up, preferred_element_type=f32
-    )
-    route_grad = (
-        (route_weights[:, :, None] * grad_f[:, None, :])
-        .astype(bf16)
-        .reshape(own_rows * TOP, model_width)
-    )
-    send_grad = jnp.where(slot_used[:, None], route_grad[slot_source], jnp.zeros((), bf16))
-    grad_arrived = route_move(
-        send_grad.reshape(per_device, exp_count, capacity, model_width)
-    ).reshape(per_device, exp_count * capacity, model_width)
-    expert_dact = jnp.einsum("erd,efd->erf", grad_arrived, expert_down, preferred_element_type=f32)
-    expert_dgate, expert_dup = silu_back(expert_pre[..., :F], expert_pre[..., F:], expert_dact)
-    expert_dpre = jnp.concatenate([expert_dgate, expert_dup], axis=-1).astype(bf16)
-    row_back = jnp.einsum(
-        "erf,edf->erd", expert_dpre, expert_gate_up, preferred_element_type=f32
-    ).astype(bf16)
-    back_home = route_move(row_back.reshape(per_device, exp_count, capacity, model_width)).reshape(
-        slot_total, model_width
-    )
-    route_in_grad = jnp.sum(
-        back_home[slot_index].reshape(own_rows, TOP, model_width).astype(f32), axis=1
-    )
-    weight_grad = jnp.sum(route_out.astype(f32) * grad_f[:, None, :], axis=-1)
-    gate_grad = jnp.sum(route_hot * weight_grad[:, :, None], axis=1)
-    logit_grad = gate_probs * (gate_grad - jnp.sum(gate_probs * gate_grad, axis=-1, keepdims=True))
-    router_term = jnp.einsum("td,te->de", mid_low.astype(f32), logit_grad, precision=highest)
-    mid_grad_own = route_in_grad + jnp.einsum(
-        "te,de->td", logit_grad, router_proj, precision=highest
-    )
-    mid_grad = sum_rows(add_own(mid_grad_all, mid_grad_own, row_offset))
+    own_expert = (jnp.arange(EXPERTS) == lax.axis_index("exp")).astype(f32)[None, :]
+    own_prob = jnp.sum(gate_probs * hot_all * own_expert, axis=1, keepdims=True)
+    shared_gate = jnp.dot(mid_all, shared_gate_up[:, 0], preferred_element_type=f32)
+    shared_up = jnp.dot(mid_all, shared_gate_up[:, 1], preferred_element_type=f32)
+    shared_act = silu(shared_gate) * shared_up
+    expert_pre = jnp.dot(mid_all, expert_gate_up[0], preferred_element_type=f32)
+    expert_gate, expert_up = expert_pre[:, :F], expert_pre[:, F:]
+    expert_act = silu(expert_gate) * expert_up
+    act_all = jnp.concatenate([shared_act, expert_act * own_prob], axis=1).astype(bf16)
+    down_all = jnp.concatenate([shared_down, expert_down[0]], axis=0)
+    moe_part = jnp.dot(act_all, down_all, preferred_element_type=f32)
+    dact_all = jnp.einsum("td,fd->tf", grad_all, down_all, preferred_element_type=f32)
+    shared_width = shared_down.shape[0]
+    shared_dgate, shared_dup = silu_back(shared_gate, shared_up, dact_all[:, :shared_width])
+    expert_dact = dact_all[:, shared_width:]
+    weight_grad = jnp.sum(expert_act * expert_dact, axis=1, keepdims=True)
+    expert_dgate, expert_dup = silu_back(expert_gate, expert_up, expert_dact * own_prob)
+    logit_term = (own_prob * weight_grad) * (own_expert - gate_probs)
+    shared_dpre = jnp.concatenate([shared_dgate, shared_dup], axis=1).astype(bf16)
+    expert_dpre = jnp.concatenate([expert_dgate, expert_dup], axis=1).astype(bf16)
+    shared_both = jnp.concatenate([shared_gate_up[:, 0], shared_gate_up[:, 1]], axis=1)
+    mid_grad_all = (
+        jnp.einsum("tf,df->td", shared_dpre, shared_both, preferred_element_type=f32)
+        + jnp.einsum("tf,df->td", expert_dpre, expert_gate_up[0], preferred_element_type=f32)
+        + jnp.einsum("te,de->td", logit_term, router_proj, preferred_element_type=f32)
+    )
+    mid_grad = sum_rows(mid_grad_all)
+    router_term = jnp.einsum("td,te->de", mid_all, logit_term.astype(bf16), preferred_element_type=f32)
+    layer_output = (residual + sum_rows(moe_part)).astype(bf16)
     mid_input_grad, ffn_gain_term = rms_back(residual, ffn_gain, mid_grad)
     residual_grad = grad_f + mid_input_grad
     attn_grad_all = gather_rows(residual_grad.astype(bf16))
@@ -269,12 +233,8 @@
         .astype(bf16)
         .reshape(block_rows, head_count, VDIM)
     )
-    block_back = lax.all_gather(key_latent, "exp", axis=0, tiled=True)
-    prev_back = shifted(block_back, "seq", 1)
-    keys_back = jnp.concatenate([prev_back, block_back], axis=0)
-    latent_back = keys_back[:, :LAT]
-    rope_back = keys_back[:, LAT:]
-    packed_back = expand_keys(latent_back, kv_proj, head_count)
+    latent_back, rope_back = latent_all, rope_all
+    packed_back = packed
     scores_back = score_block(
         queries, packed_back, rope_back, query_pos, query_seg, key_pos, key_seg
     )
@@ -315,13 +275,10 @@
     kv_term = jnp.einsum("tl,tc->lc", latent_back, packed_grad, preferred_element_type=f32)
     latent_grad_all = jnp.einsum("tc,lc->tl", packed_grad, kv_proj, preferred_element_type=f32)
     key_grad = jnp.concatenate([latent_grad_all, rope_key_grad], axis=-1)
-    prev_grad = shifted(key_grad[:block_rows].astype(jnp.bfloat16), "seq", -1).astype(jnp.float32)
-    own_key_grad = lax.psum_scatter(
-        (key_grad[block_rows:] + prev_grad).astype(jnp.bfloat16),
-        "exp",
-        scatter_dimension=0,
-        tiled=True,
-    ).astype(jnp.float32)
+    both_grad = sum_rows(jnp.concatenate([key_grad[block_rows:], key_grad[:block_rows]], axis=1))
+    own_key_grad = both_grad[:, :width] + shifted_pair(
+        both_grad[:, width:].astype(bf16), -1
+    ).astype(f32)
     latent_own = own_key_grad[:, :LAT]
     rope_own = own_key_grad[:, LAT:]
     query_term = jnp.einsum("td,tc->dc", normed_all, query_raw_grad, preferred_element_type=f32)
@@ -330,38 +287,45 @@
     latent_raw_grad = jnp.concatenate(
         [latent_pre_grad, rotate(rope_own, own_pos % key_rows, -1.0)], axis=-1
     ).astype(bf16)
-    latent_term = jnp.einsum("td,tc->dc", normed_low, latent_raw_grad, preferred_element_type=f32)
+    latent_raw_all = gather_rows(latent_raw_grad)
+    slice_width = model_width // exp_count
+    normed_slice = lax.dynamic_slice_in_dim(
+        normed_all, lax.axis_index("exp") * slice_width, slice_width, 1
+    )
+    latent_term = jnp.einsum("td,tc->dc", normed_slice, latent_raw_all, preferred_element_type=f32)
     in_grad_own = jnp.einsum("tc,dc->td", latent_raw_grad, latent_proj, preferred_element_type=f32)
     normed_grad = sum_rows(add_own(in_grad_all, in_grad_own, row_offset))
     input_part, attn_gain_term = rms_back(input_f, attn_gain, normed_grad)
     input_grad = (residual_grad + input_part).astype(bf16)
-    shared_down_term = jnp.einsum("tf,td->fd", shared_act, grad_all, preferred_element_type=f32)
-    shared_gate_term = jnp.einsum("td,tgf->dgf", mid_all, shared_dpre, preferred_element_type=f32)
-    expert_down_term = jnp.einsum(
-        "erf,erd->efd", expert_act, grad_arrived, preferred_element_type=f32
-    )
-    expert_gate_term = jnp.einsum("erd,erf->edf", arrived, expert_dpre, preferred_element_type=f32)
-    expert_gate_sum, expert_down_sum, shared_gate_sum, shared_down_sum = (
-        lax.psum_scatter(
-            expert_gate_term.astype(jnp.bfloat16), "seq", scatter_dimension=1, tiled=True
-        ).astype(jnp.float32),
-        lax.psum_scatter(
-            expert_down_term.astype(jnp.bfloat16), "seq", scatter_dimension=2, tiled=True
-        ).astype(jnp.float32),
-        lax.psum_scatter(
-            shared_gate_term.astype(jnp.bfloat16), "seq", scatter_dimension=0, tiled=True
-        ).astype(jnp.float32),
-        lax.psum_scatter(
-            shared_down_term.astype(jnp.bfloat16), "seq", scatter_dimension=1, tiled=True
-        ).astype(jnp.float32),
-    )
-    query_sum, kv_sum, output_sum = (
-        lax.psum(query_term.astype(jnp.bfloat16), "seq").astype(jnp.float32),
-        lax.psum(kv_term.astype(jnp.bfloat16), "seq").astype(jnp.float32),
-        lax.psum(output_term.astype(jnp.bfloat16), "seq").astype(jnp.float32),
-    )
-    latent_sum, attn_gain_sum, latent_gain_sum, ffn_gain_sum, router_sum = lax.psum(
-        (latent_term, attn_gain_term, latent_gain_term, ffn_gain_term, router_term), ("seq", "exp")
+    down_term = jnp.einsum("td,tf->df", grad_all, act_all, preferred_element_type=f32)
+    gate_term = jnp.einsum(
+        "td,tf->df",
+        mid_all,
+        jnp.concatenate([expert_dpre, shared_dpre], axis=1),
+        preferred_element_type=f32,
+    )
+    down_sum = lax.psum_scatter(
+        down_term.astype(bf16), "seq", scatter_dimension=0, tiled=True
+    ).astype(f32)
+    gate_sum = lax.psum_scatter(
+        gate_term.astype(bf16), "seq", scatter_dimension=0, tiled=True
+    ).astype(f32)
+    shared_down_sum = down_sum[:, :shared_width].T
+    expert_down_sum = down_sum[:, shared_width:].T[None]
+    expert_gate_sum = gate_sum[None, :, : 2 * F]
+    shared_gate_sum = gate_sum[:, 2 * F :].reshape(own_rows, 2, shared_width)
+    query_sum, kv_sum, output_sum, latent_sum = (
+        term.astype(f32)
+        for term in lax.psum(
+            tuple(
+                term.astype(bf16) for term in (query_term, kv_term, output_term, latent_term)
+            ),
+            "seq",
+        )
+    )
+    latent_sum = gather_rows(latent_sum.astype(bf16)).astype(f32)
+    attn_gain_sum, latent_gain_sum, ffn_gain_sum, router_sum = lax.psum(
+        (attn_gain_term, latent_gain_term, ffn_gain_term, router_term), ("seq", "exp")
     )
     return (
         layer_output,

time: 1420 us -> 1070 us (0.75)
  waiting for transfers between devices: 813 us -> 613 us
  local copies, waits for them, and re-layouts: 141 us -> 64.7 us
  other arithmetic: 99.3 us -> 68.5 us
  starting transfers between devices: 31.4 us -> 7.15 us
  matrix products: 243 us -> 219 us
    all_to_all x4 -> x0, waiting for transfers between devices: 180 us -> none  [route_move(): lax.all_to_all(tensor, 'exp', split_axis=1, concat_axis=1, tiled=True)]
    all_gather x4 -> x7, waiting for transfers between devices: 35.9 us -> 152 us  [gather_rows(): return lax.all_gather(tensor, 'exp', axis=0, tiled=True)]
    psum x2, waiting for transfers between devices: 224 us -> 113 us  [the longest x1 98.9 us: local(): lax.psum((attn_gain_term, latent_gain_term, ffn_gain_term, router_term),...]
    reduce_scatter x1 -> x0, waiting for transfers between devices: 87.2 us -> none  [local(): lax.psum_scatter(expert_gate_term.astype(jnp.bfloat16), 'seq', scatter_di...]
    unnamed x20 -> x19, waiting for transfers between devices: 130 us -> 212 us
    reduce_scatter x4, waiting for transfers between devices: 82.8 us -> 134 us  [sum_rows(): lax.psum_scatter(tensor.astype(jnp.bfloat16), 'exp', scatter_dimension=0,...]
    ppermute x2, waiting for transfers between devices: 46.6 us -> 2.46 us  [shifted_pair(): return lax.ppermute(block, 'seq', route)]
    gather x4 -> x0, local copies, waits for them, and re-layouts: 37 us -> none  [the longest x1 11.1 us: local(): route_grad[slot_source]]
  transfers between devices with their start and end apart: 22 -> 18, of which waited for: 17 -> 16; matrix products, arithmetic and copies ran while one was open for 22% -> 16% of each run, Pallas kernels for 0% -> 0%
where the time goes in v1:
time: 1070 us; the launch traced here: 1060 us
  waiting for transfers between devices  613 us (57%)
  matrix products  219 us (20%)
  blocking collectives  69.3 us (6%)
  other arithmetic  68.5 us (6%)
  local copies, waits for them, and re-layouts  64.7 us (6%)
  between operations  15.6 us (1%)
    unnamed x19, waiting for transfers between devices  212 us
    all_gather x7, waiting for transfers between devices, gather_rows(): return lax.all_gather(tensor, 'exp', axis=0, tiled=True)  152 us
    reduce_scatter x4, waiting for transfers between devices, sum_rows(): lax.psum_scatter(tensor.astype(jnp.bfloat16), 'exp', scatter_dimension=0,...  134 us
    psum x1, waiting for transfers between devices, local(): lax.psum((attn_gain_term, latent_gain_term, ffn_gain_term, router_term),...  98.9 us
    psum x1, blocking collectives, local(): lax.psum((attn_gain_term, latent_gain_term, ffn_gain_term, router_term),...  69.3 us
    unnamed x188, local copies, waits for them, and re-layouts  53.5 us
    dot_general x1, matrix products, local(): jnp.einsum('td,tf->df', mid_all, jnp.concatenate([expert_dpre, shared_dpr...  23.8 us
  transfers between devices with their start and end apart: 18, of which 16 were waited for; matrix products, arithmetic and copies ran while one was open for 16% of the time, Pallas kernels for 0%

profile of v1, /device:TPU:1, one launch (start us, length us, event | category | flops | bytes accessed | tf_op | source)
XLA Modules:
  0.0 1057.8 jit_solution(15395125448431316529)
XLA Ops:
  12.4 4.0 collective-permute-start
  22.6 3.5 compare_and_fusion
  26.1 26.6 %all-gather.8.cloned.1.call-done = bf16[1024,1160]{0,1:T(8,128)(2,1)} async-done(((bf16[128,1160]{0,1:T(8,128)(2,1)}), bf16[1024,1160]{0,1:T(8,128)(2,1)}) %all-gather.8.cloned.1.call-update) | async-done | bytes 2375696 | tf_op jit(solution)/shard_map/all_gather | solution.py:74
  58.6 29.5 %all-gather.10.cloned.1.call-done = bf16[1024,2048]{1,0:T(8,128)(2,1)} async-done(((bf16[128,2048]{1,0:T(8,128)(2,1)}), bf16[1024,2048]{1,0:T(8,128)(2,1)}) %all-gather.10.cloned.1.call-update) | async-done | bytes 4194320 | tf_op jit(solution)/shard_map/all_gather | solution.py:74
  88.1 4.5 fusion.139
  92.7 8.2 fusion.74
  101.0 11.9 %fusion.137 = (f32[2,1024]{1,0:T(2,128)S(1)}, f32[2,1024,2048]{2,1,0:T(8,128)}) fusion(f32[2048,1024,2]{0,1,2:T(8,128)} %fusion.74, bf16[2048,2,256]{0,2,1:T(8,128)(2,1)S(1)} %bitcast.105, f32[1024,2,192]{0,2,1:T(8,128)S(1)} %bitcast.98, pred[1024,2048]{1,0:T(8,128)(4,1)S(1)} %copy-done.5), kind=kOutput, calls=%fused_computation.240 | convolution fusion | flops 1090516992 | bytes 37232640 | tf_op jit(solution)/shard_map/qhc,khc->hqk/dot_general | solution.py:98
  112.8 8.1 fusion.2
  121.0 8.3 fusion.46
  134.1 33.9 %reduce-scatter.14.cloned.1.call-done = bf16[128,2048]{1,0:T(8,128)(2,1)} async-done(((bf16[1024,2048]{1,0:T(8,128)(2,1)}), bf16[128,2048]{1,0:T(8,128)(2,1)}) %reduce-scatter.14.cloned.1.call-update) | async-done | bytes 524304 | tf_op jit(solution)/shard_map/reduce_scatter | solution.py:78
  171.5 3.7 slice_bitcast_fusion.2
  175.2 28.9 %all-gather.14.cloned.1.call-done = bf16[1024,2048]{1,0:T(8,128)(2,1)} async-done(((bf16[128,2048]{1,0:T(8,128)(2,1)}), bf16[1024,2048]{1,0:T(8,128)(2,1)}) %all-gather.14.cloned.1.call-update) | async-done | bytes 4194320 | tf_op jit(solution)/shard_map/all_gather | solution.py:74
  204.1 13.4 %fusion.25 = f32[1024,1760]{0,1:T(8,128)} fusion(bf16[1024,2048]{1,0:T(8,128)(2,1)} %all-gather.14.cloned.1.call-done, bf16[1408,2048]{1,0:T(8,128)(2,1)} %bitcast.115, bf16[352,2048]{1,0:T(8,128)(2,1)} %param.26), kind=kOutput, calls=%fused_computation.43 | convolution fusion | flops 7396392960 | bytes 18612224 | tf_op jit(solution)/shard_map/td,fd->tf/dot_general | solution.py:209
  217.5 20.8 %all-gather.12.cloned.1.call-done = bf16[1024,2048]{1,0:T(8,128)(2,1)} async-done(((bf16[128,2048]{1,0:T(8,128)(2,1)}), bf16[1024,2048]{1,0:T(8,128)(2,1)}) %all-gather.12.cloned.1.call-update) | async-done | bytes 4194320 | tf_op jit(solution)/shard_map/all_gather | solution.py:74
  238.3 3.5 fusion.75
  242.0 17.7 %fusion.6 = f32[1024,2816]{0,1:T(8,128)} fusion(bf16[1024,2048]{1,0:T(8,128)(2,1)S(1)} %copy-done.4, bf16[1,2048,2816]{2,1,0:T(8,128)(2,1)} %param.27), kind=kOutput, calls=%fused_computation.13 | convolution fusion | flops 11811160064 | bytes 27262976 | tf_op jit(solution)/shard_map/dot_general | solution.py:203
  260.5 10.8 %multiply_convert_fusion.2 = (bf16[1024,1408]{0,1:T(8,128)(2,1)}, bf16[1024,1408]{0,1:T(8,128)(2,1)}, f32[1024]{0:T(1024)S(1)}, bf16[1024,1408]{0,1:T(8,128)(2,1)}) fusion(f32[1024,2816]{0,1:T(8,128)} %fusion.6, f32[1024,1760]{0,1:T(8,128)} %fusion.25, f32[1024]{0:T(1024)S(1)} %multiply_reduce_fusion.6), kind=kLoop, calls=%fused_computation.35 | loop fusion | flops 28834816 | bytes 25960448 | tf_op jit(solution)/shard_map/convert.16
  271.4 19.0 %fusion.4 = f32[1024,2048]{1,0:T(8,128)} fusion(bf16[1,2048,2816]{2,1,0:T(8,128)(2,1)} %param.27, bf16[1024,1408]{0,1:T(8,128)(2,1)} %get-tuple-element.92, bf16[1024,1408]{0,1:T(8,128)(2,1)} %get-tuple-element.91), kind=kOutput, calls=%fused_computation.11 | convolution fusion | flops 11822694400 | bytes 25690112 | tf_op jit(solution)/shard_map/tf,df->td/dot_general | solution.py:221
  293.7 4.8 multiply_convert_fusion.5
  299.6 3.5 fusion.27
  303.2 3.4 add_convert_fusion
  306.7 34.6 %reduce-scatter.18.cloned.1.call-done = bf16[128,2048]{1,0:T(8,128)(2,1)} async-done(((bf16[1024,2048]{1,0:T(8,128)(2,1)}), bf16[128,2048]{1,0:T(8,128)(2,1)}) %reduce-scatter.18.cloned.1.call-update) | async-done | bytes 524304 | tf_op jit(solution)/shard_map/reduce_scatter | solution.py:78
  346.8 34.1 %all-gather.16.cloned.1.call-done = bf16[1024,2048]{1,0:T(8,128)(2,1)} async-done(((bf16[128,2048]{1,0:T(8,128)(2,1)}), bf16[1024,2048]{1,0:T(8,128)(2,1)}) %all-gather.16.cloned.1.call-update) | async-done | bytes 4194320 | tf_op jit(solution)/shard_map/all_gather | solution.py:74
  380.9 3.8 convolution_convert_fusion.7
  385.4 9.9 fusion.35
  395.3 13.4 %multiply_reduce_fusion = (f32[2,1024]{1,0:T(2,128)S(1)}, f32[2,1024,2048]{2,1,0:T(8,128)}) fusion(f32[2,1024,2048]{2,1,0:T(8,128)} %get-tuple-element.129, f32[2,1024]{1,0:T(2,128)S(1)} %log_add_fusion, bf16[1024,2,128]{0,2,1:T(8,128)(2,1)} %bitcast.109, bf16[2048,2,256]{0,2,1:T(8,128)(2,1)} %bitcast.103), kind=kOutput, calls=%fused_computation.4 | convolution fusion | flops 1086322688 | bytes 35143680 | tf_op jit(solution)/shard_map/qhc,khc->hqk/dot_general | solution.py:242
  408.8 7.9 multiply_convert_fusion
  426.6 4.3 copy.77
  431.0 30.8 %reduce-scatter.22.cloned.1.call-done = bf16[128,1152]{1,0:T(8,128)(2,1)} async-done(((bf16[1024,1152]{1,0:T(8,128)(2,1)}), bf16[128,1152]{1,0:T(8,128)(2,1)}) %reduce-scatter.22.cloned.1.call-update) | async-done | bytes 294928
  466.0 6.0 fusion.51
  476.5 6.8 fusion.50
  487.8 3.6 convolution_convert_fusion.4
  491.4 11.9 %all-gather.18.cloned.1.call-done = bf16[1024,576]{0,1:T(8,128)(2,1)} async-done(((bf16[128,576]{0,1:T(8,128)(2,1)}), bf16[1024,576]{0,1:T(8,128)(2,1)}) %all-gather.18.cloned.1.call-update) | async-done | bytes 1179664 | tf_op jit(solution)/shard_map/all_gather | solution.py:74
  506.2 12.3 %fusion.19 = bf16[2048,1760]{0,1:T(8,128)(2,1)} fusion(bf16[1024,2048]{1,0:T(8,128)(2,1)} %all-gather.14.cloned.1.call-done, bf16[1024,1408]{0,1:T(8,128)(2,1)} %get-tuple-element.94, bf16[1024,352]{0,1:T(8,128)(2,1)} %get-tuple-element.97), kind=kOutput, calls=%fused_computation.29 | convolution fusion | flops 7392788480 | bytes 15007744 | tf_op jit(solution)/shard_map/td,tf->df/dot_general | solution.py:300
  518.4 10.1 copy.81
  528.6 23.8 %convolution_convert_fusion = bf16[2048,3520]{0,1:T(8,128)(2,1)} fusion(bf16[1024,2048]{1,0:T(8,128)(2,1)} %all-gather.12.cloned.1.call-done, bf16[1024,352]{0,1:T(8,128)(2,1)} %copy-done.43, bf16[1024,352]{0,1:T(8,128)(2,1)} %copy-done.42, bf16[1024,1408]{0,1:T(8,128)(2,1)} %get-tuple-element.92, bf16[1024,1408]{0,1:T(8,128)(2,1)} %get-tuple-element.91), kind=kOutput, calls=%fused_computation.8 | convolution fusion | flops 14799994880 | bytes 25821184 | tf_op jit(solution)/shard_map/td,tf->df/dot_general | solution.py:301
  552.3 18.7 %copy.79 = bf16[2048,3520]{1,0:T(8,128)(2,1)} copy(bf16[2048,3520]{0,1:T(8,128)(2,1)} %convolution_convert_fusion) | data formatting | bytes 28835840
  571.4 3.8 fusion.140
  579.6 12.4 %fusion.26 = bf16[1024,2048]{1,0:T(8,128)(2,1)} fusion(bf16[1408,2048]{1,0:T(8,128)(2,1)} %bitcast.116, bf16[352,2048]{1,0:T(8,128)(2,1)} %param.26, bf16[1024,1408]{0,1:T(8,128)(2,1)} %get-tuple-element.94, bf16[1024,352]{0,1:T(8,128)(2,1)S(1)} %copy-done.82), kind=kOutput, calls=%fused_computation.44 | convolution fusion | flops 7405699072 | bytes 15007744 | tf_op jit(solution)/shard_map/dot_general | solution.py:208
  592.1 14.6 %all-reduce.7.cloned.1.call-done = (bf16[2048,384]{1,0:T(8,128)(2,1)}, bf16[256,576]{0,1:T(8,128)(2,1)}, bf16[512,512]{1,0:T(8,128)(2,1)}, bf16[256,2048]{1,0:T(8,128)(2,1)}) async-done(((bf16[2048,384]{1,0:T(8,128)(2,1)}, bf16[256,576]{0,1:T(8,128)(2,1)}, bf16[512,512]{1,0:T(8,128)(2,1)}, bf16[256,2048]{1,0:T(8,128)(2,1)}), (bf16[2048,384]{1,0:T(8,128)(2,1)}, bf16[256,576]{0,1:T(8,128)(2,1)}, ...) | async-done | bytes 3440656 | tf_op jit(solution)/shard_map/psum | solution.py:319
  606.8 3.6 fusion.103
  610.4 81.6 %reduce-scatter.26.cloned.1.call-done = bf16[128,1760]{1,0:T(8,128)(2,1)} async-done(((bf16[2048,1760]{1,0:T(8,128)(2,1)}), bf16[128,1760]{1,0:T(8,128)(2,1)}) %reduce-scatter.26.cloned.1.call-update) | async-done | bytes 450576
  699.5 97.7 %reduce-scatter.24.cloned.1.call-done = bf16[128,3520]{1,0:T(8,128)(2,1)} async-done(((bf16[2048,3520]{1,0:T(8,128)(2,1)}), bf16[128,3520]{1,0:T(8,128)(2,1)}) %reduce-scatter.24.cloned.1.call-update) | async-done | bytes 901136
  806.4 27.8 %reduce-scatter.20.cloned.1.call-done = bf16[128,2048]{1,0:T(8,128)(2,1)} async-done(((bf16[1024,2048]{1,0:T(8,128)(2,1)}), bf16[128,2048]{1,0:T(8,128)(2,1)}) %reduce-scatter.20.cloned.1.call-update) | async-done | bytes 524304 | tf_op jit(solution)/shard_map/reduce_scatter | solution.py:78
  835.6 37.7 %reduce-scatter.16.cloned.1.call-done = bf16[128,2048]{1,0:T(8,128)(2,1)} async-done(((bf16[1024,2048]{1,0:T(8,128)(2,1)}), bf16[128,2048]{1,0:T(8,128)(2,1)}) %reduce-scatter.16.cloned.1.call-update) | async-done | bytes 524304 | tf_op jit(solution)/shard_map/reduce_scatter | solution.py:78
  876.7 69.3 %all-reduce = (f32[2048]{0:T(1024)}, f32[512]{0:T(512)}, f32[2048]{0:T(1024)}) all-reduce(f32[2048]{0:T(1024)S(1)} %get-tuple-element.72, f32[512]{0:T(512)S(1)} %get-tuple-element.74, f32[2048]{0:T(1024)S(1)} %copy-done.56), channel_id=1, replica_groups=mesh['seq'=16,'exp'=8] {'seq','exp'}, use_global_device_ids=true, to_apply=%region_20.21 | all-reduce | flops 4608 | bytes 36864 | tf_op jit(solution)/shard_map/psum | solution.py:327
  946.0 4.5 convert_element_type.203
  950.4 98.9 %all-reduce.5.cloned.1.call-done = f32[2048,8]{0,1:T(8,128)} async-done(((f32[2048,8]{0,1:T(8,128)}), f32[2048,8]{0,1:T(8,128)}) %all-reduce.5.cloned.1.call-update) | async-done | bytes 65552 | tf_op jit(solution)/shard_map/psum | solution.py:327
  (294 shorter events, 90.3 us)
Async XLA Ops:
  7.2 45.5 %all-gather.8.cloned.1.call-start = ((), (), s32[]{:S(2)}) async-start(), calls=%async_computation.7 | async-start | bytes 2672640 | tf_op jit(solution)/shard_map/all_gather | solution.py:74
  7.3 18.8 %copy-start.59 = (f32[32]{0:T(128)}, f32[32]{0:T(128)S(1)}, u32[]{:S(2)}) copy-start(f32[32]{0:T(128)S(1)} %multiply_exponential_fusion) | copy-start | bytes 388
  7.3 18.8 %copy-start.67 = (f32[128]{0:T(128)}, f32[128]{0:T(128)S(1)}, u32[]{:S(2)}) copy-start(f32[128]{0:T(128)S(1)} %fusion.112) | copy-start | bytes 1540
  12.4 6.5 collective-permute-start
  19.7 68.3 %all-gather.10.cloned.1.call-start = ((), (), s32[]{:S(2)}) async-start(), calls=%async_computation.8 | async-start | bytes 4718592 | tf_op jit(solution)/shard_map/all_gather | solution.py:74
  20.5 147.5 %reduce-scatter.14.cloned.1.call-start = ((), (), s32[]{:S(2)}) async-start(), calls=%async_computation.9 | async-start | bytes 4718592 | tf_op jit(solution)/shard_map/reduce_scatter | solution.py:78
  22.6 70.0 %copy-start.31 = (f32[1024,32]{0,1:T(8,128)}, f32[1024,32]{0,1:T(8,128)S(1)}, u32[]{:S(2)}) copy-start(f32[1024,32]{0,1:T(8,128)S(1)} %get-tuple-element.121) | copy-start | bytes 393220
  56.0 36.7 %copy-start.23 = (bf16[2048,64,1]{0,1,2:T(8,128)(2,1)}, bf16[2048,64,1]{0,1,2:T(8,128)(2,1)S(1)}, u32[]{:S(2)}) copy-start(bf16[2048,64,1]{0,1,2:T(8,128)(2,1)S(1)} %fusion.73) | copy-start | bytes 786436
  133.4 34.6 %copy-start.2 = (bf16[128,2048]{1,0:T(8,128)(2,1)S(1)}, bf16[128,2048]{1,0:T(8,128)(2,1)}, u32[]{:S(2)}) copy-start(bf16[128,2048]{1,0:T(8,128)(2,1)} %param.16) | copy-start | bytes 1572868
  133.4 35.9 %copy-start.47 = (f32[2048]{0:T(1024)S(1)}, f32[2048]{0:T(1024)}, u32[]{:S(2)}) copy-start(f32[2048]{0:T(1024)} %param.23) | copy-start | bytes 24580
  133.4 38.1 %copy-start.46 = (f32[2048,8]{0,1:T(8,128)S(1)}, f32[2048,8]{0,1:T(8,128)}, u32[]{:S(2)}) copy-start(f32[2048,8]{0,1:T(8,128)} %param.24) | copy-start | bytes 196612
  133.4 70.7 %all-gather.14.cloned.1.call-start = ((), (), s32[]{:S(2)}) async-start(), calls=%async_computation.12 | async-start | bytes 4718592 | tf_op jit(solution)/shard_map/all_gather | solution.py:74
  134.0 104.3 %all-gather.12.cloned.1.call-start = ((), (), s32[]{:S(2)}) async-start(), calls=%async_computation.10 | async-start | bytes 4718592 | tf_op jit(solution)/shard_map/all_gather | solution.py:74
  169.3 174.0 %copy-start.61 = (f32[128]{0:T(128)}, f32[128]{0:T(128)S(1)}, u32[]{:S(2)}) copy-start(f32[128]{0:T(128)S(1)} %get-tuple-element.127) | copy-start | bytes 1540
  169.3 174.0 %copy-start.72 = (f32[128]{0:T(128)}, f32[128]{0:T(128)S(1)}, u32[]{:S(2)}) copy-start(f32[128]{0:T(128)S(1)} %get-tuple-element.126) | copy-start | bytes 1540
  171.4 169.9 %reduce-scatter.18.cloned.1.call-start = ((), (), s32[]{:S(2)}) async-start(), calls=%async_computation.13 | async-start | bytes 4718592 | tf_op jit(solution)/shard_map/reduce_scatter | solution.py:78
  171.5 131.7 %copy-start.63 = (f32[8]{0:T(128)}, f32[8]{0:T(128)S(1)}, u32[]{:S(2)}) copy-start(f32[8]{0:T(128)S(1)} %compare_convert_fusion) | copy-start | bytes 100
  241.9 61.3 %copy-start.40 = (f32[1024,8]{0,1:T(8,128)}, f32[1024,8]{0,1:T(8,128)S(1)}, u32[]{:S(2)}) copy-start(f32[1024,8]{0,1:T(8,128)S(1)} %get-tuple-element.84) | copy-start | bytes 98308
  241.9 61.3 %copy-start.49 = (f32[1024]{0:T(1024)}, f32[1024]{0:T(1024)S(1)}, u32[]{:S(2)}) copy-start(f32[1024]{0:T(1024)S(1)} %get-tuple-element.83) | copy-start | bytes 12292
  241.9 61.2 %copy-start.52 = (f32[1024]{0:T(1024)}, f32[1024]{0:T(1024)S(1)}, u32[]{:S(2)}) copy-start(f32[1024]{0:T(1024)S(1)} %fusion.84) | copy-start | bytes 12292
  271.3 31.8 %copy-start.54 = (f32[1024]{0:T(1024)}, f32[1024]{0:T(1024)S(1)}, u32[]{:S(2)}) copy-start(f32[1024]{0:T(1024)S(1)} %mul.539) | copy-start | bytes 12292
  306.6 34.7 %copy-start.8 = (bf16[128,2048]{1,0:T(8,128)(2,1)S(1)}, bf16[128,2048]{1,0:T(8,128)(2,1)}, u32[]{:S(2)}) copy-start(bf16[128,2048]{1,0:T(8,128)(2,1)} %reduce-scatter.14.cloned.1.call-done) | copy-start | bytes 1572868
  306.6 74.2 %all-gather.16.cloned.1.call-start = ((), (), s32[]{:S(2)}) async-start(), calls=%async_computation.14 | async-start | bytes 4718592 | tf_op jit(solution)/shard_map/all_gather | solution.py:74
  346.3 115.5 %reduce-scatter.22.cloned.1.call-start = ((), (), s32[]{:S(2)}) async-start(), calls=%async_computation.19 | async-start | bytes 2654208
  385.4 23.3 %slice-start = ((s8[16777216]{0:T(1024)(128)(4,1)}), s8[4194304]{0:T(1024)(128)(4,1)S(1)}, s32[]{:S(2)}) async-start(s8[16777216]{0:T(1024)(128)(4,1)} %bitcast.95), calls=%async_computation.23 | async-start | bytes 8388608
  385.4 23.3 %slice-start.1 = ((s8[16777216]{0:T(1024)(128)(4,1)}), s8[4194304]{0:T(1024)(128)(4,1)S(1)}, s32[]{:S(2)}) async-start(s8[16777216]{0:T(1024)(128)(4,1)} %bitcast.95), calls=%async_computation.24 | async-start | bytes 8388608
  426.6 39.4 %copy-start.24 = (bf16[2048,64,1]{0,1,2:T(8,128)(2,1)S(1)}, bf16[2048,64,1]{0,1,2:T(8,128)(2,1)}, u32[]{:S(2)}) copy-start(bf16[2048,64,1]{0,1,2:T(8,128)(2,1)} %copy-done.23) | copy-start | bytes 786436
  430.9 72.3 %all-gather.18.cloned.1.call-start = ((), (), s32[]{:S(2)}) async-start(), calls=%async_computation.16 | async-start | bytes 1327104 | tf_op jit(solution)/shard_map/all_gather | solution.py:74
  464.3 8.7 collective-permute-start.1
  475.4 131.3 %all-reduce.7.cloned.1.call-start = ((), (), s32[]{:S(2)}) async-start(), calls=%async_computation.22 | async-start | bytes 6881280 | tf_op jit(solution)/shard_map/psum | solution.py:319
  505.9 186.1 %reduce-scatter.26.cloned.1.call-start = ((), (), s32[]{:S(2)}) async-start(), calls=%async_computation.21 | async-start | bytes 7798784
  528.5 268.7 %reduce-scatter.24.cloned.1.call-start = ((), (), s32[]{:S(2)}) async-start(), calls=%async_computation.20 | async-start | bytes 15597568
  571.1 263.1 %reduce-scatter.20.cloned.1.call-start = ((), (), s32[]{:S(2)}) async-start(), calls=%async_computation.15 | async-start | bytes 4718592 | tf_op jit(solution)/shard_map/reduce_scatter | solution.py:78
  578.5 294.8 %reduce-scatter.16.cloned.1.call-start = ((), (), s32[]{:S(2)}) async-start(), calls=%async_computation.11 | async-start | bytes 4718592 | tf_op jit(solution)/shard_map/reduce_scatter | solution.py:78
  592.0 14.8 %copy-start.55 = (f32[1024]{0:T(1024)S(1)}, f32[1024]{0:T(1024)}, u32[]{:S(2)}) copy-start(f32[1024]{0:T(1024)} %copy-done.54) | copy-start | bytes 12292
  592.1 353.9 %all-gather.20.cloned.1.call-start = ((), (), s32[]{:S(2)}) async-start(), calls=%async_computation.17 | async-start | bytes 2654208 | tf_op jit(solution)/shard_map/all_gather | solution.py:74
  606.7 88.2 %copy-start.45 = (bf16[512,512]{1,0:T(8,128)(2,1)S(1)}, bf16[512,512]{1,0:T(8,128)(2,1)}, u32[]{:S(2)}) copy-start(bf16[512,512]{1,0:T(8,128)(2,1)} %get-tuple-element.81) | copy-start | bytes 1572868
  606.7 442.6 %all-reduce.5.cloned.1.call-start = ((), (), s32[]{:S(2)}) async-start(), calls=%async_computation.18 | async-start | bytes 131072 | tf_op jit(solution)/shard_map/psum | solution.py:327
  800.8 33.4 %copy-start.3 = (bf16[128,2048]{1,0:T(8,128)(2,1)S(1)}, bf16[128,2048]{1,0:T(8,128)(2,1)}, u32[]{:S(2)}) copy-start(bf16[128,2048]{1,0:T(8,128)(2,1)} %param.16) | copy-start | bytes 1572868
  800.8 33.4 %copy-start.51 = (f32[2048]{0:T(1024)S(1)}, f32[2048]{0:T(1024)}, u32[]{:S(2)}) copy-start(f32[2048]{0:T(1024)} %param.17) | copy-start | bytes 24580
  800.8 33.4 %copy-start.66 = (f32[128]{0:T(128)S(1)}, f32[128]{0:T(128)}, u32[]{:S(2)}) copy-start(f32[128]{0:T(128)} %copy-done.65) | copy-start | bytes 1540
  800.8 72.5 %copy-start.9 = (bf16[128,2048]{1,0:T(8,128)(2,1)S(1)}, bf16[128,2048]{1,0:T(8,128)(2,1)}, u32[]{:S(2)}) copy-start(bf16[128,2048]{1,0:T(8,128)(2,1)} %reduce-scatter.14.cloned.1.call-done) | copy-start | bytes 1572868
  800.8 72.5 %copy-start.48 = (f32[2048]{0:T(1024)S(1)}, f32[2048]{0:T(1024)}, u32[]{:S(2)}) copy-start(f32[2048]{0:T(1024)} %param.23) | copy-start | bytes 24580
  800.8 72.5 %copy-start.62 = (f32[128]{0:T(128)S(1)}, f32[128]{0:T(128)}, u32[]{:S(2)}) copy-start(f32[128]{0:T(128)} %copy-done.61) | copy-start | bytes 1540
  800.8 72.5 %copy-start.73 = (f32[128]{0:T(128)S(1)}, f32[128]{0:T(128)}, u32[]{:S(2)}) copy-start(f32[128]{0:T(128)} %copy-done.72) | copy-start | bytes 1540
  800.8 72.5 %copy-start.75 = (f32[128]{0:T(128)S(1)}, f32[128]{0:T(128)}, u32[]{:S(2)}) copy-start(f32[128]{0:T(128)} %copy-done.74) | copy-start | bytes 1540
  800.8 72.5 %copy-start.76 = (f32[128]{0:T(128)S(1)}, f32[128]{0:T(128)}, u32[]{:S(2)}) copy-start(f32[128]{0:T(128)} %get-tuple-element.122) | copy-start | bytes 1540
  803.4 73.2 %copy-start.56 = (f32[2048]{0:T(1024)S(1)}, f32[2048]{0:T(1024)}, u32[]{:S(2)}) copy-start(f32[2048]{0:T(1024)} %get-tuple-element.70) | copy-start | bytes 24580
  (59 other events, 345.0 us)
Sparse Core Ops, SparseCore 0:
  19.8 32.7 all-gather.7
  55.0 33.0 all-gather.9
  133.5 34.4 reduce-scatter.13
  169.6 34.4 all-gather.13
  206.2 32.0 all-gather.11
  306.8 34.4 reduce-scatter.17
  346.4 34.4 all-gather.15
  431.1 30.7 reduce-scatter.21
  475.5 27.7 all-gather.17
  508.2 98.4 all-reduce.6
  610.6 81.3 reduce-scatter.25
  695.3 101.8 reduce-scatter.23
  800.2 33.9 reduce-scatter.19
  836.4 36.8 reduce-scatter.15
  874.8 30.8 all-gather.19
  910.9 138.3 all-reduce.4

commit v2 on v1

--- a/solution.py
+++ b/solution.py
@@ -1,8 +1,11 @@
+import functools
 import math
 
 import jax
 import jax.numpy as jnp
 from jax import lax
+from jax.experimental import pallas as pl
+from jax.experimental.pallas import tpu as pltpu
 from jax.sharding import PartitionSpec as P
 
 NOPE = 128
@@ -14,8 +17,321 @@
 EXPERTS = 8
 
 
-highest = lax.Precision.HIGHEST
+VM = pltpu.VMEM
+f32 = jnp.float32
+bf16 = jnp.bfloat16
 EPSILON = 1e-06
+
+
+def _send(src, dst, send, recv, peer):
+    copy = pltpu.make_async_remote_copy(
+        src_ref=src, dst_ref=dst, send_sem=send, recv_sem=recv,
+        device_id=peer, device_id_type=pl.DeviceIdType.MESH)
+    copy.start()
+    return copy
+
+
+def greet(peers):
+    barrier = pltpu.get_barrier_semaphore()
+    for peer in peers:
+        pl.semaphore_signal(barrier, inc=1, device_id=peer, device_id_type=pl.DeviceIdType.MESH)
+    pl.semaphore_wait(barrier, len(peers))
+
+
+def small_sum_kernel(src, out, slots, send, recv):
+    me, spot = lax.axis_index("exp"), lax.axis_index("seq")
+    chip, core = me // 2, me % 2
+    row, col = spot // 4, spot % 4
+    axes = [
+        (core, 2, lambda i: {"exp": chip * 2 + i}),
+        (chip, 4, lambda i: {"exp": i * 2 + core}),
+        (col, 4, lambda i: {"seq": row * 4 + i}),
+        (row, 4, lambda i: {"seq": i * 4 + col}),
+    ]
+    greet([name(lax.rem(place + d, n)) for place, n, name in axes for d in range(1, n)])
+    out[...] = src[...]
+    count = 0
+    sends = []
+    for stage, (place, n, name) in enumerate(axes):
+        slots[stage, place] = out[...]
+        here = [
+            _send(slots.at[stage, place], slots.at[stage, place], send.at[count + d - 1], recv.at[count + d - 1], name(lax.rem(place + d, n)))
+            for d in range(1, n)
+        ]
+        count += n - 1
+        for c in here:
+            c.wait_recv()
+        total = slots[stage, 0]
+        for i in range(1, n):
+            total = total + slots[stage, i]
+        out[...] = total
+        sends += here
+    for c in sends:
+        c.wait_send()
+
+
+def small_sum(vec, ident, name):
+    return pl.pallas_call(
+        small_sum_kernel,
+        out_shape=jax.ShapeDtypeStruct(vec.shape, f32),
+        in_specs=[pl.BlockSpec(memory_space=VM)],
+        out_specs=pl.BlockSpec(memory_space=VM),
+        scratch_shapes=[pltpu.VMEM((4, 4) + vec.shape, f32), pltpu.SemaphoreType.DMA((10,)), pltpu.SemaphoreType.DMA((10,))],
+        compiler_params=pltpu.CompilerParams(collective_id=ident, has_side_effects=True, vmem_limit_bytes=48 << 20),
+        name=name,
+    )(vec)
+
+
+class Sems:
+    def __init__(self, send, recv):
+        self.send, self.recv, self.used, self.sent = send, recv, 0, []
+
+    def start(self, src, dst, peer):
+        c = _send(src, dst, self.send.at[self.used], self.recv.at[self.used], peer)
+        self.used += 1
+        self.sent.append(c)
+        return c
+
+    def finish(self):
+        for c in self.sent:
+            c.wait_send()
+
+
+def ring_sum(sems, place, peer, block, hop, last):
+    right, left = peer(lax.rem(place + 1, 4)), peer(lax.rem(place + 3, 4))
+    to = [lax.rem(place + d, 4) for d in range(4)]
+
+    def add(ref, other):
+        ref[...] = (ref[...].astype(f32) + other[...].astype(f32)).astype(ref.dtype)
+
+    far_a = sems.start(block(to[2], 0), hop.at[0], right)
+    far_b = sems.start(block(to[2], 1), hop.at[1], left)
+    dir_b = sems.start(block(to[1], 1), last.at[0], right)
+    dir_a = sems.start(block(to[3], 0), last.at[1], left)
+    yield
+    far_a.wait_recv()
+    add(block(to[1], 0), hop.at[0])
+    acc_a = sems.start(block(to[1], 0), last.at[2], right)
+    yield
+    far_b.wait_recv()
+    add(block(to[3], 1), hop.at[1])
+    acc_b = sems.start(block(to[3], 1), last.at[3], left)
+    yield
+    dir_b.wait_recv()
+    dir_a.wait_recv()
+    add(block(to[0], 1), last.at[0])
+    add(block(to[0], 0), last.at[1])
+    yield
+    acc_a.wait_recv()
+    add(block(to[0], 0), last.at[2])
+    yield
+    acc_b.wait_recv()
+    add(block(to[0], 1), last.at[3])
+
+
+def ring_gather(sems, place, peer, block):
+    right, left = peer(lax.rem(place + 1, 4)), peer(lax.rem(place + 3, 4))
+    to = [lax.rem(place + d, 4) for d in range(4)]
+    ra = sems.start(block(to[0], 0), block(to[0], 0), right)
+    lb = sems.start(block(to[0], 1), block(to[0], 1), left)
+    rb = sems.start(block(to[0], 1), block(to[0], 1), right)
+    la = sems.start(block(to[0], 0), block(to[0], 0), left)
+    yield
+    ra.wait_recv()
+    fa = sems.start(block(to[3], 0), block(to[3], 0), right)
+    yield
+    lb.wait_recv()
+    fb = sems.start(block(to[1], 1), block(to[1], 1), left)
+    yield
+    rb.wait_recv()
+    la.wait_recv()
+    yield
+    fa.wait_recv()
+    yield
+    fb.wait_recv()
+
+
+def together(*streams):
+    streams = list(streams)
+    while streams:
+        for s in list(streams):
+            try:
+                next(s)
+            except StopIteration:
+                streams.remove(s)
+
+
+def seq_sum_kernel(cols, src, out, work, hop1, last1, hop2, last2, send, recv):
+    spot = lax.axis_index("seq")
+    z, y = spot // 4, spot % 4
+    peers = [lambda i: {"seq": z * 4 + i}, lambda i: {"seq": i * 4 + y}]
+    places = [y, z]
+    greet([peers[0](lax.rem(y + 1, 4)), peers[0](lax.rem(y + 3, 4)), peers[1](lax.rem(z + 1, 4)), peers[1](lax.rem(z + 3, 4))])
+    work[...] = src[...]
+    sems = Sems(send, recv)
+    half = cols // 2
+
+    def stream(part):
+        first, second = (0, 1) if part == 0 else (1, 0)
+        def wide(ref):
+            return lambda i, h: ref.at[part, pl.ds(i * 4 + 2 * h, 2)]
+
+        def narrow(ref):
+            return lambda i, h: ref.at[part, places[first] * 4 + i, :, pl.ds(h * half, half)]
+
+        yield from ring_sum(sems, places[first], peers[first], wide(work), hop1.at[part], last1.at[part])
+        yield from ring_sum(sems, places[second], peers[second], narrow(work), hop2.at[part], last2.at[part])
+        own = places[first] * 4 + places[second]
+        out[part, own] = work[part, own]
+        yield from ring_gather(sems, places[second], peers[second], narrow(out))
+        yield from ring_gather(sems, places[first], peers[first], wide(out))
+
+    together(stream(0), stream(1))
+    sems.finish()
+
+
+def seq_sum(parts, ident, name):
+    _, _, rows, cols = parts.shape
+    bf16 = jnp.bfloat16
+    return pl.pallas_call(
+        functools.partial(seq_sum_kernel, cols),
+        out_shape=jax.ShapeDtypeStruct(parts.shape, bf16),
+        in_specs=[pl.BlockSpec(memory_space=VM)],
+        out_specs=pl.BlockSpec(memory_space=VM),
+        scratch_shapes=[
+            pltpu.VMEM(parts.shape, bf16),
+            pltpu.VMEM((2, 2, 2, rows, cols), bf16), pltpu.VMEM((2, 4, 2, rows, cols), bf16),
+            pltpu.VMEM((2, 2, rows, cols // 2), bf16), pltpu.VMEM((2, 4, rows, cols // 2), bf16),
+            pltpu.SemaphoreType.DMA((48,)), pltpu.SemaphoreType.DMA((48,))],
+        compiler_params=pltpu.CompilerParams(collective_id=ident, has_side_effects=True, vmem_limit_bytes=56 << 20),
+        name=name,
+    )(parts)
+
+
+def x_places():
+    me = lax.axis_index("exp")
+    chip, core = me // 2, me % 2
+    right = lax.rem(chip + 1, 4) * 2 + core
+    left = lax.rem(chip + 3, 4) * 2 + core
+    far = lax.rem(chip + 2, 4) * 2 + core
+    return me, chip, core, right, left, far
+
+
+def gather_kernel(rows, src, out, send, recv, local):
+    me, chip, core, right, left, far = x_places()
+    sibling = chip * 2 + 1 - core
+    greet([{"exp": right}, {"exp": left}, {"exp": sibling}])
+    half = rows // 2
+
+    def at(owner, part):
+        return out.at[pl.ds(pl.multiple_of(owner * rows + part * half, half), half)]
+
+    def both(owner):
+        return out.at[pl.ds(pl.multiple_of(owner * rows, rows), rows)]
+
+    A, B = 0, 1
+    def own(part):
+        return src.at[pl.ds(part * half, half)]
+    copies = []
+    ra = _send(own(A), at(me, A), send.at[0], recv.at[0], {"exp": right})
+    lb = _send(own(B), at(me, B), send.at[1], recv.at[1], {"exp": left})
+    rb = _send(own(B), at(me, B), send.at[2], recv.at[2], {"exp": right})
+    la = _send(own(A), at(me, A), send.at[3], recv.at[3], {"exp": left})
+    sib = _send(src, both(me), send.at[4], recv.at[4], {"exp": sibling})
+    mine = pltpu.make_async_copy(src, both(me), local)
+    mine.start()
+    ra.wait_recv()
+    far_a = _send(at(left, A), at(left, A), send.at[5], recv.at[5], {"exp": right})
+    s_la = _send(at(left, A), at(left, A), send.at[6], recv.at[6], {"exp": sibling})
+    lb.wait_recv()
+    far_b = _send(at(right, B), at(right, B), send.at[7], recv.at[7], {"exp": left})
+    s_rb = _send(at(right, B), at(right, B), send.at[8], recv.at[8], {"exp": sibling})
+    rb.wait_recv()
+    s_lb = _send(at(left, B), at(left, B), send.at[9], recv.at[9], {"exp": sibling})
+    la.wait_recv()
+    s_ra = _send(at(right, A), at(right, A), send.at[10], recv.at[10], {"exp": sibling})
+    far_a.wait_recv()
+    s_fa = _send(at(far, A), at(far, A), send.at[11], recv.at[11], {"exp": sibling})
+    far_b.wait_recv()
+    s_fb = _send(at(far, B), at(far, B), send.at[12], recv.at[12], {"exp": sibling})
+    mine.wait()
+    for c in (sib, s_la, s_rb, s_lb, s_ra, s_fa, s_fb):
+        c.wait_recv()
+    for c in (ra, lb, rb, la, sib, far_a, s_la, far_b, s_rb, s_lb, s_ra, s_fa, s_fb):
+        c.wait_send()
+
+
+def gather_x(block, ident, name):
+    rows, cols = block.shape
+    return pl.pallas_call(
+        functools.partial(gather_kernel, rows),
+        out_shape=jax.ShapeDtypeStruct((rows * 8, cols), block.dtype),
+        in_specs=[pl.BlockSpec(memory_space=VM)],
+        out_specs=pl.BlockSpec(memory_space=VM),
+        scratch_shapes=[pltpu.SemaphoreType.DMA((13,)), pltpu.SemaphoreType.DMA((13,)), pltpu.SemaphoreType.DMA],
+        compiler_params=pltpu.CompilerParams(collective_id=ident, has_side_effects=True, vmem_limit_bytes=48 << 20),
+        name=name,
+    )(block)
+
+
+def scatter_kernel(rows, src, out, pair, hop, last, send, recv):
+    me, chip, core, right, left, far = x_places()
+    sibling = chip * 2 + 1 - core
+    greet([{"exp": right}, {"exp": left}, {"exp": sibling}])
+    half = rows // 2
+    f32 = jnp.float32
+    order = [2, 1, 3, 0]
+    sib = []
+    for i, dist in enumerate(order):
+        owner = lax.rem(chip + dist, 4) * 2 + 1 - core
+        sib.append(_send(src.at[pl.ds(pl.multiple_of(owner * rows, rows), rows)], pair.at[dist], send.at[i], recv.at[i], {"exp": sibling}))
+
+    def fold(i, dist):
+        sib[i].wait_recv()
+        owner = lax.rem(chip + dist, 4) * 2 + core
+        mine = src[pl.ds(pl.multiple_of(owner * rows, rows), rows)]
+        pair[dist] = (pair[dist].astype(f32) + mine.astype(f32)).astype(pair.dtype)
+
+    A = pl.ds(0, half)
+    B = pl.ds(half, half)
+    fold(0, 2)
+    far_a = _send(pair.at[2, A], hop.at[0], send.at[4], recv.at[4], {"exp": right})
+    far_b = _send(pair.at[2, B], hop.at[1], send.at[5], recv.at[5], {"exp": left})
+    fold(1, 1)
+    dir_b = _send(pair.at[1, B], last.at[0], send.at[6], recv.at[6], {"exp": right})
+    fold(2, 3)
+    dir_a = _send(pair.at[3, A], last.at[1], send.at[7], recv.at[7], {"exp": left})
+    far_a.wait_recv()
+    pair[1, A] = (pair[1, A].astype(f32) + hop[0].astype(f32)).astype(pair.dtype)
+    acc_a = _send(pair.at[1, A], last.at[2], send.at[8], recv.at[8], {"exp": right})
+    far_b.wait_recv()
+    pair[3, B] = (pair[3, B].astype(f32) + hop[1].astype(f32)).astype(pair.dtype)
+    acc_b = _send(pair.at[3, B], last.at[3], send.at[9], recv.at[9], {"exp": left})
+    sib[3].wait_recv()
+    mine = src[pl.ds(pl.multiple_of(me * rows, rows), rows)].astype(f32) + pair[0].astype(f32)
+    dir_b.wait_recv()
+    dir_a.wait_recv()
+    acc_a.wait_recv()
+    acc_b.wait_recv()
+    out[A] = mine[:half] + last[1].astype(f32) + last[2].astype(f32)
+    out[B] = mine[half:] + last[0].astype(f32) + last[3].astype(f32)
+    for c in sib + [far_a, far_b, dir_b, dir_a, acc_a, acc_b]:
+        c.wait_send()
+
+
+def scatter_x(part, ident, name):
+    rows, cols = part.shape[0] // 8, part.shape[1]
+    bf16 = jnp.bfloat16
+    return pl.pallas_call(
+        functools.partial(scatter_kernel, rows),
+        out_shape=jax.ShapeDtypeStruct((rows, cols), jnp.float32),
+        in_specs=[pl.BlockSpec(memory_space=VM)],
+        out_specs=pl.BlockSpec(memory_space=VM),
+        scratch_shapes=[pltpu.VMEM((4, rows, cols), bf16), pltpu.VMEM((2, rows // 2, cols), bf16), pltpu.VMEM((4, rows // 2, cols), bf16),
+                        pltpu.SemaphoreType.DMA((10,)), pltpu.SemaphoreType.DMA((10,))],
+        compiler_params=pltpu.CompilerParams(collective_id=ident, has_side_effects=True, vmem_limit_bytes=48 << 20),
+        name=name,
+    )(part)
 
 
 def shifted_pair(block, distance):
@@ -68,16 +384,6 @@
         ],
         axis=-1,
     )
-
-
-def gather_rows(tensor):
-    return lax.all_gather(tensor, "exp", axis=0, tiled=True)
-
-
-def sum_rows(tensor):
-    return lax.psum_scatter(
-        tensor.astype(jnp.bfloat16), "exp", scatter_dimension=0, tiled=True
-    ).astype(jnp.float32)
 
 
 def add_own(full_term, own_term, row_offset):
@@ -123,8 +429,6 @@
     expert_routes,
     out_grad,
 ):
-    f32 = jnp.float32
-    bf16 = jnp.bfloat16
     exp_count = lax.axis_size("exp")
     own_rows = layer_input.shape[0]
     model_width = layer_input.shape[1]
@@ -144,7 +448,7 @@
     key_seg = jnp.concatenate([prev_seg, query_seg], axis=0)
     input_f = layer_input.astype(f32)
     normed_low = rms_scale(input_f, attn_gain).astype(bf16)
-    normed_all = gather_rows(normed_low)
+    normed_all = gather_x(normed_low, 0, "gather_0")
     query_raw = jnp.dot(normed_all, query_proj, preferred_element_type=f32).reshape(
         block_rows, head_count, NOPE + ROPE
     )
@@ -159,7 +463,7 @@
     ).astype(bf16)
     key_latent = jnp.concatenate([latent_normed, rope_key], axis=-1)
     prev_latent = shifted_pair(key_latent, 1)
-    gathered = gather_rows(jnp.concatenate([key_latent, prev_latent, hot], axis=-1))
+    gathered = gather_x(jnp.concatenate([key_latent, prev_latent, hot], axis=-1), 1, "gather_1")
     width = LAT + ROPE
     keys_all = jnp.concatenate([gathered[:, width : 2 * width], gathered[:, :width]], axis=0)
     hot_all = gathered[:, 2 * width :].astype(f32)
@@ -176,12 +480,12 @@
         "hqk,khc->qhc", soft_weights.astype(bf16), packed[..., NOPE:], preferred_element_type=f32
     )
     heads_low = head_rows.astype(bf16).reshape(block_rows, head_count * VDIM)
-    attn_rows = sum_rows(jnp.dot(heads_low, output_proj, preferred_element_type=f32))
+    attn_rows = scatter_x((jnp.dot(heads_low, output_proj, preferred_element_type=f32)).astype(bf16), 10, "scatter_0")
     residual = input_f + attn_rows
     mid_low = rms_scale(residual, ffn_gain).astype(bf16)
-    mid_all = gather_rows(mid_low)
+    mid_all = gather_x(mid_low, 2, "gather_2")
     grad_f = out_grad.astype(f32)
-    grad_all = gather_rows(out_grad)
+    grad_all = gather_x(out_grad, 3, "gather_3")
     router_high = lax.reduce_precision(router_proj, 8, 7)
     router_rest = router_proj - router_high
     router_mid = lax.reduce_precision(router_rest, 8, 7)
@@ -216,17 +520,35 @@
     shared_dpre = jnp.concatenate([shared_dgate, shared_dup], axis=1).astype(bf16)
     expert_dpre = jnp.concatenate([expert_dgate, expert_dup], axis=1).astype(bf16)
     shared_both = jnp.concatenate([shared_gate_up[:, 0], shared_gate_up[:, 1]], axis=1)
+    down_term = jnp.einsum("td,tf->df", grad_all, act_all, preferred_element_type=f32)
+    gate_term = jnp.einsum(
+        "td,tf->df",
+        mid_all,
+        jnp.concatenate([expert_dpre, shared_dpre], axis=1),
+        preferred_element_type=f32,
+    )
+    weight_terms = jnp.concatenate([gate_term.astype(bf16), down_term.astype(bf16)], axis=1)
+    weight_terms, shared_dpre, expert_dpre = lax.optimization_barrier(
+        (weight_terms, shared_dpre, expert_dpre)
+    )
+    weight_sum = lax.psum_scatter(weight_terms, "seq", scatter_dimension=0, tiled=True)
+    gate_sum = weight_sum[:, : 2 * F + 2 * shared_width].astype(f32)
+    down_sum = weight_sum[:, 2 * F + 2 * shared_width :].astype(f32)
+    shared_down_sum = down_sum[:, :shared_width].T
+    expert_down_sum = down_sum[:, shared_width:].T[None]
+    expert_gate_sum = gate_sum[None, :, : 2 * F]
+    shared_gate_sum = gate_sum[:, 2 * F :].reshape(own_rows, 2, shared_width)
     mid_grad_all = (
         jnp.einsum("tf,df->td", shared_dpre, shared_both, preferred_element_type=f32)
         + jnp.einsum("tf,df->td", expert_dpre, expert_gate_up[0], preferred_element_type=f32)
         + jnp.einsum("te,de->td", logit_term, router_proj, preferred_element_type=f32)
     )
-    mid_grad = sum_rows(mid_grad_all)
+    mid_grad = scatter_x((mid_grad_all).astype(bf16), 11, "scatter_1")
     router_term = jnp.einsum("td,te->de", mid_all, logit_term.astype(bf16), preferred_element_type=f32)
-    layer_output = (residual + sum_rows(moe_part)).astype(bf16)
+    layer_output = (residual + scatter_x((moe_part).astype(bf16), 12, "scatter_2")).astype(bf16)
     mid_input_grad, ffn_gain_term = rms_back(residual, ffn_gain, mid_grad)
     residual_grad = grad_f + mid_input_grad
-    attn_grad_all = gather_rows(residual_grad.astype(bf16))
+    attn_grad_all = gather_x(residual_grad.astype(bf16), 4, "gather_4")
     output_term = jnp.einsum("tc,td->cd", heads_low, attn_grad_all, preferred_element_type=f32)
     heads_grad = (
         jnp.einsum("td,cd->tc", attn_grad_all, output_proj, preferred_element_type=f32)
@@ -275,7 +597,7 @@
     kv_term = jnp.einsum("tl,tc->lc", latent_back, packed_grad, preferred_element_type=f32)
     latent_grad_all = jnp.einsum("tc,lc->tl", packed_grad, kv_proj, preferred_element_type=f32)
     key_grad = jnp.concatenate([latent_grad_all, rope_key_grad], axis=-1)
-    both_grad = sum_rows(jnp.concatenate([key_grad[block_rows:], key_grad[:block_rows]], axis=1))
+    both_grad = scatter_x((jnp.concatenate([key_grad[block_rows:], key_grad[:block_rows]], axis=1)).astype(bf16), 13, "scatter_3")
     own_key_grad = both_grad[:, :width] + shifted_pair(
         both_grad[:, width:].astype(bf16), -1
     ).astype(f32)
@@ -287,46 +609,83 @@
     latent_raw_grad = jnp.concatenate(
         [latent_pre_grad, rotate(rope_own, own_pos % key_rows, -1.0)], axis=-1
     ).astype(bf16)
-    latent_raw_all = gather_rows(latent_raw_grad)
+    latent_raw_all = gather_x(latent_raw_grad, 5, "gather_5")
     slice_width = model_width // exp_count
     normed_slice = lax.dynamic_slice_in_dim(
         normed_all, lax.axis_index("exp") * slice_width, slice_width, 1
     )
     latent_term = jnp.einsum("td,tc->dc", normed_slice, latent_raw_all, preferred_element_type=f32)
     in_grad_own = jnp.einsum("tc,dc->td", latent_raw_grad, latent_proj, preferred_element_type=f32)
-    normed_grad = sum_rows(add_own(in_grad_all, in_grad_own, row_offset))
+    normed_grad = scatter_x((add_own(in_grad_all, in_grad_own, row_offset)).astype(bf16), 14, "scatter_4")
     input_part, attn_gain_term = rms_back(input_f, attn_gain, normed_grad)
     input_grad = (residual_grad + input_part).astype(bf16)
-    down_term = jnp.einsum("td,tf->df", grad_all, act_all, preferred_element_type=f32)
-    gate_term = jnp.einsum(
-        "td,tf->df",
-        mid_all,
-        jnp.concatenate([expert_dpre, shared_dpre], axis=1),
-        preferred_element_type=f32,
-    )
-    down_sum = lax.psum_scatter(
-        down_term.astype(bf16), "seq", scatter_dimension=0, tiled=True
-    ).astype(f32)
-    gate_sum = lax.psum_scatter(
-        gate_term.astype(bf16), "seq", scatter_dimension=0, tiled=True
-    ).astype(f32)
-    shared_down_sum = down_sum[:, :shared_width].T
-    expert_down_sum = down_sum[:, shared_width:].T[None]
-    expert_gate_sum = gate_sum[None, :, : 2 * F]
-    shared_gate_sum = gate_sum[:, 2 * F :].reshape(own_rows, 2, shared_width)
-    query_sum, kv_sum, output_sum, latent_sum = (
-        term.astype(f32)
-        for term in lax.psum(
-            tuple(
-                term.astype(bf16) for term in (query_term, kv_term, output_term, latent_term)
+    spots = lax.axis_size("seq")
+    wide = LAT
+    query_rows = query_term.shape[0] // 2
+    query_flat = jnp.concatenate(
+        [
+            jnp.concatenate([query_term[:query_rows, :256], query_term[query_rows:, :256]], axis=1),
+            query_term[:, 256:].reshape(4, query_rows // 2, 128).transpose(1, 0, 2).reshape(-1, wide),
+        ],
+        axis=0,
+    ).reshape(spots, -1, wide)
+    output_flat = jnp.stack(
+        [output_term[:, i * wide : (i + 1) * wide].reshape(spots, -1, wide) for i in range(4)], axis=1
+    ).reshape(spots, -1, wide)
+    kv_flat = kv_term.reshape(spots, -1, wide)
+    latent_turned = latent_term.T
+    latent_rows = latent_turned.shape[0] // 2
+    latent_flat = jnp.concatenate([latent_turned[:latent_rows], latent_turned[latent_rows:]], axis=1)
+    latent_one = latent_flat[: spots * 16].reshape(spots, 16, wide)
+    latent_two = latent_flat[spots * 16 :].reshape(spots, -1, wide)
+    pad = 16 - latent_two.shape[1]
+    flat = jnp.stack(
+        [
+            jnp.concatenate([query_flat, latent_one], axis=1),
+            jnp.pad(
+                jnp.concatenate([kv_flat, output_flat, latent_two], axis=1), ((0, 0), (0, pad), (0, 0))
             ),
-            "seq",
-        )
-    )
-    latent_sum = gather_rows(latent_sum.astype(bf16)).astype(f32)
-    attn_gain_sum, latent_gain_sum, ffn_gain_sum, router_sum = lax.psum(
-        (attn_gain_term, latent_gain_term, ffn_gain_term, router_term), ("seq", "exp")
-    )
+        ]
+    ).astype(bf16)
+    total = seq_sum(flat, 20, "seq_sum").astype(f32)
+    query_count, kv_count = query_flat.shape[1], kv_flat.shape[1]
+    output_count = output_flat.shape[1]
+    query_back = total[0, :, :query_count].reshape(-1, wide)
+    query_sum = jnp.concatenate(
+        [
+            jnp.concatenate([query_back[:query_rows, :256], query_back[:query_rows, 256:]], axis=0),
+            query_back[query_rows:].reshape(-1, 4, 128).transpose(1, 0, 2).reshape(-1, 128),
+        ],
+        axis=1,
+    )
+    kv_sum = total[1, :, :kv_count].reshape(kv_term.shape)
+    output_back = total[1, :, kv_count : kv_count + output_count].reshape(spots, 4, -1, wide)
+    output_sum = jnp.concatenate([output_back[:, i].reshape(-1, wide) for i in range(4)], axis=1)
+    latent_back = jnp.concatenate(
+        [
+            total[0, :, query_count:].reshape(-1, wide),
+            total[1, :, kv_count + output_count : -pad].reshape(-1, wide),
+        ],
+        axis=0,
+    )
+    half_wide = wide // 2
+    latent_sum = jnp.concatenate([latent_back[:, :half_wide], latent_back[:, half_wide:]], axis=0).T
+    latent_sum = gather_x(latent_sum.astype(bf16), 6, "gather_6").astype(f32)
+    small = jnp.concatenate(
+        [
+            router_term.reshape(-1),
+            attn_gain_term,
+            ffn_gain_term,
+            latent_gain_term,
+            jnp.zeros((512,), f32),
+        ]
+    ).reshape(-1, 128)
+    small = small_sum(small, 21, "small_sum").reshape(-1)
+    router_sum = small[: model_width * EXPERTS].reshape(model_width, EXPERTS)
+    gains = small[model_width * EXPERTS :]
+    attn_gain_sum = gains[:model_width]
+    ffn_gain_sum = gains[model_width : 2 * model_width]
+    latent_gain_sum = gains[2 * model_width : 2 * model_width + LAT]
     return (
         layer_output,
         input_grad,

time: 1070 us -> 754 us (0.70)
  waiting for transfers between devices: 613 us -> 0.02 us
  Pallas kernels: 0 us -> 320 us
  blocking collectives: 69.3 us -> 0 us
  other arithmetic: 68.5 us -> 94.7 us
  local copies, waits for them, and re-layouts: 64.7 us -> 90.6 us
    pallas_call x0 -> x14, Pallas kernels: none -> 320 us  [the longest x7 140 us: gather_x(): pl.pallas_call(functools.partial(gather_kernel, rows), out_shape=jax.Shap...]
    unnamed x19 -> x2, waiting for transfers between devices: 212 us -> 0.02 us
    all_gather x7 -> x0, waiting for transfers between devices: 152 us -> none  [gather_rows(): return lax.all_gather(tensor, 'exp', axis=0, tiled=True)]
    reduce_scatter x4 -> x0, waiting for transfers between devices: 134 us -> none  [sum_rows(): lax.psum_scatter(tensor.astype(jnp.bfloat16), 'exp', scatter_dimension=0,...]
    psum x2 -> x0, waiting for transfers between devices: 113 us -> none  [the longest x1 98.9 us: local(): lax.psum((attn_gain_term, latent_gain_term, ffn_gain_term, router_term),...]
    psum x1 -> x0, blocking collectives: 69.3 us -> none  [local(): lax.psum((attn_gain_term, latent_gain_term, ffn_gain_term, router_term),...]
    concatenate x2 -> x6, other arithmetic: 0.19 us -> 32.8 us  [the longest x1 23.9 us: local(): jnp.concatenate([gate_term.astype(bf16), down_term.astype(bf16)], axis=1)]
    slice x1 -> x19, local copies, waits for them, and re-layouts: 1.7 us -> 15.6 us  [the longest x1 2.83 us: local(): total[1, :, kv_count:kv_count + output_count].reshape(spots, 4, -1, wide)]
  transfers between devices with their start and end apart: 18 -> 3, of which waited for: 16 -> 0; matrix products, arithmetic and copies ran while one was open for 16% -> 27% of each run, Pallas kernels for 0% -> 35%
where the time goes in v2:
time: 754 us; the launch traced here: 742 us
  Pallas kernels  320 us (42%)
  matrix products  214 us (28%)
  other arithmetic  94.7 us (13%)
  local copies, waits for them, and re-layouts  90.6 us (12%)
  between operations  15.8 us (2%)
    pallas_call x7, Pallas kernels, gather_x(): pl.pallas_call(functools.partial(gather_kernel, rows), out_shape=jax.Shap...  140 us
    pallas_call x5, Pallas kernels, scatter_x(): pl.pallas_call(functools.partial(scatter_kernel, rows), out_shape=jax.Sha...  107 us
    unnamed x204, local copies, waits for them, and re-layouts  54.5 us
    pallas_call x1, Pallas kernels, seq_sum(): pl.pallas_call(functools.partial(seq_sum_kernel, cols), out_shape=jax.Sha...  53.3 us
    concatenate x1, other arithmetic, local(): jnp.concatenate([gate_term.astype(bf16), down_term.astype(bf16)], axis=1)  23.9 us
    dot_general x1, matrix products, local(): jnp.einsum('td,tf->df', mid_all, jnp.concatenate([expert_dpre, shared_dpr...  22.8 us
    pallas_call x1, Pallas kernels, small_sum(): pl.pallas_call(small_sum_kernel, out_shape=jax.ShapeDtypeStruct(vec.shape...  20.2 us
    dot_general x1, matrix products, local(): jnp.einsum('tf,df->td', expert_dpre, expert_gate_up[0], preferred_element...  19.5 us
  transfers between devices with their start and end apart: 3, of which 0 were waited for; matrix products, arithmetic and copies ran while one was open for 27% of the time, Pallas kernels for 35%

profile of v2, /device:TPU:1, one launch (start us, length us, event | category | flops | bytes accessed | tf_op | source)
XLA Modules:
  0.0 741.7 jit_solution(15580998851667195615)
XLA Ops:
  13.8 4.7 collective-permute-start
  18.6 23.6 %gather_0.1 = bf16[1024,2048]{1,0:T(8,128)(2,1)S(1)} custom-call(bf16[128,2048]{1,0:T(8,128)(2,1)S(1)} %fusion.47.src), custom_call_target="tpu_custom_call" | custom-call | tf_op jit(solution)/shard_map/gather_0/pallas_call | solution.py:266
  46.9 22.8 %gather_3.1 = bf16[1024,2048]{1,0:T(8,128)(2,1)S(1)} custom-call(bf16[128,2048]{1,0:T(8,128)(2,1)S(1)} %copy-done.9), custom_call_target="tpu_custom_call" | custom-call | tf_op jit(solution)/shard_map/gather_3/pallas_call | solution.py:266
  72.6 4.7 fusion.130
  77.2 3.5 compare_and_fusion
  81.5 11.5 %fusion.22 = f32[1024,1760]{0,1:T(8,128)} fusion(bf16[1024,2048]{1,0:T(8,128)(2,1)S(1)} %copy-done.6, bf16[1408,2048]{1,0:T(8,128)(2,1)} %bitcast.193, bf16[352,2048]{1,0:T(8,128)(2,1)S(1)} %copy-done.92), kind=kOutput, calls=%fused_computation.42 | convolution fusion | flops 7396392960 | bytes 18612224 | tf_op jit(solution)/shard_map/td,fd->tf/dot_general | solution.py:513
  94.8 16.3 %gather_1.1 = bf16[1024,1160]{1,0:T(8,128)(2,1)S(1)} custom-call(bf16[128,1160]{1,0:T(8,128)(2,1)S(1)} %concatenate.108.src), custom_call_target="tpu_custom_call" | custom-call | tf_op jit(solution)/shard_map/gather_1/pallas_call | solution.py:266
  114.0 8.2 %fusion.73 = f32[2048,1024,2]{0,1,2:T(8,128)} fusion(bf16[2048,64,1]{1,0,2:T(8,128)(2,1)S(1)} %fusion.61, bf16[1024,2,32]{0,2,1:T(8,128)(2,1)S(1)} %copy-done.57, bf16[1024,2,32]{0,2,1:T(8,128)(2,1)S(1)} %get-tuple-element.121), kind=kOutput, calls=%fused_computation.163 | convolution fusion | flops 537395200 | bytes 17301504 | tf_op jit(solution)/shard_map/qhc,kc->hqk/dot_general | solution.py:407
  122.2 12.1 %fusion.128 = (f32[2,1024]{1,0:T(2,128)S(1)}, f32[2,1024,2048]{2,1,0:T(8,128)}) fusion(f32[2048,1024,2]{0,1,2:T(8,128)} %fusion.73, bf16[2048,2,256]{0,2,1:T(8,128)(2,1)S(1)} %bitcast.162, f32[1024,2,192]{0,2,1:T(8,128)S(1)} %bitcast.156, pred[1024,2048]{1,0:T(8,128)(4,1)S(1)} %copy-done.14), kind=kOutput, calls=%fused_computation.256 | convolution fusion | flops 1090516992 | bytes 37232640 | tf_op jit(solution)/shard_map/qhc,khc->hqk/dot_general | solution.py:404
  134.3 8.1 %fusion.2 = f32[2,1024]{1,0:T(2,128)S(1)} fusion(f32[2,1024,2048]{2,1,0:T(8,128)} %get-tuple-element.157, f32[2,1024]{1,0:T(2,128)S(1)} %get-tuple-element.156), kind=kLoop, calls=%fused_computation.10 | loop fusion | flops 8386560 | bytes 16793600 | tf_op jit(solution)/shard_map/reduce_sum | solution.py:476
  142.5 8.0 %fusion.42 = bf16[2,128,1024]{2,1,0:T(8,128)(2,1)S(1)} fusion(f32[2,1024,2048]{2,1,0:T(8,128)} %get-tuple-element.157, f32[2,1024]{1,0:T(2,128)S(1)} %fusion.2, f32[2,1024]{1,0:T(2,128)S(1)} %get-tuple-element.156, bf16[2048,2,256]{0,2,1:T(8,128)(2,1)} %bitcast.163), kind=kOutput, calls=%fused_computation.95 | convolution fusion | flops 1086586880 | bytes 18366464 | tf_op jit(solution)/shard_map/hqk,khc->qhc/dot_general | solution.py:479
  152.7 22.7 %scatter_0.1 = f32[128,2048]{1,0:T(8,128)S(1)} custom-call(bf16[1024,2048]{1,0:T(8,128)(2,1)S(1)} %convolution_convert_fusion.2.src), custom_call_target="tpu_custom_call" | custom-call | tf_op jit(solution)/shard_map/scatter_0/pallas_call | solution.py:325
  176.3 22.9 %gather_2.1 = bf16[1024,2048]{1,0:T(8,128)(2,1)S(1)} custom-call(bf16[128,2048]{1,0:T(8,128)(2,1)S(1)} %multiply_convert_fusion.7.src), custom_call_target="tpu_custom_call" | custom-call | tf_op jit(solution)/shard_map/gather_2/pallas_call | solution.py:266
  204.3 17.9 %fusion.6 = f32[1024,2816]{0,1:T(8,128)} fusion(bf16[1024,2048]{1,0:T(8,128)(2,1)S(1)} %gather_2.1, bf16[1,2048,2816]{2,1,0:T(8,128)(2,1)} %param.27), kind=kOutput, calls=%fused_computation.14 | convolution fusion | flops 11811160064 | bytes 27262976 | tf_op jit(solution)/shard_map/dot_general | solution.py:507
  224.3 5.2 multiply_convert_fusion.5
  231.8 8.0 %multiply_convert_fusion.2 = (bf16[1024,1408]{0,1:T(8,128)(2,1)S(1)}, bf16[1024,1408]{0,1:T(8,128)(2,1)S(1)}, f32[1024]{0:T(1024)S(1)}, bf16[1024,1408]{0,1:T(8,128)(2,1)}) fusion(f32[1024,2816]{0,1:T(8,128)} %fusion.6, f32[1024,1760]{0,1:T(8,128)S(1)} %bitcast.167, f32[1024]{0:T(1024)S(1)} %multiply_reduce_fusion.5), kind=kLoop, calls=%fused_computation.34 | loop fusion | flops 28834816 | bytes 25960448 | tf_op jit(solution)/shard_map/convert.57
  242.2 3.1 pad_maximum_fusion.2
  245.3 22.8 %convolution_convert_fusion = bf16[2048,3520]{0,1:T(8,128)(2,1)} fusion(bf16[1024,2048]{1,0:T(8,128)(2,1)S(1)} %gather_2.1, bf16[1024,352]{0,1:T(8,128)(2,1)} %copy-done.54, bf16[1024,352]{0,1:T(8,128)(2,1)} %copy-done.53, bf16[1024,1408]{0,1:T(8,128)(2,1)} %copy-done.29, bf16[1024,1408]{0,1:T(8,128)(2,1)} %copy-done.28), kind=kOutput, calls=%fused_computation.9 | convolution fusion | flops 14799994880 | bytes 25821184 | tf_op jit(solution)/shard_map/td,tf->df/dot_general | solution.py:524
  268.1 12.2 %fusion.19 = bf16[2048,1760]{0,1:T(8,128)(2,1)} fusion(bf16[1024,2048]{1,0:T(8,128)(2,1)S(1)} %copy-done.7, bf16[1024,1408]{0,1:T(8,128)(2,1)} %get-tuple-element.105, bf16[1024,352]{0,1:T(8,128)(2,1)} %get-tuple-element.112), kind=kOutput, calls=%fused_computation.30 | convolution fusion | flops 7392788480 | bytes 15007744 | tf_op jit(solution)/shard_map/td,tf->df/dot_general | solution.py:523
  280.3 23.9 %pad_maximum_fusion = bf16[2048,5280]{0,1:T(8,128)(2,1)} fusion(bf16[2048,1760]{0,1:T(8,128)(2,1)} %fusion.19, bf16[2048,3520]{0,1:T(8,128)(2,1)} %convolution_convert_fusion), kind=kLoop, calls=%fused_computation | loop fusion | flops 43253760 | bytes 43253760 | tf_op jit(solution)/shard_map/concatenate | solution.py:530
  304.2 26.1 %copy.218 = bf16[2048,5280]{1,0:T(8,128)(2,1)} copy(bf16[2048,5280]{0,1:T(8,128)(2,1)} %pad_maximum_fusion) | data formatting | bytes 43253760
  330.3 3.9 slice_bitcast_fusion.2
  335.7 4.0 copy.188
  339.7 5.3 fusion.67
  347.2 11.3 %fusion.23.src = bf16[1024,2048]{1,0:T(8,128)(2,1)S(1)} fusion(bf16[1408,2048]{1,0:T(8,128)(2,1)} %bitcast.194, bf16[352,2048]{1,0:T(8,128)(2,1)} %param.26, bf16[1024,1408]{0,1:T(8,128)(2,1)} %get-tuple-element.105, bf16[1024,352]{0,1:T(8,128)(2,1)} %get-tuple-element.112), kind=kOutput, calls=%fused_computation.44 | convolution fusion | flops 7405699072 | bytes 15007744 | tf_op jit(solution)/shard_map/dot_general | solution.py:512
  358.6 23.3 %scatter_2.1 = f32[128,2048]{1,0:T(8,128)S(1)} custom-call(bf16[1024,2048]{1,0:T(8,128)(2,1)S(1)} %fusion.23.src), custom_call_target="tpu_custom_call" | custom-call | tf_op jit(solution)/shard_map/scatter_2/pallas_call | solution.py:325
  381.9 5.8 fusion.27
  387.7 19.5 %fusion.4 = f32[1024,2048]{1,0:T(8,128)} fusion(bf16[1024,2816]{0,1:T(8,128)(2,1)} %pad_maximum_fusion.2, bf16[1,2048,2816]{2,1,0:T(8,128)(2,1)} %param.27), kind=kOutput, calls=%fused_computation.12 | convolution fusion | flops 11811160064 | bytes 25690112 | tf_op jit(solution)/shard_map/tf,df->td/dot_general | solution.py:543
  407.2 7.7 %add_convert_fusion.src = bf16[1024,2048]{1,0:T(8,128)(2,1)S(1)} fusion(f32[1024,2048]{1,0:T(8,128)} %fusion.27, f32[1024,2048]{1,0:T(8,128)} %fusion.4, f32[2048,8]{0,1:T(8,128)S(1)} %copy-done.64, f32[1024]{0:T(1024)S(1)} %mul.539, f32[8]{0:T(128)S(1)} %compare_convert_fusion, f32[1024,8]{1,0:T(8,128)S(1)} %copy-done.31, f32[1024]{0:T(1024)S(1)} %fusion.65, ...), kind=kOutput, calls=%fused_computation.18 | convolution fusion | flops 39878656 | bytes 21082144 | tf_op jit(solution)/shard_map/te,de->td/dot_general | solution.py:544
  415.0 23.2 %scatter_1.1 = f32[128,2048]{1,0:T(8,128)S(1)} custom-call(bf16[1024,2048]{1,0:T(8,128)(2,1)S(1)} %add_convert_fusion.src), custom_call_target="tpu_custom_call" | custom-call | tf_op jit(solution)/shard_map/scatter_1/pallas_call | solution.py:325
  440.1 22.9 %gather_4.1 = bf16[1024,2048]{1,0:T(8,128)(2,1)S(1)} custom-call(bf16[128,2048]{1,0:T(8,128)(2,1)S(1)} %get-tuple-element.96.src), custom_call_target="tpu_custom_call" | custom-call | tf_op jit(solution)/shard_map/gather_4/pallas_call | solution.py:266
  464.7 11.1 %multiply_reduce_fusion = (f32[2,1024]{1,0:T(2,128)S(1)}, f32[2,1024,2048]{2,1,0:T(8,128)}) fusion(f32[2,1024,2048]{2,1,0:T(8,128)} %get-tuple-element.157, f32[2,1024]{1,0:T(2,128)S(1)} %log_add_fusion, bf16[1024,2,128]{0,2,1:T(8,128)(2,1)S(1)} %bitcast.172, bf16[2048,2,256]{0,2,1:T(8,128)(2,1)S(1)} %bitcast.164), kind=kOutput, calls=%fused_computation.5 | convolution fusion | flops 1086322688 | bytes 35143680 | tf_op jit(solution)/shard_map/qhc,khc->hqk/dot_general | solution.py:564
  475.8 12.1 %multiply_convert_fusion = bf16[2,1024,2048]{2,1,0:T(8,128)(2,1)S(1)} fusion(f32[2,1024,2048]{2,1,0:T(8,128)} %get-tuple-element.159, f32[2,1024,2048]{2,1,0:T(8,128)} %get-tuple-element.157, f32[2,1024]{1,0:T(2,128)S(1)} %get-tuple-element.158, f32[2,1024]{1,0:T(2,128)S(1)} %log_add_fusion), kind=kLoop, calls=%fused_computation.4 | loop fusion | flops 16777216 | bytes 41959424 | tf_op jit(solution)/shard_map/convert_element_type | solution.py:569
  489.2 10.3 %fusion.32 = bf16[2048,2,128]{0,2,1:T(8,128)(2,1)S(1)} fusion(bf16[1024,2,128]{0,2,1:T(8,128)(2,1)S(1)} %bitcast.173, f32[2,1024,2048]{2,1,0:T(8,128)} %get-tuple-element.157, f32[2,1024]{1,0:T(2,128)S(1)} %log_add_fusion), kind=kOutput, calls=%fused_computation.61 | convolution fusion | flops 1082130432 | bytes 18358272 | tf_op jit(solution)/shard_map/hqk,qhc->khc/dot_general | solution.py:589
  505.6 14.9 %scatter_3.1 = f32[128,1152]{1,0:T(8,128)S(1)} custom-call(bf16[1024,1152]{1,0:T(8,128)(2,1)S(1)} %pad_maximum_fusion.12.src), custom_call_target="tpu_custom_call" | custom-call | tf_op jit(solution)/shard_map/scatter_3/pallas_call | solution.py:325
  522.5 6.1 fusion.44
  528.7 6.4 fusion.43
  543.3 5.7 fusion.131
  550.9 10.8 %gather_5.1 = bf16[1024,576]{1,0:T(8,128)(2,1)S(1)} custom-call(bf16[128,576]{1,0:T(8,128)(2,1)S(1)} %pad_maximum_fusion.25.src), custom_call_target="tpu_custom_call" | custom-call | tf_op jit(solution)/shard_map/gather_5/pallas_call | solution.py:266
  567.5 53.3 %seq_sum.1 = bf16[2,16,112,512]{3,2,1,0:T(8,128)(2,1)} custom-call(bf16[2,16,112,512]{3,2,1,0:T(8,128)(2,1)} %pad_maximum_fusion.9.src), custom_call_target="tpu_custom_call" | custom-call | tf_op jit(solution)/shard_map/seq_sum/pallas_call | solution.py:196
  625.1 2.8 slice.363
  630.6 20.7 %gather_6.1 = bf16[2048,576]{1,0:T(8,128)(2,1)S(1)} custom-call(bf16[256,576]{1,0:T(8,128)(2,1)S(1)} %maximum_bitcast_fusion.1.src), custom_call_target="tpu_custom_call" | custom-call | tf_op jit(solution)/shard_map/gather_6/pallas_call | solution.py:266
  652.7 4.7 copy.197
  657.4 2.8 fusion.36
  660.3 4.0 convert_element_type.180.src
  664.3 22.7 %scatter_4.1 = f32[128,2048]{1,0:T(8,128)S(1)} custom-call(bf16[1024,2048]{1,0:T(8,128)(2,1)S(1)} %convert_element_type.180.src), custom_call_target="tpu_custom_call" | custom-call | tf_op jit(solution)/shard_map/scatter_4/pallas_call | solution.py:325
  688.9 20.2 %small_sum.1 = f32[168,128]{1,0:T(8,128)S(1)} custom-call(f32[168,128]{1,0:T(8,128)S(1)} %bitcast.154), custom_call_target="tpu_custom_call" | custom-call | tf_op jit(solution)/shard_map/small_sum/pallas_call | solution.py:74
  731.8 2.9 copy.199
  (316 shorter events, 99.2 us)
Async XLA Ops:
  7.2 716.4 %reduce-scatter.4.cloned.1.call-start = ((), (), s32[]{:S(2)}) async-start(), calls=%async_computation.1 | async-start | bytes 23396352
  7.3 38.4 %copy-start.80 = (f32[32]{0:T(128)}, f32[32]{0:T(128)S(1)}, u32[]{:S(2)}) copy-start(f32[32]{0:T(128)S(1)} %multiply_exponential_fusion) | copy-start | bytes 388
  11.5 35.4 %copy-start.9 = (bf16[128,2048]{1,0:T(8,128)(2,1)S(1)}, bf16[128,2048]{1,0:T(8,128)(2,1)}, u32[]{:S(2)}) copy-start(bf16[128,2048]{1,0:T(8,128)(2,1)} %src.1) | copy-start | bytes 1572868
  13.8 79.9 %collective-permute-start = (bf16[128,576]{1,0:T(8,128)(2,1)}, bf16[128,576]{1,0:T(8,128)(2,1)}, u32[]{:S(2)}, u32[]{:S(2)}) collective-permute-start(bf16[128,576]{1,0:T(8,128)(2,1)} %pad_maximum_fusion.24), channel_id=1, source_target_pairs={{0,8},{16,24},{32,40},{48,56},{64,72},{80,88},{96,104},{112,120},{... | collective-permute-start | bytes 442376 | tf_op jit(solution)/shard_map/ppermute | solution.py:340
  46.9 33.8 %copy-start.47 = (f32[1024,32]{0,1:T(8,128)}, f32[1024,32]{0,1:T(8,128)S(1)}, u32[]{:S(2)}) copy-start(f32[1024,32]{0,1:T(8,128)S(1)} %get-tuple-element.149) | copy-start | bytes 393220
  72.6 8.9 %copy-start.6 = (bf16[1024,2048]{1,0:T(8,128)(2,1)S(1)}, bf16[1024,2048]{1,0:T(8,128)(2,1)}, u32[]{:S(2)}) copy-start(bf16[1024,2048]{1,0:T(8,128)(2,1)} %copy-done.5) | copy-start | bytes 12582916
  72.6 8.9 %copy-start.92 = (bf16[352,2048]{1,0:T(8,128)(2,1)S(1)}, bf16[352,2048]{1,0:T(8,128)(2,1)}, u32[]{:S(2)}) copy-start(bf16[352,2048]{1,0:T(8,128)(2,1)} %param.26) | copy-start | bytes 4325380
  81.5 32.5 %copy-start.55 = (bf16[1024,2,32]{0,2,1:T(8,128)(2,1)}, bf16[1024,2,32]{0,2,1:T(8,128)(2,1)S(1)}, u32[]{:S(2)}) copy-start(bf16[1024,2,32]{0,2,1:T(8,128)(2,1)S(1)} %get-tuple-element.121) | copy-start | bytes 393220
  81.5 11.5 %copy-start.86 = (s32[128,6]{0,1:T(8,128)S(1)}, s32[128,6]{0,1:T(8,128)}, u32[]{:S(2)}) copy-start(s32[128,6]{0,1:T(8,128)} %param.30) | copy-start | bytes 9220
  81.5 12.2 %copy-start.61 = (bf16[128,32]{1,0:T(8,128)(2,1)S(1)}, bf16[128,32]{1,0:T(8,128)(2,1)}, u32[]{:S(2)}) copy-start(bf16[128,32]{1,0:T(8,128)(2,1)} %copy-done.60) | copy-start | bytes 24580
  81.5 12.2 %copy-start.63 = (bf16[128,32]{1,0:T(8,128)(2,1)S(1)}, bf16[128,32]{1,0:T(8,128)(2,1)}, u32[]{:S(2)}) copy-start(bf16[128,32]{1,0:T(8,128)(2,1)} %copy-done.62) | copy-start | bytes 24580
  113.9 8.3 %copy-start.37 = (bf16[2048,512]{0,1:T(8,128)(2,1)}, bf16[2048,512]{0,1:T(8,128)(2,1)S(1)}, u32[]{:S(2)}) copy-start(bf16[2048,512]{0,1:T(8,128)(2,1)S(1)} %convolution_convert_fusion.3) | copy-start | bytes 6291460
  114.0 8.3 %copy-start.14 = (pred[1024,2048]{1,0:T(8,128)(4,1)S(1)}, pred[1024,2048]{1,0:T(8,128)(4,1)}, u32[]{:S(2)}) copy-start(pred[1024,2048]{1,0:T(8,128)(4,1)} %compare_and_fusion) | copy-start | bytes 6291460
  114.0 8.2 %copy-start.16 = (f32[1024,384]{0,1:T(8,128)S(1)}, f32[1024,384]{0,1:T(8,128)}, u32[]{:S(2)}) copy-start(f32[1024,384]{0,1:T(8,128)} %copy-done.15) | copy-start | bytes 4718596
  134.3 8.1 %copy-start.69 = (f32[2,1024]{1,0:T(2,128)}, f32[2,1024]{1,0:T(2,128)S(1)}, u32[]{:S(2)}) copy-start(f32[2,1024]{1,0:T(2,128)S(1)} %get-tuple-element.156) | copy-start | bytes 24580
  142.5 8.0 %copy-start.71 = (f32[2,1024]{1,0:T(2,128)}, f32[2,1024]{1,0:T(2,128)S(1)}, u32[]{:S(2)}) copy-start(f32[2,1024]{1,0:T(2,128)S(1)} %fusion.2) | copy-start | bytes 24580
  142.5 8.9 %copy-start.51 = (bf16[256,2048]{1,0:T(8,128)(2,1)S(1)}, bf16[256,2048]{1,0:T(8,128)(2,1)}, u32[]{:S(2)}) copy-start(bf16[256,2048]{1,0:T(8,128)(2,1)} %param.22) | copy-start | bytes 3145732
  152.6 22.8 %copy-start.20 = (bf16[128,2048]{1,0:T(8,128)(2,1)S(1)}, bf16[128,2048]{1,0:T(8,128)(2,1)}, u32[]{:S(2)}) copy-start(bf16[128,2048]{1,0:T(8,128)(2,1)} %param.16) | copy-start | bytes 1572868
  152.6 23.5 %copy-start.66 = (f32[2048]{0:T(1024)S(1)}, f32[2048]{0:T(1024)}, u32[]{:S(2)}) copy-start(f32[2048]{0:T(1024)} %param.23) | copy-start | bytes 24580
  175.6 24.9 %copy-start.18 = (f32[128,2048]{1,0:T(8,128)}, f32[128,2048]{1,0:T(8,128)S(1)}, u32[]{:S(2)}) copy-start(f32[128,2048]{1,0:T(8,128)S(1)} %get-tuple-element.101) | copy-start | bytes 3145732
  175.6 23.6 %copy-start.73 = (bf16[2048,8]{0,1:T(8,128)(2,1)S(1)}, bf16[2048,8]{0,1:T(8,128)(2,1)}, u32[]{:S(2)}) copy-start(bf16[2048,8]{0,1:T(8,128)(2,1)} %get-tuple-element.142) | copy-start | bytes 98308
  175.6 23.6 %copy-start.74 = (bf16[2048,8]{0,1:T(8,128)(2,1)S(1)}, bf16[2048,8]{0,1:T(8,128)(2,1)}, u32[]{:S(2)}) copy-start(bf16[2048,8]{0,1:T(8,128)(2,1)} %get-tuple-element.143) | copy-start | bytes 98308
  175.6 23.6 %copy-start.75 = (bf16[2048,8]{0,1:T(8,128)(2,1)S(1)}, bf16[2048,8]{0,1:T(8,128)(2,1)}, u32[]{:S(2)}) copy-start(bf16[2048,8]{0,1:T(8,128)(2,1)} %get-tuple-element.144) | copy-start | bytes 98308
  176.2 24.3 %copy-start.84 = (f32[128]{0:T(128)}, f32[128]{0:T(128)S(1)}, u32[]{:S(2)}) copy-start(f32[128]{0:T(128)S(1)} %get-tuple-element.155) | copy-start | bytes 1540
  199.2 46.1 %copy-start.8 = (bf16[1024,2048]{1,0:T(8,128)(2,1)}, bf16[1024,2048]{1,0:T(8,128)(2,1)S(1)}, u32[]{:S(2)}) copy-start(bf16[1024,2048]{1,0:T(8,128)(2,1)S(1)} %gather_2.1) | copy-start | bytes 12582916
  202.6 20.1 %copy-start.30 = (f32[1024,8]{1,0:T(8,128)}, f32[1024,8]{1,0:T(8,128)S(1)}, u32[]{:S(2)}) copy-start(f32[1024,8]{1,0:T(8,128)S(1)} %get-tuple-element.99) | copy-start | bytes 98308
  222.6 9.2 %slice-start = ((s8[7208960]{0:T(1024)(128)(4,1)}), s8[4194304]{0:T(1024)(128)(4,1)S(1)}, s32[]{:S(2)}) async-start(s8[7208960]{0:T(1024)(128)(4,1)} %bitcast.166), calls=%async_computation.2 | async-start | bytes 8388608
  245.3 22.8 %copy-start.7 = (bf16[1024,2048]{1,0:T(8,128)(2,1)S(1)}, bf16[1024,2048]{1,0:T(8,128)(2,1)}, u32[]{:S(2)}) copy-start(bf16[1024,2048]{1,0:T(8,128)(2,1)} %copy-done.5) | copy-start | bytes 12582916
  358.6 23.3 %copy-start.34 = (bf16[1024,704]{0,1:T(8,128)(2,1)S(1)}, bf16[1024,704]{0,1:T(8,128)(2,1)}, u32[]{:S(2)}) copy-start(bf16[1024,704]{0,1:T(8,128)(2,1)} %pad_maximum_fusion.17) | copy-start | bytes 4325380
  358.6 23.3 %copy-start.35 = (bf16[2048,352]{0,1:T(8,128)(2,1)S(1)}, bf16[2048,352]{0,1:T(8,128)(2,1)}, u32[]{:S(2)}) copy-start(bf16[2048,352]{0,1:T(8,128)(2,1)} %get-tuple-element.110) | copy-start | bytes 4325380
  358.6 23.3 %copy-start.36 = (bf16[2048,352]{0,1:T(8,128)(2,1)S(1)}, bf16[2048,352]{0,1:T(8,128)(2,1)}, u32[]{:S(2)}) copy-start(bf16[2048,352]{0,1:T(8,128)(2,1)} %get-tuple-element.111) | copy-start | bytes 4325380
  387.7 19.5 %copy-start.64 = (f32[2048,8]{0,1:T(8,128)S(1)}, f32[2048,8]{0,1:T(8,128)}, u32[]{:S(2)}) copy-start(f32[2048,8]{0,1:T(8,128)} %param.24) | copy-start | bytes 196612
  414.9 23.3 %copy-start.19 = (f32[128,2048]{1,0:T(8,128)S(1)}, f32[128,2048]{1,0:T(8,128)}, u32[]{:S(2)}) copy-start(f32[128,2048]{1,0:T(8,128)} %copy-done.18) | copy-start | bytes 3145732
  414.9 23.3 %copy-start.67 = (f32[2048]{0:T(1024)S(1)}, f32[2048]{0:T(1024)}, u32[]{:S(2)}) copy-start(f32[2048]{0:T(1024)} %param.23) | copy-start | bytes 24580
  415.0 23.3 %copy-start.85 = (f32[128]{0:T(128)S(1)}, f32[128]{0:T(128)}, u32[]{:S(2)}) copy-start(f32[128]{0:T(128)} %copy-done.84) | copy-start | bytes 1540
  415.0 23.6 %copy-start.90 = (f32[128]{0:T(128)S(1)}, f32[128]{0:T(128)}, u32[]{:S(2)}) copy-start(f32[128]{0:T(128)} %get-tuple-element.154) | copy-start | bytes 1540
  440.1 22.9 %copy-start.70 = (f32[2,1024]{1,0:T(2,128)S(1)}, f32[2,1024]{1,0:T(2,128)}, u32[]{:S(2)}) copy-start(f32[2,1024]{1,0:T(2,128)} %copy-done.69) | copy-start | bytes 24580
  440.1 22.9 %copy-start.72 = (f32[2,1024]{1,0:T(2,128)S(1)}, f32[2,1024]{1,0:T(2,128)}, u32[]{:S(2)}) copy-start(f32[2,1024]{1,0:T(2,128)} %copy-done.71) | copy-start | bytes 24580
  440.1 22.9 %copy-start.52 = (bf16[256,2048]{1,0:T(8,128)(2,1)S(1)}, bf16[256,2048]{1,0:T(8,128)(2,1)}, u32[]{:S(2)}) copy-start(bf16[256,2048]{1,0:T(8,128)(2,1)} %param.22) | copy-start | bytes 3145732
  475.8 12.1 %copy-start.17 = (f32[1024,384]{0,1:T(8,128)S(1)}, f32[1024,384]{0,1:T(8,128)}, u32[]{:S(2)}) copy-start(f32[1024,384]{0,1:T(8,128)} %copy-done.15) | copy-start | bytes 4718596
  487.9 14.1 %copy-start.12 = (bf16[2,1024,2048]{2,1,0:T(8,128)(2,1)}, bf16[2,1024,2048]{2,1,0:T(8,128)(2,1)S(1)}, u32[]{:S(2)}) copy-start(bf16[2,1024,2048]{2,1,0:T(8,128)(2,1)S(1)} %multiply_convert_fusion) | copy-start | bytes 25165828
  504.8 17.6 %copy-start.40 = (bf16[2048,64,1]{1,0,2:T(8,128)(2,1)S(1)}, bf16[2048,64,1]{1,0,2:T(8,128)(2,1)}, u32[]{:S(2)}) copy-start(bf16[2048,64,1]{1,0,2:T(8,128)(2,1)} %copy-done.39) | copy-start | bytes 786436
  520.6 7.9 %copy-start.48 = (f32[1024,32]{0,1:T(8,128)S(1)}, f32[1024,32]{0,1:T(8,128)}, u32[]{:S(2)}) copy-start(f32[1024,32]{0,1:T(8,128)} %copy-done.47) | copy-start | bytes 393220
  520.6 7.9 %copy-start.59 = (f32[1024,32]{0,1:T(8,128)S(1)}, f32[1024,32]{0,1:T(8,128)}, u32[]{:S(2)}) copy-start(f32[1024,32]{0,1:T(8,128)} %get-tuple-element.147) | copy-start | bytes 393220
  520.7 29.5 %collective-permute-start.1 = (bf16[128,576]{1,0:T(8,128)(2,1)S(1)}, bf16[128,576]{1,0:T(8,128)(2,1)S(1)}, u32[]{:S(2)}, u32[]{:S(2)}) collective-permute-start(bf16[128,576]{1,0:T(8,128)(2,1)S(1)} %slice.464), channel_id=1, source_target_pairs={{8,0},{24,16},{40,32},{56,48},{72,64},{88,80},{104,96},{120,112},{... | collective-permute-start | bytes 442376 | tf_op jit(solution)/shard_map/ppermute | solution.py:340
  664.3 22.7 %copy-start.21 = (bf16[128,2048]{1,0:T(8,128)(2,1)S(1)}, bf16[128,2048]{1,0:T(8,128)(2,1)}, u32[]{:S(2)}) copy-start(bf16[128,2048]{1,0:T(8,128)(2,1)} %param.16) | copy-start | bytes 1572868
  664.3 22.7 %copy-start.68 = (f32[2048]{0:T(1024)S(1)}, f32[2048]{0:T(1024)}, u32[]{:S(2)}) copy-start(f32[2048]{0:T(1024)} %param.17) | copy-start | bytes 24580
  664.3 22.7 %copy-start.79 = (f32[128]{0:T(128)S(1)}, f32[128]{0:T(128)}, u32[]{:S(2)}) copy-start(f32[128]{0:T(128)} %copy-done.78) | copy-start | bytes 1540
  (52 other events, 156.8 us)
Sparse Core Ops, SparseCore 0:
  330.4 136.9 reduce-scatter.3

commit v3 on v1

v3 whole, which is shorter than its diff:
```python
import functools
import math

import jax
import jax.numpy as jnp
from jax import lax
from jax.experimental import pallas as pl
from jax.experimental.pallas import tpu as pltpu
from jax.sharding import PartitionSpec as P

NOPE = 128
ROPE = 64
VDIM = 128
LAT = 512
F = 1408
EXPERTS = 8
EPSILON = 1e-06

VM = pltpu.VMEM
f32 = jnp.float32
bf16 = jnp.bfloat16


class Sems:
    def __init__(self, send, recv):
        self.send, self.recv, self.used, self.sent = send, recv, 0, []

    def start(self, src, dst, peer):
        copy = pltpu.make_async_remote_copy(
            src_ref=src,
            dst_ref=dst,
            send_sem=self.send.at[self.used],
            recv_sem=self.recv.at[self.used],
            device_id=peer,
            device_id_type=pl.DeviceIdType.MESH,
        )
        copy.start()
        self.used += 1
        self.sent.append(copy)
        return copy

    def finish(self):
        for copy in self.sent:
            copy.wait_send()


class Place:
    def __init__(self):
        me, spot = lax.axis_index("exp"), lax.axis_index("seq")
        self.me = me
        self.chip, self.core = me // 2, me % 2
        self.z, self.y = spot // 4, spot % 4
        self.sibling = {"exp": self.chip * 2 + 1 - self.core}
        self.across = [lambda i: {"exp": i * 2 + self.core}, lambda i: {"seq": self.z * 4 + i}, lambda i: {"seq": i * 4 + self.y}]
        self.along = [self.chip, self.y, self.z]

    def hop(self, axis, distance):
        return self.across[axis](lax.rem(self.along[axis] + distance, 4))


def greet(peers):
    barrier = pltpu.get_barrier_semaphore()
    for peer in peers:
        pl.semaphore_signal(barrier, inc=1, device_id=peer, device_id_type=pl.DeviceIdType.MESH)
    pl.semaphore_wait(barrier, len(peers))


def together(*streams):
    streams = list(streams)
    while streams:
        for stream in list(streams):
            try:
                next(stream)
            except StopIteration:
                streams.remove(stream)


def gather_stream(sems, at, src, out, rows, local):
    half = rows // 2
    right, left = at.hop(0, 1), at.hop(0, 3)
    me = at.me
    near_right = lax.rem(at.chip + 1, 4) * 2 + at.core
    near_left = lax.rem(at.chip + 3, 4) * 2 + at.core
    far = lax.rem(at.chip + 2, 4) * 2 + at.core

    def part(owner, h):
        return out.at[pl.ds(pl.multiple_of(owner * rows + h * half, half), half)]

    def own(h):
        return src.at[pl.ds(h * half, half)]

    ra = sems.start(own(0), part(me, 0), right)
    lb = sems.start(own(1), part(me, 1), left)
    rb = sems.start(own(1), part(me, 1), right)
    la = sems.start(own(0), part(me, 0), left)
    sib = [sems.start(src, out.at[pl.ds(pl.multiple_of(me * rows, rows), rows)], at.sibling)]
    mine = pltpu.make_async_copy(src, out.at[pl.ds(pl.multiple_of(me * rows, rows), rows)], local)
    mine.start()
    yield
    ra.wait_recv()
    far_a = sems.start(part(near_left, 0), part(near_left, 0), right)
    sib.append(sems.start(part(near_left, 0), part(near_left, 0), at.sibling))
    lb.wait_recv()
    far_b = sems.start(part(near_right, 1), part(near_right, 1), left)
    sib.append(sems.start(part(near_right, 1), part(near_right, 1), at.sibling))
    yield
    rb.wait_recv()
    sib.append(sems.start(part(near_left, 1), part(near_left, 1), at.sibling))
    la.wait_recv()
    sib.append(sems.start(part(near_right, 0), part(near_right, 0), at.sibling))
    yield
    far_a.wait_recv()
    sib.append(sems.start(part(far, 0), part(far, 0), at.sibling))
    far_b.wait_recv()
    sib.append(sems.start(part(far, 1), part(far, 1), at.sibling))
    yield
    mine.wait()
    for copy in sib:
        copy.wait_recv()


def scatter_stream(sems, at, src, pair, hop, last, rows, done):
    half = rows // 2
    right, left = at.hop(0, 1), at.hop(0, 3)
    order = (2, 1, 3, 0)
    sib = []
    for dist in order:
        owner = lax.rem(at.chip + dist, 4) * 2 + 1 - at.core
        sib.append(sems.start(src.at[pl.ds(pl.multiple_of(owner * rows, rows), rows)], pair.at[dist], at.sibling))

    def fold(i):
        sib[i].wait_recv()
        owner = lax.rem(at.chip + order[i], 4) * 2 + at.core
        mine = src[pl.ds(pl.multiple_of(owner * rows, rows), rows)]
        pair[order[i]] = (pair[order[i]].astype(f32) + mine.astype(f32)).astype(bf16)

    def add(ref, other):
        ref[...] = (ref[...].astype(f32) + other[...].astype(f32)).astype(bf16)

    first, second = pl.ds(0, half), pl.ds(half, half)
    yield
    fold(0)
    far_a = sems.start(pair.at[2, first], hop.at[0], right)
    far_b = sems.start(pair.at[2, second], hop.at[1], left)
    yield
    fold(1)
    dir_b = sems.start(pair.at[1, second], last.at[0], right)
    fold(2)
    dir_a = sems.start(pair.at[3, first], last.at[1], left)
    yield
    far_a.wait_recv()
    add(pair.at[1, first], hop.at[0])
    acc_a = sems.start(pair.at[1, first], last.at[2], right)
    far_b.wait_recv()
    add(pair.at[3, second], hop.at[1])
    acc_b = sems.start(pair.at[3, second], last.at[3], left)
    yield
    sib[3].wait_recv()
    dir_b.wait_recv()
    dir_a.wait_recv()
    acc_a.wait_recv()
    acc_b.wait_recv()
    for h, ends in ((0, (1, 2)), (1, (0, 3))):
        mine = src[pl.ds(pl.multiple_of(at.me * rows + h * half, half), half)].astype(f32)
        total = mine + pair[0, pl.ds(h * half, half)].astype(f32)
        done(h, total + last[ends[0]].astype(f32) + last[ends[1]].astype(f32))


def scatter_scratch(rows, cols):
    return [
        pltpu.VMEM((4, rows, cols), bf16),
        pltpu.VMEM((2, rows // 2, cols), bf16),
        pltpu.VMEM((4, rows // 2, cols), bf16),
    ]


def ring_sum(sems, at, axis, block, hop, last):
    right, left = at.hop(axis, 1), at.hop(axis, 3)
    to = [lax.rem(at.along[axis] + d, 4) for d in range(4)]

    def add(ref, other):
        ref[...] = (ref[...].astype(f32) + other[...].astype(f32)).astype(bf16)

    far_a = sems.start(block(to[2], 0), hop.at[0], right)
    far_b = sems.start(block(to[2], 1), hop.at[1], left)
    dir_b = sems.start(block(to[1], 1), last.at[0], right)
    dir_a = sems.start(block(to[3], 0), last.at[1], left)
    yield
    far_a.wait_recv()
    add(block(to[1], 0), hop.at[0])
    acc_a = sems.start(block(to[1], 0), last.at[2], right)
    far_b.wait_recv()
    add(block(to[3], 1), hop.at[1])
    acc_b = sems.start(block(to[3], 1), last.at[3], left)
    yield
    dir_b.wait_recv()
    dir_a.wait_recv()
    add(block(to[0], 1), last.at[0])
    add(block(to[0], 0), last.at[1])
    yield
    acc_a.wait_recv()
    add(block(to[0], 0), last.at[2])
    acc_b.wait_recv()
    add(block(to[0], 1), last.at[3])


def ring_gather(sems, at, axis, block):
    right, left = at.hop(axis, 1), at.hop(axis, 3)
    to = [lax.rem(at.along[axis] + d, 4) for d in range(4)]
    ra = sems.start(block(to[0], 0), block(to[0], 0), right)
    lb = sems.start(block(to[0], 1), block(to[0], 1), left)
    rb = sems.start(block(to[0], 1), block(to[0], 1), right)
    la = sems.start(block(to[0], 0), block(to[0], 0), left)
    yield
    ra.wait_recv()
    fa = sems.start(block(to[3], 0), block(to[3], 0), right)
    lb.wait_recv()
    fb = sems.start(block(to[1], 1), block(to[1], 1), left)
    yield
    rb.wait_recv()
    la.wait_recv()
    yield
    fa.wait_recv()
    fb.wait_recv()


def seq_stream(sems, at, work, out, scratch, axes):
    half = work.shape[1] // 2
    hop1, last1, hop2, last2 = scratch

    def wide(ref):
        return lambda i, h: ref.at[pl.ds(i * 4 + 2 * h, 2)]

    def narrow(ref):
        return lambda i, h: ref.at[at.along[axes[0]] * 4 + i, pl.ds(h * half, half)]

    yield from ring_sum(sems, at, axes[0], wide(work), hop1, last1)
    yield from ring_sum(sems, at, axes[1], narrow(work), hop2, last2)
    own = at.along[axes[0]] * 4 + at.along[axes[1]]
    out[own] = work[own]
    yield from ring_gather(sems, at, axes[1], narrow(out))
    yield from ring_gather(sems, at, axes[0], wide(out))


def seq_scratch(rows, cols):
    return [
        pltpu.VMEM((2, 2, rows, cols), bf16),
        pltpu.VMEM((4, 2, rows, cols), bf16),
        pltpu.VMEM((2, rows // 2, cols), bf16),
        pltpu.VMEM((4, rows // 2, cols), bf16),
    ]


def seq_direct(sems, at, work, out, wide_in, narrow_in):
    y, z = at.y, at.z
    copies = [sems.start(work.at[pl.ds(lax.rem(y + d, 4) * 4, 4)], wide_in.at[d - 1], at.hop(1, d)) for d in (1, 2, 3)]
    yield
    for copy in copies:
        copy.wait_recv()
    mine = pl.ds(y * 4, 4)
    work[mine] = (
        work[mine].astype(f32) + wide_in[0].astype(f32) + (wide_in[1].astype(f32) + wide_in[2].astype(f32))
    ).astype(bf16)
    copies = [sems.start(work.at[y * 4 + lax.rem(z + d, 4)], narrow_in.at[d - 1], at.hop(2, d)) for d in (1, 2, 3)]
    yield
    for copy in copies:
        copy.wait_recv()
    own = y * 4 + z
    out[own] = (
        work[own].astype(f32) + narrow_in[0].astype(f32) + (narrow_in[1].astype(f32) + narrow_in[2].astype(f32))
    ).astype(bf16)
    copies = [sems.start(out.at[own], out.at[own], at.hop(2, d)) for d in (1, 2, 3)]
    yield
    for copy in copies:
        copy.wait_recv()
    copies = [sems.start(out.at[mine], out.at[mine], at.hop(1, d)) for d in (1, 2, 3)]
    yield
    for copy in copies:
        copy.wait_recv()


def small_stream(sems, at, slots, out):
    stages = [(at.core, 2, lambda d: at.sibling)] + [
        (at.along[axis], 4, functools.partial(at.hop, axis)) for axis in range(3)
    ]
    for stage, (place, count, name) in enumerate(stages):
        if stage:
            slots[stage, place] = out[...]
        copies = [sems.start(slots.at[stage, place], slots.at[stage, place], name(d)) for d in range(1, count)]
        yield
        for copy in copies:
            copy.wait_recv()
        total = slots[stage, 0]
        for i in range(1, count):
            total = total + slots[stage, i]
        out[...] = total


def swapped(tensor):
    lane = lax.broadcasted_iota(jnp.int32, tensor.shape, 1)
    return jnp.where(lane % 64 < 32, pltpu.roll(tensor, 96, 1), pltpu.roll(tensor, 32, 1))


SHARED_TILE = 384
MLP_TILES = (("s", 0, 384), ("e", 0, 512), ("e", 512, 512), ("e", 1024, 384))
ROW_STEP = 256


def dot_nn(a, b):
    return lax.dot_general(a, b, (((1,), (0,)), ((), ())), preferred_element_type=f32)


def dot_nt(a, b):
    return lax.dot_general(a, b, (((1,), (1,)), ((), ())), preferred_element_type=f32)


def dot_tn(a, b):
    return lax.dot_general(a, b, (((0,), (0,)), ((), ())), preferred_element_type=f32)


def mlp_kernel(
    mid_h, grad_h, pair_s_h, pair_e_h, down_s_h, down_e_h, router, router_turned, hot,
    mid_part, moe_part, router_out, terms_h,
    mid, grad, pair_s, pair_e, down_s, down_e, act, dpre, logit, stage, load, store,
):
    rows, width = mid_h.shape
    expert = lax.axis_index("exp")
    sources = [(mid_h, mid), (grad_h, grad), (pair_s_h, pair_s), (down_s_h, down_s), (pair_e_h, pair_e), (down_e_h, down_e)]
    loads = [pltpu.make_async_copy(src, dst, load.at[i]) for i, (src, dst) in enumerate(sources)]
    for c in loads:
        c.start()
    for c in loads[:4]:
        c.wait()
    lane = lax.broadcasted_iota(jnp.int32, (ROW_STEP, 128), 1)
    own_lane = lane == expert

    def block(index):
        return pl.ds(pl.multiple_of(index * ROW_STEP, ROW_STEP), ROW_STEP)

    def gates(r):
        raw = dot_nn(mid[r], router[...])
        raw = raw + (pltpu.roll(raw, 128 - EXPERTS, 1) + pltpu.roll(raw, 128 - 2 * EXPERTS, 1))
        raw = jnp.where(lane < EXPERTS, raw, -1e30)
        raw = jnp.exp(raw - jnp.max(raw, axis=1, keepdims=True))
        probs = raw / jnp.sum(raw, axis=1, keepdims=True)
        own = jnp.sum(jnp.where(own_lane, probs * hot[r].astype(f32), 0.0), axis=1, keepdims=True)
        return own, probs

    def piece(r, kind, start, size, own):
        pair, down = (pair_s, down_s) if kind == "s" else (pair_e, down_e)
        span = SHARED_TILE if kind == "s" else F
        act_at = F if kind == "s" else 0
        dpre_at = 2 * F if kind == "s" else 0
        gate = dot_nn(mid[r], pair[:, start : start + size])
        up = dot_nn(mid[r], pair[:, span + start : span + start + size])
        dact = dot_nt(grad[r], down[start : start + size])
        logistic = 1.0 / (1.0 + jnp.exp(-gate))
        passed = gate * logistic
        out = passed * up
        total = None
        if kind == "e":
            total = jnp.sum(out * dact, axis=1, keepdims=True)
            out = out * own
            dact = dact * own
        act[r, act_at + start : act_at + start + size] = out.astype(bf16)
        slope = logistic + passed * (1.0 - logistic)
        dpre[r, dpre_at + start : dpre_at + start + size] = (dact * up * slope).astype(bf16)
        dpre[r, dpre_at + span + start : dpre_at + span + start + size] = (dact * passed).astype(bf16)
        return total

    @pl.loop(0, rows // ROW_STEP)
    def _(index):
        piece(block(index), *MLP_TILES[0], None)

    loads[4].wait()
    loads[5].wait()

    @pl.loop(0, rows // ROW_STEP)
    def _(index):
        r = block(index)
        own, probs = gates(r)
        total = piece(r, *MLP_TILES[1], own)
        for tile in MLP_TILES[2:]:
            total = total + piece(r, *tile, own)
        logit[r] = ((own * total) * (jnp.where(own_lane, 1.0, 0.0) - probs)).astype(bf16)

    half = width // 2
    count = 0

    def flush(slot, at):
        return pltpu.make_async_copy(stage.at[slot], terms_h.at[pl.ds(at[0], half), pl.ds(at[1], 512)], store.at[slot])

    def tiles_of(left, right, columns, offset):
        @pl.loop(0, columns // 512)
        def _(index):
            spot = pl.multiple_of(index * 512, 512)
            for part in range(2):
                @pl.when(index > 0)
                def _():
                    flush(part, (part * half, pl.multiple_of(spot + offset - 512, 512))).wait()
                stage[part] = dot_tn(left[:, part * half : (part + 1) * half], right[:, pl.ds(spot, 512)]).astype(bf16)
                flush(part, (part * half, pl.multiple_of(spot + offset, 512))).start()
        for part in range(2):
            flush(part, (part * half, columns - 512 + offset)).wait()

    tiles_of(mid, dpre, dpre.shape[1], 0)
    tiles_of(grad, act, act.shape[1] // 512 * 512, dpre.shape[1])
    tail = act.shape[1] // 512 * 512
    rest = act.shape[1] - tail
    for part in range(2):
        stage[part, :, :rest] = dot_tn(grad[:, part * half : (part + 1) * half], act[:, tail:]).astype(bf16)
        last = pltpu.make_async_copy(
            stage.at[part, :, pl.ds(0, rest)],
            terms_h.at[pl.ds(part * half, half), pl.ds(dpre.shape[1] + tail, rest)], store.at[part])
        last.start()
    router_out[...] = dot_tn(logit[...], mid[...])[:EXPERTS]
    for part in range(2):
        pltpu.make_async_copy(
            stage.at[part, :, pl.ds(0, rest)],
            terms_h.at[pl.ds(part * half, half), pl.ds(dpre.shape[1] + tail, rest)], store.at[part]).wait()

    @pl.loop(0, rows // ROW_STEP)
    def _(index):
        r = block(index)
        total = dot_nt(dpre[r, : 2 * F], pair_e[...]) + dot_nt(dpre[r, 2 * F :], pair_s[...])
        mid_part[r] = (total + dot_nn(logit[r], router_turned[...])).astype(bf16)
        moe_part[r] = (dot_nn(act[r, :F], down_e[...]) + dot_nn(act[r, F:], down_s[...])).astype(bf16)


def mlp(mid_all, grad_all, pair_s, pair_e, down_s, down_e, router, router_turned, hot):
    rows, width = mid_all.shape
    hidden = F + SHARED_TILE
    whole = pl.BlockSpec(memory_space=VM)
    held = pl.BlockSpec(memory_space=pl.ANY)
    return pl.pallas_call(
        mlp_kernel,
        out_shape=[
            jax.ShapeDtypeStruct((rows, width), bf16),
            jax.ShapeDtypeStruct((rows, width), bf16),
            jax.ShapeDtypeStruct((EXPERTS, width), f32),
            jax.ShapeDtypeStruct((width, 3 * hidden), bf16),
        ],
        in_specs=[held] * 6 + [whole] * 3,
        out_specs=[whole, whole, whole, held],
        scratch_shapes=[
            pltpu.VMEM(mid_all.shape, bf16), pltpu.VMEM(grad_all.shape, bf16),
            pltpu.VMEM(pair_s.shape, bf16), pltpu.VMEM(pair_e.shape, bf16),
            pltpu.VMEM(down_s.shape, bf16), pltpu.VMEM(down_e.shape, bf16),
            pltpu.VMEM((rows, hidden), bf16), pltpu.VMEM((rows, 2 * hidden), bf16),
            pltpu.VMEM((rows, 128), bf16), pltpu.VMEM((2, width // 2, 512), bf16),
            pltpu.SemaphoreType.DMA((6,)), pltpu.SemaphoreType.DMA((2,)),
        ],
        compiler_params=pltpu.CompilerParams(vmem_limit_bytes=63 << 20),
        cost_estimate=pl.CostEstimate(flops=18 * rows * width * hidden, bytes_accessed=60 << 20, transcendentals=rows * hidden),
        name="mlp",
    )(mid_all, grad_all, pair_s, pair_e, down_s, down_e, router, router_turned, hot)


ATT = 256
SCALE = (NOPE + ROPE) ** (-0.5)
LOG2E = 1.4426950408889634


def score_pieces(q, packed, ropes, qseg, kseg, head, i):
    rows = pl.ds(ATT * i, ATT)
    prev = packed.shape[0] - q.shape[0]
    lane = lax.broadcasted_iota(jnp.int32, (ATT, 2 * ROPE), 1)
    rope = jnp.where(lane // ROPE == head, q[rows, 2 * NOPE :], jnp.zeros((), bf16))
    query = jnp.concatenate([q[rows, head * NOPE : (head + 1) * NOPE], rope], axis=1)
    edge = prev + ATT * i
    pieces = []
    for start, end in ((0, edge), (edge, edge + ATT)):
        keys = jnp.concatenate(
            [packed[start:end, head * 2 * NOPE : head * 2 * NOPE + NOPE], ropes[start:end]], axis=1
        )
        scores = dot_nt(query, keys)
        allowed = qseg[rows] == kseg[:, start:end]
        if start:
            allowed = allowed & (
                lax.broadcasted_iota(jnp.int32, scores.shape, 1)
                <= lax.broadcasted_iota(jnp.int32, scores.shape, 0)
            )
        pieces.append((start, end, jnp.where(allowed, scores, -1e30), keys))
    return query, pieces


def attend_kernel(q, packed, ropes, qseg, kseg, heads, lse):
    for head in range(2):
        for i in range(q.shape[0] // ATT):
            rows = pl.ds(ATT * i, ATT)
            _, pieces = score_pieces(q, packed, ropes, qseg, kseg, head, i)
            top = jnp.maximum(*[jnp.max(scores, axis=1, keepdims=True) for _, _, scores, _ in pieces])
            total, out = 0.0, 0.0
            for start, end, scores, _ in pieces:
                weights = jnp.exp2((scores - top) * (SCALE * LOG2E))
                total = total + jnp.sum(weights, axis=1, keepdims=True)
                values = packed[start:end, head * 2 * NOPE + NOPE : (head + 1) * 2 * NOPE]
                out = out + dot_nn(weights.astype(bf16), values)
            heads[rows, head * VDIM : (head + 1) * VDIM] = (out / total).astype(bf16)
            lse[head, rows] = top * (SCALE * LOG2E) + jnp.log2(total)


def attend(q, packed, ropes, qseg, kseg):
    whole = pl.BlockSpec(memory_space=VM)
    rows = q.shape[0]
    return pl.pallas_call(
        attend_kernel,
        out_shape=[jax.ShapeDtypeStruct((rows, 2 * VDIM), bf16), jax.ShapeDtypeStruct((2, rows, 1), f32)],
        in_specs=[whole] * 5,
        out_specs=[whole] * 2,
        compiler_params=pltpu.CompilerParams(vmem_limit_bytes=56 << 20),
        name="attend",
    )(q, packed, ropes, qseg, kseg)


def attend_back_kernel(
    grad, wo, heads, q, packed, ropes, qseg, kseg, lse, cosine, sine, kv_proj, latents,
    dq, key_grad, kvo, head_grad, dkey, dvalue, drope, dpacked,
):
    rows = q.shape[0]
    prev = packed.shape[0] - rows
    step = 256
    for i in range(rows // step):
        r = pl.ds(i * step, step)
        head_grad[r] = dot_nt(grad[r], wo[...]).astype(bf16)
    for head in range(2):
        dkey[...] = jnp.zeros_like(dkey)
        dvalue[...] = jnp.zeros_like(dvalue)
        for i in range(rows // ATT):
            r = pl.ds(ATT * i, ATT)
            query, pieces = score_pieces(q, packed, ropes, qseg, kseg, head, i)
            upstream = head_grad[r, head * VDIM : (head + 1) * VDIM]
            probs, dprobs = [], []
            inner = 0.0
            for start, end, scores, _ in pieces:
                p = jnp.exp2(scores * (SCALE * LOG2E) - lse[head, r])
                d = dot_nt(upstream, packed[start:end, head * 2 * NOPE + NOPE : (head + 1) * 2 * NOPE])
                inner = inner + jnp.sum(p * d, axis=1, keepdims=True)
                probs.append(p)
                dprobs.append(d)
            dquery = 0.0
            for (start, end, _, keys), p, d in zip(pieces, probs, dprobs):
                ds = (p * (d - inner)).astype(bf16)
                dquery = dquery + dot_nn(ds, keys)
                dkey[start:end] += dot_tn(ds, query)
                dvalue[start:end] += dot_tn(p.astype(bf16), upstream)
            dquery = dquery * SCALE
            dq[r, head * NOPE : (head + 1) * NOPE] = dquery[:, :NOPE].astype(bf16)
            rope = dquery[:, NOPE:]
            rope = rope * cosine[r] - swapped(rope) * sine[r]
            lane = lax.broadcasted_iota(jnp.int32, rope.shape, 1)
            if head == 0:
                dq[r, 2 * NOPE :] = rope.astype(bf16)
            else:
                dq[r, 2 * NOPE :] = jnp.where(lane < ROPE, dq[r, 2 * NOPE :], rope.astype(bf16))
        dpacked[:, head * 2 * NOPE : head * 2 * NOPE + NOPE] = (dkey[:, :NOPE] * SCALE).astype(bf16)
        dpacked[:, head * 2 * NOPE + NOPE : (head + 1) * 2 * NOPE] = dvalue[...].astype(bf16)
        if head == 0:
            drope[...] = dkey[:, NOPE:]
        else:
            drope[...] += dkey[:, NOPE:]
    span = LAT + 2 * ROPE
    for i in range(packed.shape[0] // 512):
        r = pl.ds(512 * i, 512)
        at = span if i * 512 < prev else 0
        to = pl.ds(512 * i - (0 if i * 512 < prev else prev), 512)
        key_grad[to, at : at + LAT] = dot_nt(dpacked[r], kv_proj[...]).astype(bf16)
        rope = drope[r]
        key_grad[to, at + LAT : at + span] = ((rope + pltpu.roll(rope, ROPE, 1)) * SCALE).astype(bf16)
    spots, wide = kvo.shape[0], kvo.shape[2]
    kv = dot_tn(latents[...], dpacked[...]).astype(bf16)
    kv_rows = kv.shape[0] // spots
    kvo[:, :kv_rows] = kv.reshape(spots, kv_rows, wide)
    out_rows = wo.shape[0] // spots
    for j in range(grad.shape[1] // wide):
        term = dot_tn(heads[...], grad[:, j * wide : (j + 1) * wide]).astype(bf16)
        kvo[:, kv_rows + j * out_rows : kv_rows + (j + 1) * out_rows] = term.reshape(spots, out_rows, wide)


def attend_back(grad, wo, heads, q, packed, ropes, qseg, kseg, lse, cosine, sine, kv_proj, latents):
    whole = pl.BlockSpec(memory_space=VM)
    rows, keys = q.shape[0], packed.shape[0]
    spots = lax.axis_size("seq")
    kvo_rows = (kv_proj.shape[0] * kv_proj.shape[1] + wo.shape[0] * wo.shape[1]) // spots // LAT
    return pl.pallas_call(
        attend_back_kernel,
        out_shape=[
            jax.ShapeDtypeStruct(q.shape, bf16),
            jax.ShapeDtypeStruct((rows, 2 * (LAT + 2 * ROPE)), bf16),
            jax.ShapeDtypeStruct((spots, kvo_rows, LAT), bf16),
        ],
        in_specs=[whole] * 13,
        out_specs=[whole] * 3,
        scratch_shapes=[
            pltpu.VMEM((rows, 2 * VDIM), bf16),
            pltpu.VMEM((keys, 2 * NOPE), f32),
            pltpu.VMEM((keys, VDIM), f32),
            pltpu.VMEM((keys, 2 * ROPE), f32),
            pltpu.VMEM(packed.shape, bf16),
        ],
        compiler_params=pltpu.CompilerParams(vmem_limit_bytes=56 << 20),
        name="attend_back",
    )(grad, wo, heads, q, packed, ropes, qseg, kseg, lse, cosine, sine, kv_proj, latents)


SPAN = LAT + 2 * ROPE


def tail_kernel(
    dq, key_grad, kvo, normed, wq, wl, raw, latent_gain, cosine, sine, gain, upstream, rows_in, small_in,
    query_out, kvo_out, latent_out, grad_out, small_out,
    work0, work1, key_sum, in_part, in_sum, in_own, lat_rows, lat_all, lat_work, lat_sum, prev_out, prev_in, small,
    r0, r1, r2, r3, s0, s1, s2, s3, k0, k1, k2, n0, n1, n2, lw, ln, send, recv, local,
):
    at = Place()
    sems = Sems(send, recv)
    greet([at.sibling] + [at.hop(axis, d) for axis in range(3) for d in (1, 2, 3)])
    rows = raw.shape[0]
    half = rows // 2
    own = pl.ds(pl.multiple_of(at.me * rows, rows), rows)

    def keep_key(h, total):
        key_sum[h * half : (h + 1) * half] = total

    def keep_in(h, total):
        in_sum[h * half : (h + 1) * half] = total

    keys = scatter_stream(sems, at, key_grad, k0, k1, k2, rows, keep_key)
    next(keys)
    work0[...] = dot_tn(normed[...], dq[...]).astype(bf16).reshape(work0.shape)
    work1[...] = kvo[...]
    first = seq_stream(sems, at, work0, query_out, (r0, r1, r2, r3), (1, 2))
    second = seq_stream(sems, at, work1, kvo_out, (s0, s1, s2, s3), (2, 1))
    next(first)
    next(second)
    next(keys)
    gain_part = jnp.zeros((1, normed.shape[1]), f32)
    step = 256
    for i in range(dq.shape[0] // step):
        r = pl.ds(i * step, step)
        part = dot_nt(dq[r], wq[...])
        gain_part = gain_part + jnp.sum(part * normed[r].astype(f32), axis=0, keepdims=True)
        in_part[r] = part.astype(bf16)
        if i == 1:
            next(keys)
    in_rows = scatter_stream(sems, at, in_part, n0, n1, n2, rows, keep_in)
    running = []

    def latents():
        yield from keys
        prev_out[...] = key_sum[:, SPAN:].astype(bf16)
        partner = at.across[1](at.y + 1 - 2 * lax.rem(at.y, 2))
        swap = sems.start(prev_out, prev_in, partner)
        yield
        swap.wait_recv()
        own_grad = key_sum[:, :SPAN] + jnp.where(lax.rem(at.y, 2) == 0, prev_in[...].astype(f32), 0.0)
        x = raw[...]
        inverse = lax.rsqrt(jnp.mean(x * x, axis=1, keepdims=True) + EPSILON)
        u = own_grad[:, :LAT]
        lat_gain_part = jnp.sum(u * x * inverse, axis=0, keepdims=True)
        s = u * latent_gain[...]
        inner = jnp.mean(s * x, axis=1, keepdims=True)
        lat_rows[:, :LAT] = (inverse * s - x * (inverse * inverse * inverse) * inner).astype(bf16)
        rope = own_grad[:, LAT:]
        rope = rope * cosine[...] - swapped(rope) * sine[...]
        lane = lax.broadcasted_iota(jnp.int32, rope.shape, 1)
        lat_rows[:, LAT:] = jnp.where(lane < ROPE, rope, 0.0).astype(bf16)
        gathered = gather_stream(sems, at, lat_rows, lat_all, rows, local.at[0])
        next(gathered)
        in_own[...] = dot_nt(lat_rows[...], wl[...])
        attn_gain = gain_part + jnp.sum(in_own[...] * normed[own].astype(f32), axis=0, keepdims=True)
        small[0, at.core] = small_in[...]
        small[0, at.core, EXPERTS : EXPERTS + 1] = attn_gain / gain[...]
        small[0, at.core, EXPERTS + 2 : EXPERTS + 3, :LAT] = lat_gain_part
        running.append(small_stream(sems, at, small, small_out))
        yield from gathered
        width = lat_work.shape[0] * lat_work.shape[1]
        mine = normed[:, pl.ds(pl.multiple_of(at.me * width, width), width)]
        lat_work[...] = dot_tn(mine, lat_all[...]).astype(bf16).reshape(lat_work.shape)
        yield from seq_direct(sems, at, lat_work, lat_sum, lw, ln)
        yield from gather_stream(sems, at, lat_sum, latent_out, lat_sum.shape[0], local.at[1])

    running += [latents(), in_rows, first, second]
    while running:
        for stream in list(running):
            try:
                next(stream)
            except StopIteration:
                running.remove(stream)
    u = in_sum[...] + in_own[...]
    x = rows_in[...].astype(f32)
    inverse = lax.rsqrt(jnp.mean(x * x, axis=1, keepdims=True) + EPSILON)
    s = u * gain[...]
    inner = jnp.mean(s * x, axis=1, keepdims=True)
    grad_out[...] = (upstream[...] + (inverse * s - x * (inverse * inverse * inverse) * inner)).astype(bf16)
    sems.finish()


def tail(dq, key_grad, kvo, normed, wq, wl, raw, latent_gain, cosine, sine, gain, upstream, rows_in, small_in):
    whole = pl.BlockSpec(memory_space=VM)
    rows, width = rows_in.shape
    spots = kvo.shape[0]
    query_shape = (spots, width // spots, dq.shape[1])
    slice_rows = width // lax.axis_size("exp") // spots
    lat_shape = (spots, slice_rows, SPAN)
    return pl.pallas_call(
        tail_kernel,
        out_shape=[
            jax.ShapeDtypeStruct(query_shape, bf16),
            jax.ShapeDtypeStruct(kvo.shape, bf16),
            jax.ShapeDtypeStruct((8 * spots, slice_rows, SPAN), bf16),
            jax.ShapeDtypeStruct((rows, width), bf16),
            jax.ShapeDtypeStruct(small_in.shape, f32),
        ],
        in_specs=[whole] * 14,
        out_specs=[whole] * 5,
        scratch_shapes=[
            pltpu.VMEM(query_shape, bf16),
            pltpu.VMEM(kvo.shape, bf16),
            pltpu.VMEM((rows, 2 * SPAN), f32),
            pltpu.VMEM((8 * rows, width), bf16),
            pltpu.VMEM((rows, width), f32),
            pltpu.VMEM((rows, width), f32),
            pltpu.VMEM((rows, SPAN), bf16),
            pltpu.VMEM((8 * rows, SPAN), bf16),
            pltpu.VMEM(lat_shape, bf16),
            pltpu.VMEM(lat_shape, bf16),
            pltpu.VMEM((rows, SPAN), bf16),
            pltpu.VMEM((rows, SPAN), bf16),
            pltpu.VMEM((4, 4) + small_in.shape, f32),
            *seq_scratch(*query_shape[1:]),
            *seq_scratch(*kvo.shape[1:]),
            *scatter_scratch(rows, 2 * SPAN),
            *scatter_scratch(rows, width),
            pltpu.VMEM((3, 4, slice_rows, SPAN), bf16),
            pltpu.VMEM((3, slice_rows, SPAN), bf16),
            pltpu.SemaphoreType.DMA((120,)),
            pltpu.SemaphoreType.DMA((120,)),
            pltpu.SemaphoreType.DMA((2,)),
        ],
        compiler_params=pltpu.CompilerParams(collective_id=3, has_side_effects=True, vmem_limit_bytes=60 << 20),
        name="tail",
    )(dq, key_grad, kvo, normed, wq, wl, raw, latent_gain, cosine, sine, gain, upstream, rows_in, small_in)


def start_kernel(
    rows_in, gain, wl, latent_gain, wq, kv_proj, cosine, sine, own_cosine, own_sine, hot,
    normed, q, packed, keys, hot_all, raw,
    own_normed, ext, ext_all, prev_out, send, recv, local,
):
    at = Place()
    sems = Sems(send, recv)
    partner = at.across[1](at.y + 1 - 2 * lax.rem(at.y, 2))
    greet([at.hop(0, 1), at.hop(0, 3), at.sibling, partner])
    rows = rows_in.shape[0]
    x = rows_in[...].astype(f32)
    own_normed[...] = (x * lax.rsqrt(jnp.mean(x * x, axis=1, keepdims=True) + EPSILON) * gain[...]).astype(bf16)
    big = gather_stream(sems, at, own_normed, normed, rows, local.at[0])
    next(big)
    lat = dot_nn(own_normed[...], wl[...])
    raw[...] = lat[:, :LAT]
    x = lat[:, :LAT]
    x = x * lax.rsqrt(jnp.mean(x * x, axis=1, keepdims=True) + EPSILON) * latent_gain[...]
    rope = lat[:, LAT:]
    rope = rope * own_cosine[...] + swapped(rope) * own_sine[...]
    rope = rope + pltpu.roll(rope, ROPE, 1)
    prev_out[:, :LAT] = x.astype(bf16)
    prev_out[:, LAT:] = rope.astype(bf16)
    swap = sems.start(prev_out, ext.at[:, pl.ds(SPAN, SPAN)], partner)
    ext[:, :SPAN] = prev_out[...]
    ext[:, 2 * SPAN :] = hot[...]
    next(big)
    swap.wait_recv()
    little = gather_stream(sems, at, ext, ext_all, rows, local.at[1])
    next(little)
    together(big, little)
    block = normed.shape[0]
    step = 256
    for i in range(block // step):
        r = pl.ds(i * step, step)
        query = dot_nn(normed[r], wq[...])
        q[r, : 2 * NOPE] = query[:, : 2 * NOPE].astype(bf16)
        rope = query[:, 2 * NOPE :]
        q[r, 2 * NOPE :] = (rope * cosine[r] + swapped(rope) * sine[r]).astype(bf16)
    for part in range(2):
        r = slice((1 - part) * block, (2 - part) * block)
        keys[r] = ext_all[:, part * SPAN : (part + 1) * SPAN]
        packed[r] = dot_nn(ext_all[:, part * SPAN : part * SPAN + LAT], kv_proj[...]).astype(bf16)
    hot_all[...] = ext_all[:, 2 * SPAN :]
    sems.finish()


def start(rows_in, gain, wl, latent_gain, wq, kv_proj, cosine, sine, own_cosine, own_sine, hot):
    whole = pl.BlockSpec(memory_space=VM)
    rows, width = rows_in.shape
    block = 8 * rows
    ext_width = 2 * SPAN + hot.shape[1]
    return pl.pallas_call(
        start_kernel,
        out_shape=[
            jax.ShapeDtypeStruct((block, width), bf16),
            jax.ShapeDtypeStruct((block, wq.shape[1]), bf16),
            jax.ShapeDtypeStruct((2 * block, kv_proj.shape[1]), bf16),
            jax.ShapeDtypeStruct((2 * block, SPAN), bf16),
            jax.ShapeDtypeStruct((block, hot.shape[1]), bf16),
            jax.ShapeDtypeStruct((rows, LAT), f32),
        ],
        in_specs=[whole] * 11,
        out_specs=[whole] * 6,
        scratch_shapes=[
            pltpu.VMEM((rows, width), bf16),
            pltpu.VMEM((rows, ext_width), bf16),
            pltpu.VMEM((block, ext_width), bf16),
            pltpu.VMEM((rows, SPAN), bf16),
            pltpu.SemaphoreType.DMA((27,)),
            pltpu.SemaphoreType.DMA((27,)),
            pltpu.SemaphoreType.DMA((2,)),
        ],
        compiler_params=pltpu.CompilerParams(collective_id=0, has_side_effects=True, vmem_limit_bytes=56 << 20),
        name="start",
    )(rows_in, gain, wl, latent_gain, wq, kv_proj, cosine, sine, own_cosine, own_sine, hot)


def middle_kernel(
    heads, wo, rows_in, gain, residual, mid_all, part, own_mid, p0, p1, p2, send, recv, local
):
    at = Place()
    sems = Sems(send, recv)
    rows = rows_in.shape[0]
    half = rows // 2
    step = 256
    for i in range(heads.shape[0] // step):
        r = pl.ds(i * step, step)
        part[r] = dot_nn(heads[r], wo[...]).astype(bf16)
    greet([at.hop(0, 1), at.hop(0, 3), at.sibling])

    def done(h, total):
        r = slice(h * half, (h + 1) * half)
        x = rows_in[r].astype(f32) + total
        residual[r] = x
        own_mid[r] = (x * lax.rsqrt(jnp.mean(x * x, axis=1, keepdims=True) + EPSILON) * gain[...]).astype(bf16)

    together(scatter_stream(sems, at, part, p0, p1, p2, rows, done))
    together(gather_stream(sems, at, own_mid, mid_all, rows, local))
    sems.finish()


def middle(heads, wo, rows_in, gain):
    whole = pl.BlockSpec(memory_space=VM)
    rows, width = rows_in.shape
    return pl.pallas_call(
        middle_kernel,
        out_shape=[jax.ShapeDtypeStruct((rows, width), f32), jax.ShapeDtypeStruct((8 * rows, width), bf16)],
        in_specs=[whole] * 4,
        out_specs=[whole] * 2,
        scratch_shapes=[
            pltpu.VMEM((8 * rows, width), bf16),
            pltpu.VMEM((rows, width), bf16),
            *scatter_scratch(rows, width),
            pltpu.SemaphoreType.DMA((23,)),
            pltpu.SemaphoreType.DMA((23,)),
            pltpu.SemaphoreType.DMA,
        ],
        compiler_params=pltpu.CompilerParams(collective_id=1, has_side_effects=True, vmem_limit_bytes=56 << 20),
        name="middle",
    )(heads, wo, rows_in, gain)


def turn_kernel(
    part, residual, gain, upstream, residual_grad, gain_term, grad_all, own_grad, p0, p1, p2, send, recv, local
):
    at = Place()
    sems = Sems(send, recv)
    rows = residual.shape[0]
    half = rows // 2
    greet([at.hop(0, 1), at.hop(0, 3), at.sibling])
    gain_term[...] = jnp.zeros_like(gain_term)

    def done(h, total):
        r = slice(h * half, (h + 1) * half)
        x = residual[r]
        inverse = lax.rsqrt(jnp.mean(x * x, axis=1, keepdims=True) + EPSILON)
        gain_term[...] += jnp.sum(total * x * inverse, axis=0, keepdims=True)
        s = total * gain[...]
        inner = jnp.mean(s * x, axis=1, keepdims=True)
        grad = upstream[r].astype(f32) + (inverse * s - x * (inverse * inverse * inverse) * inner)
        residual_grad[r] = grad
        own_grad[r] = grad.astype(bf16)

    together(scatter_stream(sems, at, part, p0, p1, p2, rows, done))
    together(gather_stream(sems, at, own_grad, grad_all, rows, local))
    sems.finish()


def turn(part, residual, gain, upstream):
    whole = pl.BlockSpec(memory_space=VM)
    rows, width = residual.shape
    return pl.pallas_call(
        turn_kernel,
        out_shape=[
            jax.ShapeDtypeStruct((rows, width), f32),
            jax.ShapeDtypeStruct((1, width), f32),
            jax.ShapeDtypeStruct((8 * rows, width), bf16),
        ],
        in_specs=[whole] * 4,
        out_specs=[whole] * 3,
        scratch_shapes=[
            pltpu.VMEM((rows, width), bf16),
            *scatter_scratch(rows, width),
            pltpu.SemaphoreType.DMA((23,)),
            pltpu.SemaphoreType.DMA((23,)),
            pltpu.SemaphoreType.DMA,
        ],
        compiler_params=pltpu.CompilerParams(collective_id=2, has_side_effects=True, vmem_limit_bytes=56 << 20),
        name="turn",
    )(part, residual, gain, upstream)


def tables(position):
    lane = jnp.arange(2 * ROPE, dtype=jnp.int32)
    half = ROPE // 2
    frequency = jnp.exp((lane % half).astype(f32) * (-math.log(10000.0) / half))
    angles = position.astype(f32)[:, None] * frequency[None, :]
    sign = jnp.where(lane % ROPE < half, -1.0, 1.0)
    return jnp.cos(angles), jnp.sin(angles) * sign[None, :]


def local(
    layer_input, attn_gain, query_proj, latent_proj, latent_gain, kv_proj, output_proj, ffn_gain, router_proj,
    shared_gate_up, shared_down, expert_gate_up, expert_down, segment_ids, expert_routes, out_grad,
):
    own_rows, model_width = layer_input.shape
    block_rows = own_rows * lax.axis_size("exp")
    seq_rows = 2 * block_rows
    block_start = lax.axis_index("seq") * block_rows
    row_offset = lax.axis_index("exp") * own_rows
    query_pos = block_start + jnp.arange(block_rows, dtype=jnp.int32)
    query_seg = lax.dynamic_slice_in_dim(segment_ids, block_start, block_rows)
    key_start = block_start - block_rows
    prev_seg = lax.dynamic_slice_in_dim(segment_ids, jnp.maximum(key_start, 0), block_rows)
    prev_seg = jnp.where(key_start >= 0, prev_seg, -1)
    key_seg = jnp.concatenate([prev_seg, query_seg], axis=0)
    cosine, sine = tables(query_pos % seq_rows)
    own_cosine = lax.dynamic_slice_in_dim(cosine, row_offset, own_rows)
    own_sine = lax.dynamic_slice_in_dim(sine, row_offset, own_rows)
    head = NOPE + ROPE
    wq = jnp.concatenate(
        [
            query_proj[:, :NOPE],
            query_proj[:, head : head + NOPE],
            query_proj[:, NOPE:head],
            query_proj[:, head + NOPE :],
        ],
        axis=1,
    )
    wl = jnp.pad(latent_proj, ((0, 0), (0, SPAN - latent_proj.shape[1])))
    hot = jnp.sum(
        expert_routes[:, :, None] == jnp.arange(128, dtype=jnp.int32)[None, None, :], axis=1
    ).astype(bf16)
    attn_row, latent_row, ffn_row = attn_gain[None], latent_gain[None], ffn_gain[None]
    normed_all, q, packed, keys, hot_all, latent_raw = start(
        layer_input, attn_row, wl, latent_row, wq, kv_proj, cosine, sine, own_cosine, own_sine, hot
    )
    ropes, latents = keys[:, LAT:], keys[:, :LAT]
    late_grad, q = lax.optimization_barrier((out_grad, q))
    grad_all = lax.all_gather(late_grad, "exp", axis=0, tiled=True)
    qseg, kseg = query_seg[:, None], key_seg[None, :]
    heads, lse = attend(q, packed, ropes, qseg, kseg)
    residual, mid_all = middle(heads, output_proj, layer_input, ffn_row)

    router_high = lax.reduce_precision(router_proj, 8, 7)
    router_rest = router_proj - router_high
    router_mid = lax.reduce_precision(router_rest, 8, 7)
    router_low = router_rest - router_mid
    router_pieces = jnp.concatenate([router_high, router_mid, router_low], axis=1).astype(bf16)
    router_pieces = jnp.pad(router_pieces, ((0, 0), (0, 128 - 3 * EXPERTS)))
    router_turned = jnp.pad(router_proj.T.astype(bf16), ((0, 128 - EXPERTS), (0, 0)))
    shared_width = shared_down.shape[0]
    fill = SHARED_TILE - shared_width
    pair_s = jnp.pad(shared_gate_up, ((0, 0), (0, 0), (0, fill))).reshape(model_width, 2 * SHARED_TILE)
    down_s = jnp.pad(shared_down, ((0, fill), (0, 0)))
    mid_part, moe_part, router_term, weight_terms = mlp(
        mid_all, grad_all, pair_s, expert_gate_up[0], down_s, expert_down[0], router_pieces, router_turned, hot_all
    )
    weight_sum = lax.psum_scatter(weight_terms, "seq", scatter_dimension=0, tiled=True)
    residual_grad, ffn_term, attn_grad_all = turn(mid_part, residual, ffn_row, out_grad)
    dq, key_grad, kvo = attend_back(
        attn_grad_all, output_proj, heads, q, packed, ropes, qseg, kseg, lse, cosine, sine, kv_proj, latents
    )
    weight_sum, moe_part, dq = lax.optimization_barrier((weight_sum, moe_part, dq))
    moe_rows = lax.psum_scatter(moe_part, "exp", scatter_dimension=0, tiled=True)
    small = jnp.concatenate([router_term, jnp.zeros_like(ffn_term), ffn_term, jnp.zeros((6, model_width), f32)], axis=0)
    query_sum, kvo_sum, latent_sum, input_grad, small = tail(
        dq, key_grad, kvo, normed_all, wq, wl, latent_raw, latent_row, own_cosine, own_sine, attn_row,
        residual_grad, layer_input, small,
    )
    layer_output = (residual + moe_rows.astype(f32)).astype(bf16)
    query_sum = query_sum.reshape(model_width, -1)
    query_sum = jnp.concatenate(
        [
            query_sum[:, :NOPE],
            query_sum[:, 2 * NOPE : 2 * NOPE + ROPE],
            query_sum[:, NOPE : 2 * NOPE],
            query_sum[:, 2 * NOPE + ROPE :],
        ],
        axis=1,
    ).astype(f32)
    spots = kvo_sum.shape[0]
    kv_rows = kv_proj.shape[0] // spots
    kv_sum = kvo_sum[:, :kv_rows].reshape(kv_proj.shape).astype(f32)
    out_rows = output_proj.shape[0] // spots
    output_sum = (
        kvo_sum[:, kv_rows:]
        .reshape(spots, -1, out_rows, LAT)
        .transpose(0, 2, 1, 3)
        .reshape(output_proj.shape)
        .astype(f32)
    )
    latent_sum = latent_sum.reshape(model_width, SPAN)[:, : LAT + ROPE].astype(f32)
    pair_width = 2 * (F + SHARED_TILE)
    expert_gate_sum = weight_sum[None, :, : 2 * F].astype(f32)
    shared_gate_sum = (
        weight_sum[:, 2 * F : pair_width].reshape(own_rows, 2, SHARED_TILE)[..., :shared_width].astype(f32)
    )
    expert_down_sum = weight_sum[:, pair_width : pair_width + F].astype(f32).T[None]
    shared_down_sum = weight_sum[:, pair_width + F : pair_width + F + shared_width].astype(f32).T
    return (
        layer_output,
        input_grad,
        small[EXPERTS],
        query_sum,
        latent_sum,
        small[EXPERTS + 2, :LAT],
        kv_sum,
        output_sum,
        small[EXPERTS + 1],
        small[:EXPERTS].T,
        shared_gate_sum,
        shared_down_sum,
        expert_gate_sum,
        expert_down_sum,
    )


def solution(mesh):
    in_specs = (
        P(("seq", "exp"), None),
        P(),
        P(None, "exp"),
        P(),
        P(),
        P(None, "exp"),
        P("exp", None),
        P(),
        P(),
        P(None, None, "exp"),
        P("exp", None),
        P("exp", None, None),
        P("exp", None, None),
        P(),
        P(("seq", "exp"), None),
        P(("seq", "exp"), None),
    )
    out_specs = (
        P(("seq", "exp"), None),
        P(("seq", "exp"), None),
        P(),
        P(None, "exp"),
        P(),
        P(),
        P(None, "exp"),
        P("exp", None),
        P(),
        P(),
        P("seq", None, "exp"),
        P("exp", "seq"),
        P("exp", "seq", None),
        P("exp", None, "seq"),
    )
    return jax.shard_map(local, mesh=mesh, in_specs=in_specs, out_specs=out_specs, check_vma=False)
```

time: 1070 us -> 529 us (0.49); the launches traced: 1060 us -> 528 us
  waiting for transfers between devices: 613 us -> 59.3 us
  Pallas kernels: 0 us -> 396 us
  matrix products: 219 us -> 0 us
  blocking collectives: 69.3 us -> 0 us
  other arithmetic: 68.5 us -> 17.9 us
  local copies, waits for them, and re-layouts: 64.7 us -> 39.3 us
    pallas_call x0 -> x7, Pallas kernels: none -> 396 us  [the longest x1 111 us: tail(): pl.pallas_call(tail_kernel, out_shape=[jax.ShapeDtypeStruct(query_shape,...]
    dot_general x33 -> x0, matrix products: 219 us -> none  [the longest x1 23.8 us: local(): jnp.einsum('td,tf->df', mid_all, jnp.concatenate([expert_dpre, shared_dpr...]
    unnamed x19 -> x3, waiting for transfers between devices: 212 us -> 0.05 us
    all_gather x7 -> x1, waiting for transfers between devices: 152 us -> 0.02 us  [local(): grad_all = lax.all_gather(late_grad, 'exp', axis=0, tiled=True)]
    psum x2 -> x0, waiting for transfers between devices: 113 us -> none  [the longest x1 98.9 us: local(): lax.psum((attn_gain_term, latent_gain_term, ffn_gain_term, router_term),...]
    reduce_scatter x4 -> x2, waiting for transfers between devices: 134 us -> 59.2 us  [the longest x1 59.2 us: local(): lax.psum_scatter(weight_terms, 'seq', scatter_dimension=0, tiled=True)]
    psum x1 -> x0, blocking collectives: 69.3 us -> none  [local(): lax.psum((attn_gain_term, latent_gain_term, ffn_gain_term, router_term),...]
    unnamed x188 -> x44, local copies, waits for them, and re-layouts: 53.5 us -> 13.3 us
  transfers between devices with their start and end apart: 18 -> 3, of which waited for: 16 -> 1; matrix products, arithmetic and copies ran while one was open for 16% -> 7% of each run, Pallas kernels for 0% -> 46%
where the time goes in v3:
time: 529 us; the launch traced here: 528 us
  Pallas kernels  396 us (75%)
  waiting for transfers between devices  59.3 us (11%)
  local copies, waits for them, and re-layouts  39.3 us (7%)
  other arithmetic  17.9 us (3%)
  between operations  14.3 us (3%)
    pallas_call x1, Pallas kernels, tail(): pl.pallas_call(tail_kernel, out_shape=[jax.ShapeDtypeStruct(query_shape,...  111 us
    pallas_call x1, Pallas kernels, mlp(): pl.pallas_call(mlp_kernel, out_shape=[jax.ShapeDtypeStruct((rows, width),...  106 us
    reduce_scatter x1, waiting for transfers between devices, local(): lax.psum_scatter(weight_terms, 'seq', scatter_dimension=0, tiled=True)  59.2 us
    pallas_call x1, Pallas kernels, turn(): pl.pallas_call(turn_kernel, out_shape=[jax.ShapeDtypeStruct((rows, width)...  50 us
    pallas_call x1, Pallas kernels, middle(): pl.pallas_call(middle_kernel, out_shape=[jax.ShapeDtypeStruct((rows, widt...  48.4 us
    pallas_call x1, Pallas kernels, start(): pl.pallas_call(start_kernel, out_shape=[jax.ShapeDtypeStruct((block, widt...  47 us
    pallas_call x1, Pallas kernels, attend_back(): pl.pallas_call(attend_back_kernel, out_shape=[jax.ShapeDtypeStruct(q.shap...  24.1 us
    unnamed x44, local copies, waits for them, and re-layouts  13.3 us
  transfers between devices with their start and end apart: 3, of which 1 were waited for; matrix products, arithmetic and copies ran while one was open for 7% of the time, Pallas kernels for 46%

profile of v3, /device:TPU:1, one launch (start us, length us, event | category | flops | bytes accessed | tf_op | source)
XLA Modules:
  0.0 527.6 jit_solution(17098416643993314958)
XLA Ops:
  7.3 2.6 fusion.12
  9.9 1.2 fusion.13
  11.3 0.6 convert_element_type.81.hot
  11.9 1.9 fusion
  13.9 0.7 constant_dynamic-slice_fusion.own_sine.sine
  14.7 0.6 constant_dynamic-slice_fusion.1.own_cosine.cosine
  15.3 3.1 copy.63
  18.4 1.7 pad.20.wl
  20.2 0.5 copy-done.9
  20.7 1.6 pad_maximum_fusion.wq
  22.3 47.0 %start.1 = (bf16[1024,2048]{1,0:T(8,128)(2,1)}, bf16[1024,384]{1,0:T(8,128)(2,1)}, bf16[2048,512]{1,0:T(8,128)(2,1)}, bf16[2048,640]{1,0:T(8,128)(2,1)}, bf16[1024,128]{1,0:T(8,128)(2,1)}, /*index=5*/f32[128,512]{1,0:T(8,128)}) custom-call(bf16[128,2048]{1,0:T(8,128)(2,1)} %rows_in.5, f32[1,2048]{1,0:T(1,128)} %bitcast.50, bf16[2048,640]{1,0:T(8,128)(2,1)} %pad.20.wl, ...), custom_call_target="tpu_custom_call" | custom-call | tf_op jit(solution)/shard_map/start/pallas_call | solution.py:798
  70.0 0.9 pad.23.router
  70.9 0.9 pad.24.router_turned
  71.7 0.8 dynamic-slice_select_fusion
  72.6 1.0 copy.64.qseg
  73.6 1.3 pad.22.down_s_h
  74.9 2.1 pad.21
  77.0 2.8 copy.73.pair_s_h
  79.8 1.9 slice.70.ropes
  81.8 0.6 pad_add_fusion
  82.4 9.9 %attend.1 = (bf16[1024,256]{1,0:T(8,128)(2,1)}, f32[2,1024,1]{2,1,0:T(8,128)}) custom-call(bf16[1024,384]{1,0:T(8,128)(2,1)} %get-tuple-element.45.q, bf16[2048,512]{1,0:T(8,128)(2,1)} %get-tuple-element.46.packed, bf16[2048,128]{1,0:T(8,128)(2,1)} %slice.70.ropes, s32[1024,1]{1,0:T(8,128)} %copy.64.qseg, s32[1,2048]{1,0:T(1,128)} %bitcast.47), custom_call_target="tpu_custom_call" | custom-call | tf_op jit(solution)/shard_map/attend/pallas_call | solution.py:506
  92.3 48.4 %middle.1 = (f32[128,2048]{1,0:T(8,128)}, bf16[1024,2048]{1,0:T(8,128)(2,1)}) custom-call(bf16[1024,256]{1,0:T(8,128)(2,1)} %get-tuple-element.48.heads, bf16[256,2048]{1,0:T(8,128)(2,1)} %wo.3, bf16[128,2048]{1,0:T(8,128)(2,1)} %rows_in.5, f32[1,2048]{1,0:T(1,128)} %bitcast.52), custom_call_target="tpu_custom_call" | custom-call | tf_op jit(solution)/shard_map/middle/pallas_call | solution.py:851
  140.7 106.0 %mlp.1 = (bf16[1024,2048]{1,0:T(8,128)(2,1)}, bf16[1024,2048]{1,0:T(8,128)(2,1)}, f32[8,2048]{1,0:T(8,128)}, bf16[2048,5376]{1,0:T(8,128)(2,1)}) custom-call(bf16[1024,2048]{1,0:T(8,128)(2,1)} %get-tuple-element.50.mid_h, bf16[1024,2048]{1,0:T(8,128)(2,1)} %all-gather.2.cloned.1.call-done.grad_h, bf16[2048,768]{1,0:T(8,128)(2,1)} %copy.73.pair_s_h, ...), custom_call_target="tpu_custom_call" | custom-call | flops 67645734912 | bytes 62914560 | tf_op jit(solution)/shard_map/mlp/pallas_call | solution.py:435
  246.8 1.7 copy-done.5
  248.5 1.5 slice.71.latents
  249.9 50.0 %turn.1 = (f32[128,2048]{1,0:T(8,128)}, f32[1,2048]{1,0:T(1,128)}, bf16[1024,2048]{1,0:T(8,128)(2,1)}) custom-call(bf16[1024,2048]{1,0:T(8,128)(2,1)} %get-tuple-element.55.part, f32[128,2048]{1,0:T(8,128)} %get-tuple-element.49.residual, f32[1,2048]{1,0:T(1,128)} %bitcast.53, bf16[128,2048]{1,0:T(8,128)(2,1)} %upstream.1), custom_call_target="tpu_custom_call" | custom-call | tf_op jit(solution)/shard_map/turn/pallas_call | solution.py:898
  299.9 24.1 %attend_back.1 = (bf16[1024,384]{1,0:T(8,128)(2,1)}, bf16[1024,1280]{1,0:T(8,128)(2,1)}, bf16[16,96,512]{2,1,0:T(8,128)(2,1)}) custom-call(bf16[1024,2048]{1,0:T(8,128)(2,1)} %get-tuple-element.56.grad, bf16[256,2048]{1,0:T(8,128)(2,1)} %wo.3, bf16[1024,256]{1,0:T(8,128)(2,1)} %get-tuple-element.48.heads, bf16[1024,384]{1,0:T(8,128)(2,1)} %get-tuple-element.45.q, ...), custom_call_target="tpu_custom_call" | custom-call | tf_op jit(solution)/shard_map/attend_back/pallas_call | solution.py:585
  324.0 59.2 %reduce-scatter.3.cloned.1.call-done = bf16[128,5376]{1,0:T(8,128)(2,1)} async-done(((bf16[2048,5376]{1,0:T(8,128)(2,1)}), bf16[128,5376]{1,0:T(8,128)(2,1)}) %reduce-scatter.3.cloned.1.call-update) | async-done | bytes 1376272 | tf_op jit(solution)/shard_map/reduce_scatter | solution.py:985
  383.4 0.7 maximum_maximum_fusion.small_in
  384.1 111.1 %tail.1 = (bf16[16,128,384]{2,1,0:T(8,128)(2,1)}, bf16[16,96,512]{2,1,0:T(8,128)(2,1)}, bf16[128,16,640]{2,1,0:T(8,128)(2,1)}, bf16[128,2048]{1,0:T(8,128)(2,1)}, f32[16,2048]{1,0:T(8,128)}) custom-call(bf16[1024,384]{1,0:T(8,128)(2,1)} %get-tuple-element.60.dq, bf16[1024,1280]{1,0:T(8,128)(2,1)} %get-tuple-element.61.key_grad, ...), custom_call_target="tpu_custom_call" | custom-call | tf_op jit(solution)/shard_map/tail/pallas_call | solution.py:706
  495.3 1.2 slice.79
  496.5 1.3 slice.80
  497.8 0.6 slice.78
  498.4 0.8 copy.71
  499.4 1.0 convert_bitcast_fusion.1
  500.4 1.1 copy.72
  501.8 1.4 copy.69
  503.2 2.2 copy.76
  505.4 2.9 copy.75
  508.4 2.8 convert_element_type.87
  511.2 0.8 slice_convert_fusion
  511.9 1.1 bitcast_convert_fusion.1
  513.4 2.3 maximum_convert_fusion
  515.7 0.6 fusion.14
  516.3 0.6 slice_bitcast_fusion
  516.9 1.2 bitcast_convert_fusion
  518.1 1.9 add_convert_fusion
  520.1 0.8 copy.78
  (60 shorter events, 2.1 us)
Async XLA Ops:
  7.2 2.7 copy-start.3
  7.2 3.9 copy-start.18
  7.2 133.5 %all-gather.2.cloned.1.call-start = ((), (), s32[]{:S(2)}) async-start(), calls=%async_computation.2 | async-start | bytes 4718592 | tf_op jit(solution)/shard_map/all_gather | solution.py:966
  13.8 0.8 copy-start.1
  13.8 4.5 copy-start
  18.4 1.8 copy-start.6
  18.4 1.8 copy-start.7
  18.4 1.8 copy-start.8
  18.4 2.3 copy-start.9
  22.3 47.3 %copy-start.14 = (f32[2048,8]{0,1:T(8,128)S(1)}, f32[2048,8]{0,1:T(8,128)}, u32[]{:S(2)}) copy-start(f32[2048,8]{0,1:T(8,128)} %param.24) | copy-start | bytes 196612
  69.3 4.3 copy-start.10
  69.3 313.9 %reduce-scatter.3.cloned.1.call-start = ((), (), s32[]{:S(2)}) async-start(), calls=%async_computation.3 | async-start | bytes 23396352 | tf_op jit(solution)/shard_map/reduce_scatter | solution.py:985
  246.7 1.7 copy-start.5
  246.8 271.4 %reduce-scatter.5.cloned.1.call-start = ((), (), s32[]{:S(2)}) async-start(), calls=%async_computation.4 | async-start | bytes 4718592 | tf_op jit(solution)/shard_map/reduce_scatter | solution.py:991
  324.0 59.4 %copy-start.15 = (f32[8,2048]{1,0:T(8,128)S(1)}, f32[8,2048]{1,0:T(8,128)}, u32[]{:S(2)}) copy-start(f32[8,2048]{1,0:T(8,128)} %get-tuple-element.66) | copy-start | bytes 196612
  324.0 59.4 %copy-start.17 = (f32[1,2048]{1,0:T(1,128)S(1)}, f32[1,2048]{1,0:T(1,128)}, u32[]{:S(2)}) copy-start(f32[1,2048]{1,0:T(1,128)} %get-tuple-element.67) | copy-start | bytes 24580
  495.2 2.6 copy-start.16
  495.2 3.2 copy-start.11
  495.2 4.0 slice-start
  511.2 1.9 copy-start.4
  513.4 3.5 copy-start.12
  513.4 4.7 copy-start.2
  515.7 4.4 copy-start.13
Sparse Core Ops, SparseCore 0:
  69.4 33.1 all-gather.1
  246.9 136.2 reduce-scatter.2
  385.8 63.0 reduce-scatter.4

commit v4 on v3

--- a/solution.py
+++ b/solution.py
@@ -3,6 +3,7 @@
 
 import jax
 import jax.numpy as jnp
+import numpy as np
 from jax import lax
 from jax.experimental import pallas as pl
 from jax.experimental.pallas import tpu as pltpu
@@ -119,12 +120,15 @@
         copy.wait_recv()
 
 
-def scatter_stream(sems, at, src, pair, hop, last, rows, done):
+def scatter_stream(sems, at, src, pair, hop, last, rows, done, ready=None):
     half = rows // 2
     right, left = at.hop(0, 1), at.hop(0, 3)
     order = (2, 1, 3, 0)
     sib = []
-    for dist in order:
+
+    def offer(dist):
+        if ready is not None:
+            ready(dist)
         owner = lax.rem(at.chip + dist, 4) * 2 + 1 - at.core
         sib.append(sems.start(src.at[pl.ds(pl.multiple_of(owner * rows, rows), rows)], pair.at[dist], at.sibling))
 
@@ -138,13 +142,23 @@
         ref[...] = (ref[...].astype(f32) + other[...].astype(f32)).astype(bf16)
 
     first, second = pl.ds(0, half), pl.ds(half, half)
-    yield
+    offer(2)
+    offer(1)
+    if ready is None:
+        offer(3)
+        offer(0)
+        yield
     fold(0)
     far_a = sems.start(pair.at[2, first], hop.at[0], right)
     far_b = sems.start(pair.at[2, second], hop.at[1], left)
-    yield
+    if ready is None:
+        yield
+    else:
+        offer(3)
     fold(1)
     dir_b = sems.start(pair.at[1, second], last.at[0], right)
+    if ready is not None:
+        offer(0)
     fold(2)
     dir_a = sems.start(pair.at[3, first], last.at[1], left)
     yield
@@ -301,8 +315,7 @@
     return jnp.where(lane % 64 < 32, pltpu.roll(tensor, 96, 1), pltpu.roll(tensor, 32, 1))
 
 
-SHARED_TILE = 384
-MLP_TILES = (("s", 0, 384), ("e", 0, 512), ("e", 512, 512), ("e", 1024, 384))
+PAD = 384
 ROW_STEP = 256
 
 
@@ -318,27 +331,38 @@
     return lax.dot_general(a, b, (((0,), (0,)), ((), ())), preferred_element_type=f32)
 
 
+def row_block(index):
+    return pl.ds(pl.multiple_of(index * ROW_STEP, ROW_STEP), ROW_STEP)
+
+
+def router_pieces(router):
+    high = router.astype(bf16).astype(f32)
+    middle_part = (router - high).astype(bf16).astype(f32)
+    low = router - high - middle_part
+    fill = jnp.zeros((128 - 3 * EXPERTS, router.shape[1]), f32)
+    return jnp.concatenate([high, middle_part, low, fill], axis=0).astype(bf16)
+
+
 def mlp_kernel(
-    mid_h, grad_h, pair_s_h, pair_e_h, down_s_h, down_e_h, router, router_turned, hot,
-    mid_part, moe_part, router_out, terms_h,
-    mid, grad, pair_s, pair_e, down_s, down_e, act, dpre, logit, stage, load, store,
+    mid_h, grad_h, pair_s_h, pair_e_h, down_s_h, down_e_h, router, hot,
+    terms_h, act_h, dpre_h, logit, router_out,
+    mid, grad, pair_s, pair_e, down_s, down_e, act, dpre, pieces, stage, load, store, keep,
 ):
     rows, width = mid_h.shape
+    shared = down_s.shape[0]
     expert = lax.axis_index("exp")
     sources = [(mid_h, mid), (grad_h, grad), (pair_s_h, pair_s), (down_s_h, down_s), (pair_e_h, pair_e), (down_e_h, down_e)]
     loads = [pltpu.make_async_copy(src, dst, load.at[i]) for i, (src, dst) in enumerate(sources)]
     for c in loads:
         c.start()
+    pieces[...] = router_pieces(router[...])
     for c in loads[:4]:
         c.wait()
     lane = lax.broadcasted_iota(jnp.int32, (ROW_STEP, 128), 1)
     own_lane = lane == expert
 
-    def block(index):
-        return pl.ds(pl.multiple_of(index * ROW_STEP, ROW_STEP), ROW_STEP)
-
     def gates(r):
-        raw = dot_nn(mid[r], router[...])
+        raw = dot_nt(mid[r], pieces[...])
         raw = raw + (pltpu.roll(raw, 128 - EXPERTS, 1) + pltpu.roll(raw, 128 - 2 * EXPERTS, 1))
         raw = jnp.where(lane < EXPERTS, raw, -1e30)
         raw = jnp.exp(raw - jnp.max(raw, axis=1, keepdims=True))
@@ -346,123 +370,230 @@
         own = jnp.sum(jnp.where(own_lane, probs * hot[r].astype(f32), 0.0), axis=1, keepdims=True)
         return own, probs
 
-    def piece(r, kind, start, size, own):
-        pair, down = (pair_s, down_s) if kind == "s" else (pair_e, down_e)
-        span = SHARED_TILE if kind == "s" else F
-        act_at = F if kind == "s" else 0
-        dpre_at = 2 * F if kind == "s" else 0
-        gate = dot_nn(mid[r], pair[:, start : start + size])
-        up = dot_nn(mid[r], pair[:, span + start : span + start + size])
-        dact = dot_nt(grad[r], down[start : start + size])
+    def piece(r, gate, up, dact, act_at, gate_at, up_at, own):
+        size = gate.shape[1]
         logistic = 1.0 / (1.0 + jnp.exp(-gate))
         passed = gate * logistic
         out = passed * up
         total = None
-        if kind == "e":
+        if own is not None:
             total = jnp.sum(out * dact, axis=1, keepdims=True)
             out = out * own
             dact = dact * own
-        act[r, act_at + start : act_at + start + size] = out.astype(bf16)
+        act[r, act_at : act_at + size] = out.astype(bf16)
         slope = logistic + passed * (1.0 - logistic)
-        dpre[r, dpre_at + start : dpre_at + start + size] = (dact * up * slope).astype(bf16)
-        dpre[r, dpre_at + span + start : dpre_at + span + start + size] = (dact * passed).astype(bf16)
+        dpre[r, gate_at : gate_at + size] = (dact * up * slope).astype(bf16)
+        dpre[r, up_at : up_at + size] = (dact * passed).astype(bf16)
         return total
 
     @pl.loop(0, rows // ROW_STEP)
     def _(index):
-        piece(block(index), *MLP_TILES[0], None)
+        r = row_block(index)
+        gate, up = dot_nt(mid[r], pair_s[:shared]), dot_nt(mid[r], pair_s[shared:])
+        piece(r, gate, up, dot_nt(grad[r], down_s[...]), F, 2 * F, 2 * F + PAD, None)
 
     loads[4].wait()
     loads[5].wait()
 
     @pl.loop(0, rows // ROW_STEP)
     def _(index):
-        r = block(index)
+        r = row_block(index)
         own, probs = gates(r)
-        total = piece(r, *MLP_TILES[1], own)
-        for tile in MLP_TILES[2:]:
-            total = total + piece(r, *tile, own)
+        total = 0.0
+        for start, end in ((0, 512), (512, 1024), (1024, F)):
+            gate, up = dot_nn(mid[r], pair_e[:, start:end]), dot_nn(mid[r], pair_e[:, F + start : F + end])
+            total = total + piece(r, gate, up, dot_nt(grad[r], down_e[start:end]), start, start, F + start, own)
         logit[r] = ((own * total) * (jnp.where(own_lane, 1.0, 0.0) - probs)).astype(bf16)
 
+    keeps = [pltpu.make_async_copy(act, act_h, keep.at[0]), pltpu.make_async_copy(dpre, dpre_h, keep.at[1])]
+    for c in keeps:
+        c.start()
+
     half = width // 2
-    count = 0
-
-    def flush(slot, at):
-        return pltpu.make_async_copy(stage.at[slot], terms_h.at[pl.ds(at[0], half), pl.ds(at[1], 512)], store.at[slot])
-
-    def tiles_of(left, right, columns, offset):
-        @pl.loop(0, columns // 512)
-        def _(index):
-            spot = pl.multiple_of(index * 512, 512)
-            for part in range(2):
-                @pl.when(index > 0)
-                def _():
-                    flush(part, (part * half, pl.multiple_of(spot + offset - 512, 512))).wait()
-                stage[part] = dot_tn(left[:, part * half : (part + 1) * half], right[:, pl.ds(spot, 512)]).astype(bf16)
-                flush(part, (part * half, pl.multiple_of(spot + offset, 512))).start()
+    slots = half // 128
+    jobs = []
+    for start in range(0, 2 * F, 512):
+        size = min(512, 2 * F - start)
+        jobs.append((mid, dpre, start, size, start, True))
+    for start in range(0, F, 512):
+        size = min(512, F - start)
+        jobs.append((grad, act, start, size, 2 * F + start, False))
+    for index, (left, right, start) in enumerate(((mid, dpre, 2 * F), (mid, dpre, 2 * F + PAD), (grad, act, F))):
+        jobs.append((left, right, start, shared, 3 * F + index * shared, False))
+
+    def flush(part, at, size):
+        return pltpu.make_async_copy(
+            stage.at[part, :, pl.ds(0, size)], terms_h.at[pl.ds(part * slots, slots), pl.ds(at, size)], store.at[part]
+        )
+
+    before = None
+    for left, right, start, size, at, by_column in jobs:
         for part in range(2):
-            flush(part, (part * half, columns - 512 + offset)).wait()
-
-    tiles_of(mid, dpre, dpre.shape[1], 0)
-    tiles_of(grad, act, act.shape[1] // 512 * 512, dpre.shape[1])
-    tail = act.shape[1] // 512 * 512
-    rest = act.shape[1] - tail
-    for part in range(2):
-        stage[part, :, :rest] = dot_tn(grad[:, part * half : (part + 1) * half], act[:, tail:]).astype(bf16)
-        last = pltpu.make_async_copy(
-            stage.at[part, :, pl.ds(0, rest)],
-            terms_h.at[pl.ds(part * half, half), pl.ds(dpre.shape[1] + tail, rest)], store.at[part])
-        last.start()
+            if before is not None:
+                flush(part, *before).wait()
+            wide = left[:, part * half : (part + 1) * half]
+            if by_column:
+                value = dot_tn(wide, right[:, start : start + size]).astype(bf16)
+                for s in range(slots):
+                    for c in range(size // 128):
+                        stage[part, s, c * 128 : (c + 1) * 128] = value[s * 128 : (s + 1) * 128, c * 128 : (c + 1) * 128]
+            else:
+                value = dot_tn(right[:, start : start + size], wide).astype(bf16)
+                for s in range(slots):
+                    stage[part, s, :size] = value[:, s * 128 : (s + 1) * 128]
+            flush(part, at, size).start()
+        before = (at, size)
     router_out[...] = dot_tn(logit[...], mid[...])[:EXPERTS]
     for part in range(2):
-        pltpu.make_async_copy(
-            stage.at[part, :, pl.ds(0, rest)],
-            terms_h.at[pl.ds(part * half, half), pl.ds(dpre.shape[1] + tail, rest)], store.at[part]).wait()
-
-    @pl.loop(0, rows // ROW_STEP)
-    def _(index):
-        r = block(index)
-        total = dot_nt(dpre[r, : 2 * F], pair_e[...]) + dot_nt(dpre[r, 2 * F :], pair_s[...])
-        mid_part[r] = (total + dot_nn(logit[r], router_turned[...])).astype(bf16)
-        moe_part[r] = (dot_nn(act[r, :F], down_e[...]) + dot_nn(act[r, F:], down_s[...])).astype(bf16)
-
-
-def mlp(mid_all, grad_all, pair_s, pair_e, down_s, down_e, router, router_turned, hot):
+        flush(part, *before).wait()
+    for c in keeps:
+        c.wait()
+
+
+def mlp(mid_all, grad_all, pair_s, pair_e, down_s, down_e, router, hot):
     rows, width = mid_all.shape
-    hidden = F + SHARED_TILE
+    shared = down_s.shape[0]
     whole = pl.BlockSpec(memory_space=VM)
     held = pl.BlockSpec(memory_space=pl.ANY)
+    act_shape, dpre_shape = (rows, F + PAD), (rows, 2 * (F + PAD))
     return pl.pallas_call(
         mlp_kernel,
         out_shape=[
-            jax.ShapeDtypeStruct((rows, width), bf16),
-            jax.ShapeDtypeStruct((rows, width), bf16),
+            jax.ShapeDtypeStruct((width // 128, 3 * (F + shared), 128), bf16),
+            jax.ShapeDtypeStruct(act_shape, bf16),
+            jax.ShapeDtypeStruct(dpre_shape, bf16),
+            jax.ShapeDtypeStruct((rows, 128), bf16),
             jax.ShapeDtypeStruct((EXPERTS, width), f32),
-            jax.ShapeDtypeStruct((width, 3 * hidden), bf16),
         ],
-        in_specs=[held] * 6 + [whole] * 3,
-        out_specs=[whole, whole, whole, held],
+        in_specs=[held] * 6 + [whole] * 2,
+        out_specs=[held, held, held, whole, whole],
         scratch_shapes=[
             pltpu.VMEM(mid_all.shape, bf16), pltpu.VMEM(grad_all.shape, bf16),
             pltpu.VMEM(pair_s.shape, bf16), pltpu.VMEM(pair_e.shape, bf16),
             pltpu.VMEM(down_s.shape, bf16), pltpu.VMEM(down_e.shape, bf16),
-            pltpu.VMEM((rows, hidden), bf16), pltpu.VMEM((rows, 2 * hidden), bf16),
-            pltpu.VMEM((rows, 128), bf16), pltpu.VMEM((2, width // 2, 512), bf16),
-            pltpu.SemaphoreType.DMA((6,)), pltpu.SemaphoreType.DMA((2,)),
+            pltpu.VMEM(act_shape, bf16), pltpu.VMEM(dpre_shape, bf16),
+            pltpu.VMEM((128, width), bf16), pltpu.VMEM((2, width // 256, 512, 128), bf16),
+            pltpu.SemaphoreType.DMA((6,)), pltpu.SemaphoreType.DMA((2,)), pltpu.SemaphoreType.DMA((2,)),
         ],
-        compiler_params=pltpu.CompilerParams(vmem_limit_bytes=63 << 20),
-        cost_estimate=pl.CostEstimate(flops=18 * rows * width * hidden, bytes_accessed=60 << 20, transcendentals=rows * hidden),
+        compiler_params=pltpu.CompilerParams(vmem_limit_bytes=62 << 20),
+        cost_estimate=pl.CostEstimate(flops=12 * rows * width * (F + shared), bytes_accessed=60 << 20, transcendentals=rows * F),
         name="mlp",
-    )(mid_all, grad_all, pair_s, pair_e, down_s, down_e, router, router_turned, hot)
-
-
+    )(mid_all, grad_all, pair_s, pair_e, down_s, down_e, router, hot)
+
+
+def turn_kernel(
+    dpre_h, act_h, pair_s_h, pair_e_h, down_s_h, down_e_h, logit, router, residual, gain, upstream,
+    residual_grad, gain_term, grad_all, moe_part,
+    dpre, act, pair_s, pair_e, down_s, down_e, part, pieces, own_grad, p0, p1, p2, load, send, recv, local,
+):
+    at = Place()
+    sems = Sems(send, recv)
+    rows = residual.shape[0]
+    half = rows // 2
+    shared = down_s.shape[0]
+    sources = [
+        (dpre_h, dpre), (pair_e_h.at[:, pl.ds(0, F)], pair_e.at[:, pl.ds(0, F)]),
+        (pair_e_h.at[:, pl.ds(F, F)], pair_e.at[:, pl.ds(F, F)]), (pair_s_h, pair_s),
+        (act_h, act), (down_e_h, down_e), (down_s_h, down_s),
+    ]
+    loads = [pltpu.make_async_copy(src, dst, load.at[i]) for i, (src, dst) in enumerate(sources)]
+    for c in loads:
+        c.start()
+    greet([at.hop(0, 1), at.hop(0, 3), at.sibling])
+    gain_term[...] = jnp.zeros_like(gain_term)
+    pieces[...] = router_pieces(router[...])
+    loads[0].wait()
+
+    def ready(dist):
+        r = row_block(lax.rem(at.chip + dist, 4))
+        if dist == 2:
+            loads[1].wait()
+        total = dot_nt(dpre[r, :F], pair_e[:, :F])
+        if dist == 2:
+            loads[2].wait()
+        total = total + dot_nt(dpre[r, F : 2 * F], pair_e[:, F:])
+        if dist == 2:
+            loads[3].wait()
+        total = total + dot_nn(dpre[r, 2 * F : 2 * F + shared], pair_s[:shared])
+        total = total + dot_nn(dpre[r, 2 * F + PAD : 2 * F + PAD + shared], pair_s[shared:])
+        part[r] = (total + dot_nn(logit[r], pieces[...])).astype(bf16)
+
+    def done(h, total):
+        r = slice(h * half, (h + 1) * half)
+        x = residual[r]
+        inverse = lax.rsqrt(jnp.mean(x * x, axis=1, keepdims=True) + EPSILON)
+        gain_term[...] += jnp.sum(total * x * inverse, axis=0, keepdims=True)
+        s = total * gain[...]
+        inner = jnp.mean(s * x, axis=1, keepdims=True)
+        grad = upstream[r].astype(f32) + (inverse * s - x * (inverse * inverse * inverse) * inner)
+        residual_grad[r] = grad
+        own_grad[r] = grad.astype(bf16)
+
+    def moe(index):
+        r = pl.ds(index * ROW_STEP, ROW_STEP)
+        moe_part[r] = (dot_nn(act[r, :F], down_e[...]) + dot_nn(act[r, F : F + shared], down_s[...])).astype(bf16)
+
+    together(scatter_stream(sems, at, part, p0, p1, p2, rows, done, ready))
+    for c in loads[4:]:
+        c.wait()
+    gathered = gather_stream(sems, at, own_grad, grad_all, rows, local)
+    next(gathered)
+    for index in range(4):
+        moe(index)
+        next(gathered, None)
+    together(gathered)
+    sems.finish()
+
+
+def turn(dpre, act, pair_s, pair_e, down_s, down_e, logit, router, residual, gain, upstream):
+    whole = pl.BlockSpec(memory_space=VM)
+    held = pl.BlockSpec(memory_space=pl.ANY)
+    rows, width = residual.shape
+    return pl.pallas_call(
+        turn_kernel,
+        out_shape=[
+            jax.ShapeDtypeStruct((rows, width), f32),
+            jax.ShapeDtypeStruct((1, width), f32),
+            jax.ShapeDtypeStruct((8 * rows, width), bf16),
+            jax.ShapeDtypeStruct((8 * rows, width), bf16),
+        ],
+        in_specs=[held] * 6 + [whole] * 5,
+        out_specs=[whole] * 4,
+        scratch_shapes=[
+            pltpu.VMEM(dpre.shape, bf16), pltpu.VMEM(act.shape, bf16),
+            pltpu.VMEM(pair_s.shape, bf16), pltpu.VMEM(pair_e.shape, bf16),
+            pltpu.VMEM(down_s.shape, bf16), pltpu.VMEM(down_e.shape, bf16),
+            pltpu.VMEM((8 * rows, width), bf16),
+            pltpu.VMEM((128, width), bf16),
+            pltpu.VMEM((rows, width), bf16),
+            *scatter_scratch(rows, width),
+            pltpu.SemaphoreType.DMA((7,)),
+            pltpu.SemaphoreType.DMA((23,)),
+            pltpu.SemaphoreType.DMA((23,)),
+            pltpu.SemaphoreType.DMA,
+        ],
+        compiler_params=pltpu.CompilerParams(collective_id=2, has_side_effects=True, vmem_limit_bytes=62 << 20),
+        name="turn",
+    )(dpre, act, pair_s, pair_e, down_s, down_e, logit, router, residual, gain, upstream)
+
+
+SPAN = LAT + 2 * ROPE
 ATT = 256
 SCALE = (NOPE + ROPE) ** (-0.5)
 LOG2E = 1.4426950408889634
 
 
-def score_pieces(q, packed, ropes, qseg, kseg, head, i):
-    rows = pl.ds(ATT * i, ATT)
+def segments(segs, count):
+    spot = lax.axis_index("seq")
+    own = segs[:, pl.ds(pl.multiple_of(spot * count, count), count)].astype(f32)
+    before = segs[:, pl.ds(pl.multiple_of(jnp.maximum(spot - 1, 0) * count, count), count)].astype(f32)
+    before = jnp.where(lax.rem(spot, 2) == 1, before, -1.0)
+    column = jnp.transpose(jnp.broadcast_to(own, (128, count)))[:, :1]
+    return column, jnp.concatenate([before, own], axis=1)
+
+
+def score_pieces(q, packed, keys_all, qseg, kseg, head, i):
+    rows = slice(ATT * i, ATT * (i + 1))
     prev = packed.shape[0] - q.shape[0]
     lane = lax.broadcasted_iota(jnp.int32, (ATT, 2 * ROPE), 1)
     rope = jnp.where(lane // ROPE == head, q[rows, 2 * NOPE :], jnp.zeros((), bf16))
@@ -471,7 +602,7 @@
     pieces = []
     for start, end in ((0, edge), (edge, edge + ATT)):
         keys = jnp.concatenate(
-            [packed[start:end, head * 2 * NOPE : head * 2 * NOPE + NOPE], ropes[start:end]], axis=1
+            [packed[start:end, head * 2 * NOPE : head * 2 * NOPE + NOPE], keys_all[start:end, LAT:]], axis=1
         )
         scores = dot_nt(query, keys)
         allowed = qseg[rows] == kseg[:, start:end]
@@ -484,11 +615,12 @@
     return query, pieces
 
 
-def attend_kernel(q, packed, ropes, qseg, kseg, heads, lse):
+def attend_kernel(q, packed, keys_all, segs, heads, lse):
+    qseg, kseg = segments(segs, q.shape[0])
     for head in range(2):
         for i in range(q.shape[0] // ATT):
             rows = pl.ds(ATT * i, ATT)
-            _, pieces = score_pieces(q, packed, ropes, qseg, kseg, head, i)
+            _, pieces = score_pieces(q, packed, keys_all, qseg, kseg, head, i)
             top = jnp.maximum(*[jnp.max(scores, axis=1, keepdims=True) for _, _, scores, _ in pieces])
             total, out = 0.0, 0.0
             for start, end, scores, _ in pieces:
@@ -500,23 +632,43 @@
             lse[head, rows] = top * (SCALE * LOG2E) + jnp.log2(total)
 
 
-def attend(q, packed, ropes, qseg, kseg):
+def attend(q, packed, keys_all, segs):
     whole = pl.BlockSpec(memory_space=VM)
     rows = q.shape[0]
     return pl.pallas_call(
         attend_kernel,
         out_shape=[jax.ShapeDtypeStruct((rows, 2 * VDIM), bf16), jax.ShapeDtypeStruct((2, rows, 1), f32)],
-        in_specs=[whole] * 5,
+        in_specs=[whole] * 4,
         out_specs=[whole] * 2,
         compiler_params=pltpu.CompilerParams(vmem_limit_bytes=56 << 20),
         name="attend",
-    )(q, packed, ropes, qseg, kseg)
+    )(q, packed, keys_all, segs)
 
 
 def attend_back_kernel(
-    grad, wo, heads, q, packed, ropes, qseg, kseg, lse, cosine, sine, kv_proj, latents,
-    dq, key_grad, kvo, head_grad, dkey, dvalue, drope, dpacked,
+    grad, wo, heads, q, packed, keys_all, segs, lse, kv_proj, moe_part, residual, cosine_h, sine_h,
+    dq, key_grad, kvo, layer_out,
+    head_grad, dkey, dvalue, drope, dpacked, nope, rope_sum, cosine, sine, p0, p1, p2, send, recv, local,
 ):
+    at = Place()
+    sems = Sems(send, recv)
+    block = pl.ds(pl.multiple_of(lax.rem(at.y, 2) * q.shape[0], q.shape[0]), q.shape[0])
+    loads = [
+        pltpu.make_async_copy(cosine_h.at[block], cosine, local.at[0]),
+        pltpu.make_async_copy(sine_h.at[block], sine, local.at[1]),
+    ]
+    for c in loads:
+        c.start()
+    greet([at.hop(0, 1), at.hop(0, 3), at.sibling])
+    own_rows = residual.shape[0]
+
+    def done(h, total):
+        r = slice(h * (own_rows // 2), (h + 1) * (own_rows // 2))
+        layer_out[r] = (residual[r] + total).astype(bf16)
+
+    moe = scatter_stream(sems, at, moe_part, p0, p1, p2, own_rows, done)
+    next(moe)
+    qseg, kseg = segments(segs, q.shape[0])
     rows = q.shape[0]
     prev = packed.shape[0] - rows
     step = 256
@@ -528,7 +680,7 @@
         dvalue[...] = jnp.zeros_like(dvalue)
         for i in range(rows // ATT):
             r = pl.ds(ATT * i, ATT)
-            query, pieces = score_pieces(q, packed, ropes, qseg, kseg, head, i)
+            query, pieces = score_pieces(q, packed, keys_all, qseg, kseg, head, i)
             upstream = head_grad[r, head * VDIM : (head + 1) * VDIM]
             probs, dprobs = [], []
             inner = 0.0
@@ -545,21 +697,29 @@
                 dkey[start:end] += dot_tn(ds, query)
                 dvalue[start:end] += dot_tn(p.astype(bf16), upstream)
             dquery = dquery * SCALE
-            dq[r, head * NOPE : (head + 1) * NOPE] = dquery[:, :NOPE].astype(bf16)
+            nope[head, r] = dquery[:, :NOPE]
             rope = dquery[:, NOPE:]
-            rope = rope * cosine[r] - swapped(rope) * sine[r]
             lane = lax.broadcasted_iota(jnp.int32, rope.shape, 1)
             if head == 0:
-                dq[r, 2 * NOPE :] = rope.astype(bf16)
+                rope_sum[r] = rope
             else:
-                dq[r, 2 * NOPE :] = jnp.where(lane < ROPE, dq[r, 2 * NOPE :], rope.astype(bf16))
+                rope = jnp.where(lane < ROPE, rope_sum[r], rope)
+                if i == 0:
+                    for c in loads:
+                        c.wait()
+                rope = rope * cosine[r] - swapped(rope) * sine[r]
+                turned = pltpu.roll(nope[1, r], ROPE, 1)
+                dq[r, :NOPE] = nope[0, r].astype(bf16)
+                dq[r, NOPE : 2 * NOPE] = jnp.where(lane < ROPE, rope, turned).astype(bf16)
+                dq[r, 2 * NOPE :] = jnp.where(lane < ROPE, turned, rope).astype(bf16)
+            next(moe, None)
         dpacked[:, head * 2 * NOPE : head * 2 * NOPE + NOPE] = (dkey[:, :NOPE] * SCALE).astype(bf16)
         dpacked[:, head * 2 * NOPE + NOPE : (head + 1) * 2 * NOPE] = dvalue[...].astype(bf16)
         if head == 0:
             drope[...] = dkey[:, NOPE:]
         else:
             drope[...] += dkey[:, NOPE:]
-    span = LAT + 2 * ROPE
+    span = SPAN
     for i in range(packed.shape[0] // 512):
         r = pl.ds(512 * i, 512)
         at = span if i * 512 < prev else 0
@@ -568,49 +728,59 @@
         rope = drope[r]
         key_grad[to, at + LAT : at + span] = ((rope + pltpu.roll(rope, ROPE, 1)) * SCALE).astype(bf16)
     spots, wide = kvo.shape[0], kvo.shape[2]
-    kv = dot_tn(latents[...], dpacked[...]).astype(bf16)
+    kv = dot_tn(keys_all[:, :LAT], dpacked[...]).astype(bf16)
     kv_rows = kv.shape[0] // spots
     kvo[:, :kv_rows] = kv.reshape(spots, kv_rows, wide)
     out_rows = wo.shape[0] // spots
     for j in range(grad.shape[1] // wide):
         term = dot_tn(heads[...], grad[:, j * wide : (j + 1) * wide]).astype(bf16)
         kvo[:, kv_rows + j * out_rows : kv_rows + (j + 1) * out_rows] = term.reshape(spots, out_rows, wide)
-
-
-def attend_back(grad, wo, heads, q, packed, ropes, qseg, kseg, lse, cosine, sine, kv_proj, latents):
+    together(moe)
+    sems.finish()
+
+
+def attend_back(grad, wo, heads, q, packed, keys_all, segs, lse, kv_proj, moe_part, residual, cosine, sine):
     whole = pl.BlockSpec(memory_space=VM)
+    held = pl.BlockSpec(memory_space=pl.ANY)
     rows, keys = q.shape[0], packed.shape[0]
+    own_rows, width = residual.shape
     spots = lax.axis_size("seq")
     kvo_rows = (kv_proj.shape[0] * kv_proj.shape[1] + wo.shape[0] * wo.shape[1]) // spots // LAT
     return pl.pallas_call(
         attend_back_kernel,
         out_shape=[
             jax.ShapeDtypeStruct(q.shape, bf16),
-            jax.ShapeDtypeStruct((rows, 2 * (LAT + 2 * ROPE)), bf16),
+            jax.ShapeDtypeStruct((rows, 2 * SPAN), bf16),
             jax.ShapeDtypeStruct((spots, kvo_rows, LAT), bf16),
+            jax.ShapeDtypeStruct((own_rows, width), bf16),
         ],
-        in_specs=[whole] * 13,
-        out_specs=[whole] * 3,
+        in_specs=[whole] * 11 + [held] * 2,
+        out_specs=[whole] * 4,
         scratch_shapes=[
             pltpu.VMEM((rows, 2 * VDIM), bf16),
             pltpu.VMEM((keys, 2 * NOPE), f32),
             pltpu.VMEM((keys, VDIM), f32),
             pltpu.VMEM((keys, 2 * ROPE), f32),
             pltpu.VMEM(packed.shape, bf16),
+            pltpu.VMEM((2, rows, NOPE), f32),
+            pltpu.VMEM((rows, 2 * ROPE), f32),
+            pltpu.VMEM((rows, 2 * ROPE), f32),
+            pltpu.VMEM((rows, 2 * ROPE), f32),
+            *scatter_scratch(own_rows, width),
+            pltpu.SemaphoreType.DMA((10,)),
+            pltpu.SemaphoreType.DMA((10,)),
+            pltpu.SemaphoreType.DMA((2,)),
         ],
-        compiler_params=pltpu.CompilerParams(vmem_limit_bytes=56 << 20),
+        compiler_params=pltpu.CompilerParams(collective_id=4, has_side_effects=True, vmem_limit_bytes=60 << 20),
         name="attend_back",
-    )(grad, wo, heads, q, packed, ropes, qseg, kseg, lse, cosine, sine, kv_proj, latents)
-
-
-SPAN = LAT + 2 * ROPE
+    )(grad, wo, heads, q, packed, keys_all, segs, lse, kv_proj, moe_part, residual, cosine, sine)
 
 
 def tail_kernel(
-    dq, key_grad, kvo, normed, wq, wl, raw, latent_gain, cosine, sine, gain, upstream, rows_in, small_in,
+    dq, key_grad, kvo, normed, wq, wl, raw, latent_gain, gain, upstream, rows_in, router_in, ffn_in, cosine_h, sine_h,
     query_out, kvo_out, latent_out, grad_out, small_out,
     work0, work1, key_sum, in_part, in_sum, in_own, lat_rows, lat_all, lat_work, lat_sum, prev_out, prev_in, small,
-    r0, r1, r2, r3, s0, s1, s2, s3, k0, k1, k2, n0, n1, n2, lw, ln, send, recv, local,
+    r0, r1, r2, r3, s0, s1, s2, s3, k0, k1, k2, n0, n1, n2, lw, ln, cosine, sine, send, recv, local,
 ):
     at = Place()
     sems = Sems(send, recv)
@@ -625,6 +795,13 @@
     def keep_in(h, total):
         in_sum[h * half : (h + 1) * half] = total
 
+    spot = pl.multiple_of(lax.rem(at.y, 2) * 8 * rows + at.me * rows, rows)
+    loads = [
+        pltpu.make_async_copy(cosine_h.at[pl.ds(spot, rows)], cosine, local.at[2]),
+        pltpu.make_async_copy(sine_h.at[pl.ds(spot, rows)], sine, local.at[3]),
+    ]
+    for c in loads:
+        c.start()
     keys = scatter_stream(sems, at, key_grad, k0, k1, k2, rows, keep_key)
     next(keys)
     work0[...] = dot_tn(normed[...], dq[...]).astype(bf16).reshape(work0.shape)
@@ -662,15 +839,19 @@
         inner = jnp.mean(s * x, axis=1, keepdims=True)
         lat_rows[:, :LAT] = (inverse * s - x * (inverse * inverse * inverse) * inner).astype(bf16)
         rope = own_grad[:, LAT:]
+        for c in loads:
+            c.wait()
         rope = rope * cosine[...] - swapped(rope) * sine[...]
         lane = lax.broadcasted_iota(jnp.int32, rope.shape, 1)
         lat_rows[:, LAT:] = jnp.where(lane < ROPE, rope, 0.0).astype(bf16)
         gathered = gather_stream(sems, at, lat_rows, lat_all, rows, local.at[0])
         next(gathered)
-        in_own[...] = dot_nt(lat_rows[...], wl[...])
+        in_own[...] = dot_nn(lat_rows[:, : LAT + ROPE], wl[...])
         attn_gain = gain_part + jnp.sum(in_own[...] * normed[own].astype(f32), axis=0, keepdims=True)
-        small[0, at.core] = small_in[...]
+        small[0, at.core, :EXPERTS] = router_in[...]
+        small[0, at.core, EXPERTS:] = jnp.zeros_like(router_in)
         small[0, at.core, EXPERTS : EXPERTS + 1] = attn_gain / gain[...]
+        small[0, at.core, EXPERTS + 1 : EXPERTS + 2] = ffn_in[...]
         small[0, at.core, EXPERTS + 2 : EXPERTS + 3, :LAT] = lat_gain_part
         running.append(small_stream(sems, at, small, small_out))
         yield from gathered
@@ -696,7 +877,7 @@
     sems.finish()
 
 
-def tail(dq, key_grad, kvo, normed, wq, wl, raw, latent_gain, cosine, sine, gain, upstream, rows_in, small_in):
+def tail(dq, key_grad, kvo, normed, wq, wl, raw, latent_gain, gain, upstream, rows_in, router_in, ffn_in, cosine, sine):
     whole = pl.BlockSpec(memory_space=VM)
     rows, width = rows_in.shape
     spots = kvo.shape[0]
@@ -710,9 +891,9 @@
             jax.ShapeDtypeStruct(kvo.shape, bf16),
             jax.ShapeDtypeStruct((8 * spots, slice_rows, SPAN), bf16),
             jax.ShapeDtypeStruct((rows, width), bf16),
-            jax.ShapeDtypeStruct(small_in.shape, f32),
+            jax.ShapeDtypeStruct((2 * EXPERTS, width), f32),
         ],
-        in_specs=[whole] * 14,
+        in_specs=[whole] * 13 + [pl.BlockSpec(memory_space=pl.ANY)] * 2,
         out_specs=[whole] * 5,
         scratch_shapes=[
             pltpu.VMEM(query_shape, bf16),
@@ -727,74 +908,97 @@
             pltpu.VMEM(lat_shape, bf16),
             pltpu.VMEM((rows, SPAN), bf16),
             pltpu.VMEM((rows, SPAN), bf16),
-            pltpu.VMEM((4, 4) + small_in.shape, f32),
+            pltpu.VMEM((4, 4, 2 * EXPERTS, width), f32),
             *seq_scratch(*query_shape[1:]),
             *seq_scratch(*kvo.shape[1:]),
             *scatter_scratch(rows, 2 * SPAN),
             *scatter_scratch(rows, width),
             pltpu.VMEM((3, 4, slice_rows, SPAN), bf16),
             pltpu.VMEM((3, slice_rows, SPAN), bf16),
+            pltpu.VMEM((rows, 2 * ROPE), f32),
+            pltpu.VMEM((rows, 2 * ROPE), f32),
             pltpu.SemaphoreType.DMA((120,)),
             pltpu.SemaphoreType.DMA((120,)),
-            pltpu.SemaphoreType.DMA((2,)),
+            pltpu.SemaphoreType.DMA((4,)),
         ],
         compiler_params=pltpu.CompilerParams(collective_id=3, has_side_effects=True, vmem_limit_bytes=60 << 20),
         name="tail",
-    )(dq, key_grad, kvo, normed, wq, wl, raw, latent_gain, cosine, sine, gain, upstream, rows_in, small_in)
+    )(dq, key_grad, kvo, normed, wq, wl, raw, latent_gain, gain, upstream, rows_in, router_in, ffn_in, cosine, sine)
 
 
 def start_kernel(
-    rows_in, gain, wl, latent_gain, wq, kv_proj, cosine, sine, own_cosine, own_sine, hot,
+    rows_in, gain, wl, latent_gain, wq, kv_proj, routes, cosine_h, sine_h,
     normed, q, packed, keys, hot_all, raw,
-    own_normed, ext, ext_all, prev_out, send, recv, local,
+    own_normed, ext, ext_all, prev_out, cosine, sine, send, recv, local,
 ):
     at = Place()
     sems = Sems(send, recv)
+    rows = rows_in.shape[0]
+    block = 8 * rows
+    half_seq = pl.ds(pl.multiple_of(lax.rem(at.y, 2) * block, block), block)
+    loads = [
+        pltpu.make_async_copy(cosine_h.at[half_seq], cosine, local.at[2]),
+        pltpu.make_async_copy(sine_h.at[half_seq], sine, local.at[3]),
+    ]
+    for c in loads:
+        c.start()
+    x = rows_in[...].astype(f32)
+    own_normed[...] = (x * lax.rsqrt(jnp.mean(x * x, axis=1, keepdims=True) + EPSILON) * gain[...]).astype(bf16)
     partner = at.across[1](at.y + 1 - 2 * lax.rem(at.y, 2))
     greet([at.hop(0, 1), at.hop(0, 3), at.sibling, partner])
-    rows = rows_in.shape[0]
-    x = rows_in[...].astype(f32)
-    own_normed[...] = (x * lax.rsqrt(jnp.mean(x * x, axis=1, keepdims=True) + EPSILON) * gain[...]).astype(bf16)
     big = gather_stream(sems, at, own_normed, normed, rows, local.at[0])
     next(big)
-    lat = dot_nn(own_normed[...], wl[...])
+    lat = dot_nt(own_normed[...], wl[...])
     raw[...] = lat[:, :LAT]
     x = lat[:, :LAT]
     x = x * lax.rsqrt(jnp.mean(x * x, axis=1, keepdims=True) + EPSILON) * latent_gain[...]
-    rope = lat[:, LAT:]
-    rope = rope * own_cosine[...] + swapped(rope) * own_sine[...]
-    rope = rope + pltpu.roll(rope, ROPE, 1)
+    rope = jnp.concatenate([lat[:, LAT:], lat[:, LAT:]], axis=1)
+    for c in loads:
+        c.wait()
+    own = pl.ds(pl.multiple_of(at.me * rows, rows), rows)
+    rope = rope * cosine[own] + swapped(rope) * sine[own]
+    number = lax.broadcasted_iota(jnp.int32, (128, rows), 0)
+    hot = jnp.zeros((128, rows), f32)
+    for k in range(routes.shape[0]):
+        hot = hot + jnp.where(number == routes[k : k + 1], 1.0, 0.0)
+    hot = pltpu.roll(jnp.transpose(hot), ROPE, 1)
+    lane = lax.broadcasted_iota(jnp.int32, rope.shape, 1)
     prev_out[:, :LAT] = x.astype(bf16)
-    prev_out[:, LAT:] = rope.astype(bf16)
+    prev_out[:, LAT:] = jnp.where(lane < ROPE, rope, hot).astype(bf16)
     swap = sems.start(prev_out, ext.at[:, pl.ds(SPAN, SPAN)], partner)
     ext[:, :SPAN] = prev_out[...]
-    ext[:, 2 * SPAN :] = hot[...]
     next(big)
     swap.wait_recv()
     little = gather_stream(sems, at, ext, ext_all, rows, local.at[1])
     next(little)
     together(big, little)
-    block = normed.shape[0]
     step = 256
+    lane = lax.broadcasted_iota(jnp.int32, (step, 2 * ROPE), 1)
     for i in range(block // step):
         r = pl.ds(i * step, step)
         query = dot_nn(normed[r], wq[...])
-        q[r, : 2 * NOPE] = query[:, : 2 * NOPE].astype(bf16)
-        rope = query[:, 2 * NOPE :]
+        q[r, :NOPE] = query[:, :NOPE].astype(bf16)
+        one, two = query[:, NOPE : 2 * NOPE], query[:, 2 * NOPE :]
+        q[r, NOPE : 2 * NOPE] = jnp.where(lane < ROPE, pltpu.roll(one, ROPE, 1), pltpu.roll(two, ROPE, 1)).astype(bf16)
+        rope = jnp.where(lane < ROPE, one, two)
         q[r, 2 * NOPE :] = (rope * cosine[r] + swapped(rope) * sine[r]).astype(bf16)
     for part in range(2):
         r = slice((1 - part) * block, (2 - part) * block)
-        keys[r] = ext_all[:, part * SPAN : (part + 1) * SPAN]
+        keys[r, :LAT] = ext_all[:, part * SPAN : part * SPAN + LAT]
+        rope = ext_all[:, part * SPAN + LAT : (part + 1) * SPAN].astype(f32)
+        turned = pltpu.roll(rope, ROPE, 1)
+        if part == 0:
+            hot_all[...] = turned.astype(bf16)
+        wide_lane = lax.broadcasted_iota(jnp.int32, rope.shape, 1)
+        keys[r, LAT:] = jnp.where(wide_lane < ROPE, rope, turned).astype(bf16)
         packed[r] = dot_nn(ext_all[:, part * SPAN : part * SPAN + LAT], kv_proj[...]).astype(bf16)
-    hot_all[...] = ext_all[:, 2 * SPAN :]
     sems.finish()
 
 
-def start(rows_in, gain, wl, latent_gain, wq, kv_proj, cosine, sine, own_cosine, own_sine, hot):
+def start(rows_in, gain, wl, latent_gain, wq, kv_proj, routes, cosine, sine):
     whole = pl.BlockSpec(memory_space=VM)
     rows, width = rows_in.shape
     block = 8 * rows
-    ext_width = 2 * SPAN + hot.shape[1]
     return pl.pallas_call(
         start_kernel,
         out_shape=[
@@ -802,23 +1006,25 @@
             jax.ShapeDtypeStruct((block, wq.shape[1]), bf16),
             jax.ShapeDtypeStruct((2 * block, kv_proj.shape[1]), bf16),
             jax.ShapeDtypeStruct((2 * block, SPAN), bf16),
-            jax.ShapeDtypeStruct((block, hot.shape[1]), bf16),
+            jax.ShapeDtypeStruct((block, 2 * ROPE), bf16),
             jax.ShapeDtypeStruct((rows, LAT), f32),
         ],
-        in_specs=[whole] * 11,
+        in_specs=[whole] * 7 + [pl.BlockSpec(memory_space=pl.ANY)] * 2,
         out_specs=[whole] * 6,
         scratch_shapes=[
             pltpu.VMEM((rows, width), bf16),
-            pltpu.VMEM((rows, ext_width), bf16),
-            pltpu.VMEM((block, ext_width), bf16),
+            pltpu.VMEM((rows, 2 * SPAN), bf16),
+            pltpu.VMEM((block, 2 * SPAN), bf16),
             pltpu.VMEM((rows, SPAN), bf16),
+            pltpu.VMEM((block, 2 * ROPE), f32),
+            pltpu.VMEM((block, 2 * ROPE), f32),
             pltpu.SemaphoreType.DMA((27,)),
             pltpu.SemaphoreType.DMA((27,)),
-            pltpu.SemaphoreType.DMA((2,)),
+            pltpu.SemaphoreType.DMA((4,)),
         ],
         compiler_params=pltpu.CompilerParams(collective_id=0, has_side_effects=True, vmem_limit_bytes=56 << 20),
         name="start",
-    )(rows_in, gain, wl, latent_gain, wq, kv_proj, cosine, sine, own_cosine, own_sine, hot)
+    )(rows_in, gain, wl, latent_gain, wq, kv_proj, routes, cosine, sine)
 
 
 def middle_kernel(
@@ -866,63 +1072,51 @@
     )(heads, wo, rows_in, gain)
 
 
-def turn_kernel(
-    part, residual, gain, upstream, residual_grad, gain_term, grad_all, own_grad, p0, p1, p2, send, recv, local
-):
-    at = Place()
-    sems = Sems(send, recv)
-    rows = residual.shape[0]
-    half = rows // 2
-    greet([at.hop(0, 1), at.hop(0, 3), at.sibling])
-    gain_term[...] = jnp.zeros_like(gain_term)
-
-    def done(h, total):
-        r = slice(h * half, (h + 1) * half)
-        x = residual[r]
-        inverse = lax.rsqrt(jnp.mean(x * x, axis=1, keepdims=True) + EPSILON)
-        gain_term[...] += jnp.sum(total * x * inverse, axis=0, keepdims=True)
-        s = total * gain[...]
-        inner = jnp.mean(s * x, axis=1, keepdims=True)
-        grad = upstream[r].astype(f32) + (inverse * s - x * (inverse * inverse * inverse) * inner)
-        residual_grad[r] = grad
-        own_grad[r] = grad.astype(bf16)
-
-    together(scatter_stream(sems, at, part, p0, p1, p2, rows, done))
-    together(gather_stream(sems, at, own_grad, grad_all, rows, local))
-    sems.finish()
-
-
-def turn(part, residual, gain, upstream):
+def finish_kernel(weights, query, kvo, latent, expert_gate, expert_down, shared_gate, shared_down, query_out, kv_out, out_out, latent_out):
+    for c in range(expert_gate.shape[1] // 128):
+        expert_gate[:, c * 128 : (c + 1) * 128] = weights[c * 128 : (c + 1) * 128].astype(f32)
+    spot = expert_gate.shape[1]
+    for ref in (expert_down, shared_gate, shared_down):
+        ref[...] = weights[spot : spot + ref.shape[0]].astype(f32)
+        spot += ref.shape[0]
+    query_out[...] = query[...].reshape(query_out.shape).astype(f32)
+    spots, _, wide = kvo.shape
+    kv_rows = kv_out.shape[0] // spots
+    kv_out[...] = kvo[:, :kv_rows].reshape(kv_out.shape).astype(f32)
+    out_rows = out_out.shape[0] // spots
+    for j in range(out_out.shape[1] // wide):
+        piece = kvo[:, kv_rows + j * out_rows : kv_rows + (j + 1) * out_rows]
+        out_out[:, j * wide : (j + 1) * wide] = piece.reshape(out_out.shape[0], wide).astype(f32)
+    step = 512
+    for i in range(latent_out.shape[1] // step):
+        spot = step // latent.shape[1]
+        rows = latent[i * spot : (i + 1) * spot].reshape(step, latent.shape[2]).astype(f32)
+        latent_out[:, i * step : (i + 1) * step] = jnp.transpose(rows)[: latent_out.shape[0]]
+
+
+def finish(weights, query, kvo, latent, shared, model_width, kv_shape, out_shape):
     whole = pl.BlockSpec(memory_space=VM)
-    rows, width = residual.shape
+    shapes = [
+        (128, 2 * F), (F, 128), (2 * shared, 128), (shared, 128),
+        (model_width, query.shape[2]), kv_shape, out_shape, (LAT + ROPE, model_width),
+    ]
     return pl.pallas_call(
-        turn_kernel,
-        out_shape=[
-            jax.ShapeDtypeStruct((rows, width), f32),
-            jax.ShapeDtypeStruct((1, width), f32),
-            jax.ShapeDtypeStruct((8 * rows, width), bf16),
-        ],
+        finish_kernel,
+        out_shape=[jax.ShapeDtypeStruct(shape, f32) for shape in shapes],
         in_specs=[whole] * 4,
-        out_specs=[whole] * 3,
-        scratch_shapes=[
-            pltpu.VMEM((rows, width), bf16),
-            *scatter_scratch(rows, width),
-            pltpu.SemaphoreType.DMA((23,)),
-            pltpu.SemaphoreType.DMA((23,)),
-            pltpu.SemaphoreType.DMA,
-        ],
-        compiler_params=pltpu.CompilerParams(collective_id=2, has_side_effects=True, vmem_limit_bytes=56 << 20),
-        name="turn",
-    )(part, residual, gain, upstream)
-
-
-def tables(position):
-    lane = jnp.arange(2 * ROPE, dtype=jnp.int32)
+        out_specs=[whole] * 8,
+        compiler_params=pltpu.CompilerParams(vmem_limit_bytes=56 << 20),
+        name="finish",
+    )(weights, query, kvo, latent)
+
+
+def tables(seq_rows):
+    lane = np.arange(2 * ROPE)
     half = ROPE // 2
-    frequency = jnp.exp((lane % half).astype(f32) * (-math.log(10000.0) / half))
-    angles = position.astype(f32)[:, None] * frequency[None, :]
-    sign = jnp.where(lane % ROPE < half, -1.0, 1.0)
-    return jnp.cos(angles), jnp.sin(angles) * sign[None, :]
+    frequency = np.exp((lane % half) * (-math.log(10000.0) / half))
+    angles = np.arange(seq_rows)[:, None] * frequency[None, :]
+    sign = np.where(lane % ROPE < half, -1.0, 1.0)
+    return np.cos(angles).astype(np.float32), (np.sin(angles) * sign[None, :]).astype(np.float32)
 
 
 def local(
@@ -930,115 +1124,53 @@
     shared_gate_up, shared_down, expert_gate_up, expert_down, segment_ids, expert_routes, out_grad,
 ):
     own_rows, model_width = layer_input.shape
-    block_rows = own_rows * lax.axis_size("exp")
-    seq_rows = 2 * block_rows
-    block_start = lax.axis_index("seq") * block_rows
-    row_offset = lax.axis_index("exp") * own_rows
-    query_pos = block_start + jnp.arange(block_rows, dtype=jnp.int32)
-    query_seg = lax.dynamic_slice_in_dim(segment_ids, block_start, block_rows)
-    key_start = block_start - block_rows
-    prev_seg = lax.dynamic_slice_in_dim(segment_ids, jnp.maximum(key_start, 0), block_rows)
-    prev_seg = jnp.where(key_start >= 0, prev_seg, -1)
-    key_seg = jnp.concatenate([prev_seg, query_seg], axis=0)
-    cosine, sine = tables(query_pos % seq_rows)
-    own_cosine = lax.dynamic_slice_in_dim(cosine, row_offset, own_rows)
-    own_sine = lax.dynamic_slice_in_dim(sine, row_offset, own_rows)
-    head = NOPE + ROPE
-    wq = jnp.concatenate(
-        [
-            query_proj[:, :NOPE],
-            query_proj[:, head : head + NOPE],
-            query_proj[:, NOPE:head],
-            query_proj[:, head + NOPE :],
-        ],
-        axis=1,
+    cosine, sine = tables(2 * own_rows * lax.axis_size("exp"))
+    wl = latent_proj.T
+    router = router_proj.T
+    shared = shared_down.shape[0]
+    pair_s = shared_gate_up.transpose(1, 2, 0).reshape(2 * shared, model_width)
+    pair_e, down_e = expert_gate_up[0], expert_down[0]
+    segs = segment_ids[None]
+    attn_row, latent_row, ffn_row = attn_gain[None], latent_gain[None], ffn_gain[None]
+    normed_all, q, packed, keys, hot, latent_raw = start(
+        layer_input, attn_row, wl, latent_row, query_proj, kv_proj, expert_routes.T, cosine, sine
     )
-    wl = jnp.pad(latent_proj, ((0, 0), (0, SPAN - latent_proj.shape[1])))
-    hot = jnp.sum(
-        expert_routes[:, :, None] == jnp.arange(128, dtype=jnp.int32)[None, None, :], axis=1
-    ).astype(bf16)
-    attn_row, latent_row, ffn_row = attn_gain[None], latent_gain[None], ffn_gain[None]
-    normed_all, q, packed, keys, hot_all, latent_raw = start(
-        layer_input, attn_row, wl, latent_row, wq, kv_proj, cosine, sine, own_cosine, own_sine, hot
-    )
-    ropes, latents = keys[:, LAT:], keys[:, :LAT]
     late_grad, q = lax.optimization_barrier((out_grad, q))
     grad_all = lax.all_gather(late_grad, "exp", axis=0, tiled=True)
-    qseg, kseg = query_seg[:, None], key_seg[None, :]
-    heads, lse = attend(q, packed, ropes, qseg, kseg)
+    heads, lse = attend(q, packed, keys, segs)
     residual, mid_all = middle(heads, output_proj, layer_input, ffn_row)
-
-    router_high = lax.reduce_precision(router_proj, 8, 7)
-    router_rest = router_proj - router_high
-    router_mid = lax.reduce_precision(router_rest, 8, 7)
-    router_low = router_rest - router_mid
-    router_pieces = jnp.concatenate([router_high, router_mid, router_low], axis=1).astype(bf16)
-    router_pieces = jnp.pad(router_pieces, ((0, 0), (0, 128 - 3 * EXPERTS)))
-    router_turned = jnp.pad(router_proj.T.astype(bf16), ((0, 128 - EXPERTS), (0, 0)))
-    shared_width = shared_down.shape[0]
-    fill = SHARED_TILE - shared_width
-    pair_s = jnp.pad(shared_gate_up, ((0, 0), (0, 0), (0, fill))).reshape(model_width, 2 * SHARED_TILE)
-    down_s = jnp.pad(shared_down, ((0, fill), (0, 0)))
-    mid_part, moe_part, router_term, weight_terms = mlp(
-        mid_all, grad_all, pair_s, expert_gate_up[0], down_s, expert_down[0], router_pieces, router_turned, hot_all
+    terms, act, dpre, logit, router_term = mlp(
+        mid_all, grad_all, pair_s, pair_e, shared_down, down_e, router, hot
     )
-    weight_sum = lax.psum_scatter(weight_terms, "seq", scatter_dimension=0, tiled=True)
-    residual_grad, ffn_term, attn_grad_all = turn(mid_part, residual, ffn_row, out_grad)
-    dq, key_grad, kvo = attend_back(
-        attn_grad_all, output_proj, heads, q, packed, ropes, qseg, kseg, lse, cosine, sine, kv_proj, latents
+    weight_sum = lax.psum_scatter(terms.reshape(-1, 128), "seq", scatter_dimension=0, tiled=True)
+    residual_grad, ffn_term, attn_grad_all, moe_part = turn(
+        dpre, act, pair_s, pair_e, shared_down, down_e, logit, router, residual, ffn_row, out_grad
     )
-    weight_sum, moe_part, dq = lax.optimization_barrier((weight_sum, moe_part, dq))
-    moe_rows = lax.psum_scatter(moe_part, "exp", scatter_dimension=0, tiled=True)
-    small = jnp.concatenate([router_term, jnp.zeros_like(ffn_term), ffn_term, jnp.zeros((6, model_width), f32)], axis=0)
+    dq, key_grad, kvo, layer_output = attend_back(
+        attn_grad_all, output_proj, heads, q, packed, keys, segs, lse, kv_proj, moe_part, residual, cosine, sine
+    )
     query_sum, kvo_sum, latent_sum, input_grad, small = tail(
-        dq, key_grad, kvo, normed_all, wq, wl, latent_raw, latent_row, own_cosine, own_sine, attn_row,
-        residual_grad, layer_input, small,
+        dq, key_grad, kvo, normed_all, query_proj, wl, latent_raw, latent_row, attn_row,
+        residual_grad, layer_input, router_term, ffn_term, cosine, sine,
     )
-    layer_output = (residual + moe_rows.astype(f32)).astype(bf16)
-    query_sum = query_sum.reshape(model_width, -1)
-    query_sum = jnp.concatenate(
-        [
-            query_sum[:, :NOPE],
-            query_sum[:, 2 * NOPE : 2 * NOPE + ROPE],
-            query_sum[:, NOPE : 2 * NOPE],
-            query_sum[:, 2 * NOPE + ROPE :],
-        ],
-        axis=1,
-    ).astype(f32)
-    spots = kvo_sum.shape[0]
-    kv_rows = kv_proj.shape[0] // spots
-    kv_sum = kvo_sum[:, :kv_rows].reshape(kv_proj.shape).astype(f32)
-    out_rows = output_proj.shape[0] // spots
-    output_sum = (
-        kvo_sum[:, kv_rows:]
-        .reshape(spots, -1, out_rows, LAT)
-        .transpose(0, 2, 1, 3)
-        .reshape(output_proj.shape)
-        .astype(f32)
+    expert_gate, expert_down_sum, shared_gate, shared_down_sum, query_sum, kv_sum, output_sum, latent_sum = finish(
+        weight_sum, query_sum, kvo_sum, latent_sum, shared, model_width, kv_proj.shape, output_proj.shape
     )
-    latent_sum = latent_sum.reshape(model_width, SPAN)[:, : LAT + ROPE].astype(f32)
-    pair_width = 2 * (F + SHARED_TILE)
-    expert_gate_sum = weight_sum[None, :, : 2 * F].astype(f32)
-    shared_gate_sum = (
-        weight_sum[:, 2 * F : pair_width].reshape(own_rows, 2, SHARED_TILE)[..., :shared_width].astype(f32)
-    )
-    expert_down_sum = weight_sum[:, pair_width : pair_width + F].astype(f32).T[None]
-    shared_down_sum = weight_sum[:, pair_width + F : pair_width + F + shared_width].astype(f32).T
     return (
         layer_output,
         input_grad,
         small[EXPERTS],
         query_sum,
-        latent_sum,
+        latent_sum.T,
         small[EXPERTS + 2, :LAT],
         kv_sum,
         output_sum,
         small[EXPERTS + 1],
         small[:EXPERTS].T,
-        shared_gate_sum,
+        shared_gate.reshape(2, shared, 128).transpose(2, 0, 1),
         shared_down_sum,
-        expert_gate_sum,
-        expert_down_sum,
+        expert_gate[None],
+        expert_down_sum[None],
     )
 
 

time: 529 us -> 432 us (0.82)
  waiting for transfers between devices: 59.3 us -> 0.06 us
  local copies, waits for them, and re-layouts: 39.3 us -> 5.89 us
  other arithmetic: 17.9 us -> 0 us
  Pallas kernels: 396 us -> 407 us
    reduce_scatter x2 -> x1, waiting for transfers between devices: 59.2 us -> 0.01 us  [local(): lax.psum_scatter(terms.reshape(-1, 128), 'seq', scatter_dimension=0, tile...]
    pallas_call x1 -> x2, Pallas kernels: 106 us -> 75.7 us  [the longest x1 66.8 us: mlp(): pl.pallas_call(mlp_kernel, out_shape=[jax.ShapeDtypeStruct((width // 128,...]
    pallas_call x1, Pallas kernels: 24.1 us -> 43 us  [attend_back(): pl.pallas_call(attend_back_kernel, out_shape=[jax.ShapeDtypeStruct(q.shap...]
    pallas_call x1, Pallas kernels: 50 us -> 68.1 us  [turn(): pl.pallas_call(turn_kernel, out_shape=[jax.ShapeDtypeStruct((rows, width)...]
    pallas_call x1, Pallas kernels: 48.4 us -> 60.6 us  [middle(): pl.pallas_call(middle_kernel, out_shape=[jax.ShapeDtypeStruct((rows, widt...]
    unnamed x44 -> x6, local copies, waits for them, and re-layouts: 13.3 us -> 1.59 us
    convert_element_type x10 -> x0, other arithmetic: 11 us -> none  [the longest x1 2.8 us: local(): latent_sum.reshape(model_width, SPAN)[:, :LAT + ROPE].astype(f32)]
    slice x10 -> x0, local copies, waits for them, and re-layouts: 10.1 us -> none  [the longest x2 3.42 us: local(): ropes, latents = (keys[:, LAT:], keys[:, :LAT])]
  transfers between devices with their start and end apart: 3 -> 2, of which waited for: 1 -> 0; matrix products, arithmetic and copies ran while one was open for 7% -> 1% of each run, Pallas kernels for 46% -> 67%
where the time goes in v4:
time: 432 us; the launch traced here: 428 us
  Pallas kernels  407 us (94%)
  between operations  14.3 us (3%)
  local copies, waits for them, and re-layouts  5.89 us (1%)
    pallas_call x1, Pallas kernels, tail(): pl.pallas_call(tail_kernel, out_shape=[jax.ShapeDtypeStruct(query_shape,...  104 us
    pallas_call x1, Pallas kernels, turn(): pl.pallas_call(turn_kernel, out_shape=[jax.ShapeDtypeStruct((rows, width)...  68.1 us
    pallas_call x1, Pallas kernels, mlp(): pl.pallas_call(mlp_kernel, out_shape=[jax.ShapeDtypeStruct((width // 128,...  66.8 us
    pallas_call x1, Pallas kernels, middle(): pl.pallas_call(middle_kernel, out_shape=[jax.ShapeDtypeStruct((rows, widt...  60.6 us
    pallas_call x1, Pallas kernels, start(): pl.pallas_call(start_kernel, out_shape=[jax.ShapeDtypeStruct((block, widt...  45.6 us
    pallas_call x1, Pallas kernels, attend_back(): pl.pallas_call(attend_back_kernel, out_shape=[jax.ShapeDtypeStruct(q.shap...  43 us
    pallas_call x1, Pallas kernels, attend(): pl.pallas_call(attend_kernel, out_shape=[jax.ShapeDtypeStruct((rows, 2 *...  10.4 us
    pallas_call x1, Pallas kernels, finish(): pl.pallas_call(finish_kernel, out_shape=[jax.ShapeDtypeStruct(shape, f32)...  8.97 us
  transfers between devices with their start and end apart: 2, of which 0 were waited for; matrix products, arithmetic and copies ran while one was open for 1% of the time, Pallas kernels for 67%

profile of v4, /device:TPU:1, one launch (start us, length us, event | category | flops | bytes accessed | tf_op | source)
XLA Modules:
  0.0 427.7 jit_solution(3032807202243677453)
XLA Ops:
  7.2 0.0 all-gather.2.cloned.1.call-start
  7.2 45.6 %start.1 = (bf16[1024,2048]{1,0:T(8,128)(2,1)}, bf16[1024,384]{1,0:T(8,128)(2,1)}, bf16[2048,512]{1,0:T(8,128)(2,1)}, bf16[2048,640]{1,0:T(8,128)(2,1)}, bf16[1024,128]{1,0:T(8,128)(2,1)}, /*index=5*/f32[128,512]{1,0:T(8,128)}) custom-call(bf16[128,2048]{1,0:T(8,128)(2,1)} %rows_in.5, f32[1,2048]{1,0:T(1,128)} %bitcast.39, bf16[576,2048]{1,0:T(8,128)(2,1)} %bitcast.27, ...), custom_call_target="tpu_custom_call" | custom-call | tf_op jit(solution)/shard_map/start/pallas_call | solution.py:1002
  52.9 0.0 all-gather.2.cloned.1.call-update
  52.9 0.2 reduce-scatter.2.cloned.1.call-start
  53.1 10.4 %attend.1 = (bf16[1024,256]{1,0:T(8,128)(2,1)}, f32[2,1024,1]{2,1,0:T(8,128)}) custom-call(bf16[1024,384]{1,0:T(8,128)(2,1)} %get-tuple-element.53.q, bf16[2048,512]{1,0:T(8,128)(2,1)} %get-tuple-element.54.packed, bf16[2048,640]{1,0:T(8,128)(2,1)} %get-tuple-element.55.keys_all, s32[1,16384]{1,0:T(1,128)} %bitcast.33), custom_call_target="tpu_custom_call" | custom-call | tf_op jit(solution)/shard_map/attend/pallas_call | solution.py:638
  63.5 60.6 %middle.1 = (f32[128,2048]{1,0:T(8,128)}, bf16[1024,2048]{1,0:T(8,128)(2,1)}) custom-call(bf16[1024,256]{1,0:T(8,128)(2,1)} %get-tuple-element.56.heads, bf16[256,2048]{1,0:T(8,128)(2,1)} %wo.3, bf16[128,2048]{1,0:T(8,128)(2,1)} %rows_in.5, f32[1,2048]{1,0:T(1,128)} %bitcast.37), custom_call_target="tpu_custom_call" | custom-call | tf_op jit(solution)/shard_map/middle/pallas_call | solution.py:1057
  124.1 0.0 all-gather.2.cloned.1.call-done.grad_h
  124.1 66.8 %mlp.1 = (bf16[16,5280,128]{2,1,0:T(8,128)(2,1)}, bf16[1024,1792]{1,0:T(8,128)(2,1)}, bf16[1024,3584]{1,0:T(8,128)(2,1)}, bf16[1024,128]{1,0:T(8,128)(2,1)}, f32[8,2048]{1,0:T(8,128)}) custom-call(bf16[1024,2048]{1,0:T(8,128)(2,1)} %get-tuple-element.57.mid_h, bf16[1024,2048]{1,0:T(8,128)(2,1)} %all-gather.2.cloned.1.call-done.grad_h, ...), custom_call_target="tpu_custom_call" | custom-call | flops 44291850240 | bytes 62914560 | tf_op jit(solution)/shard_map/mlp/pallas_call | solution.py:459
  190.9 0.0 reduce-scatter.2.cloned.1.call-update
  190.9 68.1 %turn.1 = (f32[128,2048]{1,0:T(8,128)}, f32[1,2048]{1,0:T(1,128)}, bf16[1024,2048]{1,0:T(8,128)(2,1)}, bf16[1024,2048]{1,0:T(8,128)(2,1)}) custom-call(bf16[1024,3584]{1,0:T(8,128)(2,1)} %get-tuple-element.60.dpre_h, bf16[1024,1792]{1,0:T(8,128)(2,1)} %get-tuple-element.61.act_h, bf16[704,2048]{1,0:T(8,128)(2,1)} %bitcast.32, bf16[2048,2816]{1,0:T(8,128)(2,1)} %bitcast.26, ...), custom_call_target="tpu_custom_call" | custom-call | tf_op jit(solution)/shard_map/turn/pallas_call | solution.py:552
  259.0 43.0 %attend_back.1 = (bf16[1024,384]{1,0:T(8,128)(2,1)}, bf16[1024,1280]{1,0:T(8,128)(2,1)}, bf16[16,96,512]{2,1,0:T(8,128)(2,1)}, bf16[128,2048]{1,0:T(8,128)(2,1)}) custom-call(bf16[1024,2048]{1,0:T(8,128)(2,1)} %get-tuple-element.64.grad, bf16[256,2048]{1,0:T(8,128)(2,1)} %wo.3, bf16[1024,256]{1,0:T(8,128)(2,1)} %get-tuple-element.56.heads, ...), custom_call_target="tpu_custom_call" | custom-call | tf_op jit(solution)/shard_map/attend_back/pallas_call | solution.py:749
  301.9 103.8 %tail.1 = (bf16[16,128,384]{2,1,0:T(8,128)(2,1)}, bf16[16,96,512]{2,1,0:T(8,128)(2,1)}, bf16[128,16,640]{2,1,0:T(8,128)(2,1)}, bf16[128,2048]{1,0:T(8,128)(2,1)}, f32[16,2048]{1,0:T(8,128)}) custom-call(bf16[1024,384]{1,0:T(8,128)(2,1)} %get-tuple-element.68.dq, bf16[1024,1280]{1,0:T(8,128)(2,1)} %get-tuple-element.69.key_grad, ...), custom_call_target="tpu_custom_call" | custom-call | tf_op jit(solution)/shard_map/tail/pallas_call | solution.py:887
  405.7 1.3 slice.13
  407.0 1.5 fusion
  408.6 1.5 slice_bitcast_fusion
  410.0 0.0 reduce-scatter.2.cloned.1.call-done.weights
  410.0 0.0 copy-start
  410.0 0.0 copy-start.1
  410.1 9.0 %finish.1 = (f32[128,2816]{1,0:T(8,128)}, f32[1408,128]{1,0:T(8,128)}, f32[704,128]{1,0:T(8,128)}, f32[352,128]{1,0:T(8,128)}, f32[2048,384]{1,0:T(8,128)}, /*in...) custom-call(bf16[5280,128]{1,0:T(8,128)(2,1)} %reduce-scatter.2.cloned.1.call-done.weights, ...), custom_call_target="tpu_custom_call" | custom-call | tf_op jit(solution)/shard_map/finish/pallas_call | solution.py:1103
  419.0 0.0 copy-done
  419.0 0.8 copy.34
  419.8 0.0 copy-done.1
  419.8 0.8 copy.35
Async XLA Ops:
  7.2 116.9 %all-gather.2.cloned.1.call-start = ((), (), s32[]{:S(2)}) async-start(), calls=%async_computation.1 | async-start | bytes 4718592 | tf_op jit(solution)/shard_map/all_gather | solution.py:1139
  52.9 357.2 %reduce-scatter.2.cloned.1.call-start = ((), (), s32[]{:S(2)}) async-start(), calls=%async_computation.2 | async-start | bytes 22978560 | tf_op jit(solution)/shard_map/reduce_scatter | solution.py:1145
  410.0 9.0 %copy-start = (bf16[128,2048]{1,0:T(8,128)(2,1)S(1)}, bf16[128,2048]{1,0:T(8,128)(2,1)}, u32[]{:S(2)}) copy-start(bf16[128,2048]{1,0:T(8,128)(2,1)} %get-tuple-element.106) | copy-start | bytes 1572868
  410.0 9.8 %copy-start.1 = (bf16[128,2048]{1,0:T(8,128)(2,1)S(1)}, bf16[128,2048]{1,0:T(8,128)(2,1)}, u32[]{:S(2)}) copy-start(bf16[128,2048]{1,0:T(8,128)(2,1)} %get-tuple-element.107) | copy-start | bytes 1572868
Sparse Core Ops, SparseCore 0:
  53.0 45.2 all-gather.1
  191.0 142.9 reduce-scatter.1
